TPU v7x, 32 devices: a whole 2x2x4 slice. The times are simulated.
32 devices in a mesh: rep: 8 (over y, x, core), fsdp: 4 (over z).
Axes of the slice: x: 2, y: 2, z: 4, core: 2. Of those that a mesh axis runs over, the one named last changes fastest.
Arguments:
- tokens: bfloat16 [8, 1024, 2048], P('rep', 'fsdp'), may hold values from -6 to 6
- cotangent: bfloat16 [8, 1024, 2048], P('rep', 'fsdp'), may hold values from -6 to 6
- lengths: int32 [8], P('rep'), may hold values from 256 to 1024, as said below
- w_mix: float32 [4, 2048, 2048], P(None, 'fsdp', 'rep'), may hold values from -0.125 to 0.125
- w_in: float32 [2, 2048, 5632], P(None, 'fsdp', 'rep'), may hold values from -0.125 to 0.125
- w_down: float32 [5632, 2048], P('fsdp', 'rep'), may hold values from -0.078125 to 0.078125
- gains: float32 [4, 2048], P(None, 'fsdp')
- m_mix: float32 [4, 2048, 2048], P(None, 'fsdp', 'rep'), may hold values from -224 to 224
- m_in: float32 [2, 2048, 5632], P(None, 'fsdp', 'rep'), may hold values from -224 to 224
- m_down: float32 [5632, 2048], P('fsdp', 'rep'), may hold values from -224 to 224
- m_gain: float32 [4, 2048], P(None, 'fsdp'), may hold values from -224 to 224
- v_mix: float32 [4, 2048, 2048], P(None, 'fsdp', 'rep'), may hold values from 819.2 to 3276.8
- v_in: float32 [2, 2048, 5632], P(None, 'fsdp', 'rep'), may hold values from 819.2 to 3276.8
- v_down: float32 [5632, 2048], P('fsdp', 'rep'), may hold values from 819.2 to 3276.8
- v_gain: float32 [4, 2048], P(None, 'fsdp'), may hold values from 819.2 to 3276.8
Outputs:
- mixed: bfloat16 [8, 1024, 2048], P('rep', 'fsdp')
- token_grad: float32 [8, 1024, 2048], P('rep', 'fsdp')
- new_mix: float32 [4, 2048, 2048], P(None, 'fsdp', 'rep')
- new_in: float32 [2, 2048, 5632], P(None, 'fsdp', 'rep')
- new_down: float32 [5632, 2048], P('fsdp', 'rep')
- new_gains: float32 [4, 2048], P(None, 'fsdp')
- first_mix: float32 [4, 2048, 2048], P(None, 'fsdp', 'rep')
- first_in: float32 [2, 2048, 5632], P(None, 'fsdp', 'rep')
- first_down: float32 [5632, 2048], P('fsdp', 'rep')
- first_gains: float32 [4, 2048], P(None, 'fsdp')
- second_mix: float32 [4, 2048, 2048], P(None, 'fsdp', 'rep')
- second_in: float32 [2, 2048, 5632], P(None, 'fsdp', 'rep')
- second_down: float32 [5632, 2048], P('fsdp', 'rep')
- second_gains: float32 [4, 2048], P(None, 'fsdp')
- copy_mix: bfloat16 [4, 2048, 2048], P(None, 'fsdp', 'rep')
- copy_in: bfloat16 [2, 2048, 5632], P(None, 'fsdp', 'rep')
- copy_down: bfloat16 [5632, 2048], P('fsdp', 'rep')
Inputs may be any that keep to these rules, and one draw needn't show every extreme that they name: `lengths`: every length lies between 256 and 1024; at least one sequence has length 1024.
All inputs are finite; a program needn't handle non-finite values.
Results may differ from a plain program's by a relative error of at most 0.0085.
The roundings to bfloat16 on the way count: a program that leaves them out, or rounds other values in their place, can miss the bound.
Values may be sent and summed in bfloat16 or wider, within the bound.
No kernel may reach another device: no remote copies, remote signals or barrier semaphores. Data moves between devices by JAX's collectives and lax.ppermute only.
A program may use at most 640 MiB of HBM per device.

v0:
```python
import jax
import jax.numpy as jnp
from jax import lax
from jax.sharding import PartitionSpec as P

D = 2048
HEAD = 128
STRETCH = 32
STEP = 10


epsilon = 1e-06
adam_epsilon = 1e-08
beta_first = 0.5
beta_second = 0.5
rate_matrix = 0.04
rate_gain = 0.3
decay_matrix = 0.1
highest_precision = lax.Precision.HIGHEST


def carried_in(part, axis, combine, identity, reverse):
    count = lax.axis_size(axis)
    place = lax.axis_index(axis)
    ahead = count - 1 - place if reverse else place
    gathered = jax.tree.map(lambda a: lax.all_gather(a, axis), part)
    state = jax.tree.map(lambda a, e: jnp.zeros_like(a) + jnp.asarray(e, a.dtype), part, identity)

    def one(step, state):
        source = count - 1 - step if reverse else step
        return combine(
            state, jax.tree.map(lambda a: lax.dynamic_index_in_dim(a, source, 0, False), gathered)
        )

    return lax.fori_loop(0, ahead, one, state)


def rms_scale(value_input, scales):
    return (
        value_input
        * lax.rsqrt(jnp.mean(value_input * value_input, axis=-1, keepdims=True) + epsilon)
        * scales
    )


def gate_terms(query_pre, forget_pre, forget_bias):
    shifted = forget_pre + forget_bias
    return (jax.nn.silu(query_pre), jax.nn.log_sigmoid(shifted), jax.nn.sigmoid(-shifted))


def swiglu(gate_pre, up_pre):
    return jax.nn.silu(gate_pre) * up_pre


def stretch_step(initial_state, block_data):
    query_input, log_decay, input_keys, value_input = block_data
    cumulative_decay = jnp.cumsum(log_decay, axis=0)
    block_len = query_input.shape[0]
    causal = (jnp.arange(block_len)[:, None] >= jnp.arange(block_len)[None, :])[:, :, None, None]
    log_gap = jnp.where(causal, cumulative_decay[:, None] - cumulative_decay[None, :], 0.0)
    weights = jnp.where(causal, jnp.exp(log_gap), 0.0)
    scores = jnp.einsum(
        "thk,tshk,shk->tsh", query_input, weights, input_keys, precision=highest_precision
    )
    inside = jnp.einsum("tsh,shv->thv", scores, value_input, precision=highest_precision)
    outside_state = jnp.einsum(
        "nip,ipc->nic",
        query_input * jnp.exp(cumulative_decay),
        initial_state,
        precision=highest_precision,
    )
    final_log_decay = cumulative_decay[-1]
    carried_state = jnp.exp(final_log_decay)[:, :, None] * initial_state + jnp.einsum(
        "ril,rit->ilt",
        input_keys * jnp.exp(final_log_decay[None] - cumulative_decay),
        value_input,
        precision=highest_precision,
    )
    return (carried_state, inside + outside_state)


def recurrence(query_input, log_decay, input_keys, value_input, initial_state):
    row_count = query_input.shape[0]

    def blocked(source):
        return source.reshape((row_count // STRETCH, STRETCH) + source.shape[1:])

    end_state, outputs = lax.scan(
        jax.checkpoint(stretch_step),
        initial_state,
        (blocked(query_input), blocked(log_decay), blocked(input_keys), blocked(value_input)),
    )
    return (outputs.reshape((row_count,) + outputs.shape[2:]), end_state)


def combine(earlier, following):
    return (earlier[0] * following[0], following[0][..., None] * earlier[1] + following[1])


def product(left, right):
    return jnp.dot(left, right, preferred_element_type=jnp.float32)


def adam(weight, first, second, gradient, step_rate, decay_on):
    first_new = beta_first * first + (1.0 - beta_first) * gradient
    second_new = beta_second * second + (1.0 - beta_second) * gradient * gradient
    first_fix = 1.0 - beta_first**STEP
    second_fix = 1.0 - beta_second**STEP
    weight_new = weight - step_rate * (
        first_new / first_fix / (jnp.sqrt(second_new / second_fix) + adam_epsilon)
        + decay_on * weight
    )
    return (weight_new, first_new, second_new)


def shards(
    tokens,
    cotangent,
    lengths,
    w_mix,
    w_in,
    w_down,
    gains,
    m_mix,
    m_in,
    m_down,
    m_gain,
    v_mix,
    v_in,
    v_down,
    v_gain,
):
    seg_rows = tokens.shape[1]
    head_count = D // HEAD
    inputs = tokens[0].astype(jnp.float32)
    position = lax.axis_index("fsdp") * seg_rows + jnp.arange(seg_rows)
    valid = (position < lengths[0]).astype(jnp.float32)[:, None]
    mix_part, in_part, down_part = (
        lax.all_gather(w_mix.astype(jnp.bfloat16), "rep", axis=2, tiled=True),
        lax.all_gather(w_in.astype(jnp.bfloat16), "rep", axis=2, tiled=True),
        lax.all_gather(w_down.astype(jnp.bfloat16), "rep", axis=1, tiled=True),
    )
    mix_full, gain_full = (
        lax.all_gather(mix_part, "fsdp", axis=1, tiled=True),
        lax.all_gather(gains.astype(jnp.bfloat16), "fsdp", axis=1, tiled=True),
    )
    scales = gain_full.astype(jnp.float32)
    normed_one, norm_one_pull = jax.vjp(rms_scale, inputs, scales[0])
    normed_a = normed_one.astype(jnp.bfloat16)
    query_pre = product(normed_a, mix_full[0])
    forget_pre = product(normed_a, mix_full[1])
    value_pre = product(normed_a, mix_full[2])
    (act_query, log_decay, input_keys), gate_pull = jax.vjp(
        gate_terms, query_pre, forget_pre, scales[3]
    )

    def heads_of(source):
        return source.reshape(seg_rows, head_count, HEAD)

    def flatten_heads(source):
        return source.reshape(seg_rows, D)

    query_heads = heads_of(act_query)
    decay_heads = heads_of(log_decay)
    key_heads = heads_of(input_keys)
    value_heads = heads_of(value_pre)
    zero_state = jnp.zeros((head_count, HEAD, HEAD), jnp.float32)
    local_output, local_end = recurrence(
        query_heads, decay_heads, key_heads, value_heads, zero_state
    )
    cumulative_decay = jnp.cumsum(decay_heads, axis=0)
    decay_total = jnp.exp(cumulative_decay[-1])
    identity = (jnp.ones_like(decay_total), jnp.zeros_like(local_end))
    incoming_state = carried_in((decay_total, local_end), "fsdp", combine, identity, False)[1]
    reach_decay = query_heads * jnp.exp(cumulative_decay)
    recurrence_output = local_output + jnp.einsum(
        "nip,ipc->nic", reach_decay, incoming_state, precision=highest_precision
    )

    def head_norm(outputs, head_scales):
        return rms_scale(outputs, head_scales.reshape(head_count, HEAD)).reshape(seg_rows, D)

    head_normed, head_pull = jax.vjp(head_norm, recurrence_output, scales[2])
    head_out = head_normed.astype(jnp.bfloat16)
    middle = inputs + product(head_out, mix_full[3])
    normed_two, norm_two_pull = jax.vjp(rms_scale, middle, scales[1])
    normed_b = normed_two.astype(jnp.bfloat16)
    in_full, down_full = (
        lax.all_gather(in_part, "fsdp", axis=1, tiled=True),
        lax.all_gather(down_part, "fsdp", axis=0, tiled=True),
    )
    gate_pre = product(normed_b, in_full[0])
    up_pre = product(normed_b, in_full[1])
    hidden_full, swiglu_pull = jax.vjp(swiglu, gate_pre, up_pre)
    hidden = hidden_full.astype(jnp.bfloat16)
    mixed = (middle + product(hidden, down_full)).astype(jnp.bfloat16)
    cot_rows = cotangent[0].astype(jnp.float32) * valid
    cot_back = cot_rows.astype(jnp.bfloat16)
    in_back, down_back = (
        lax.all_gather(in_part, "fsdp", axis=1, tiled=True),
        lax.all_gather(down_part, "fsdp", axis=0, tiled=True),
    )
    grad_down = jnp.einsum("tf,td->fd", hidden, cot_back, preferred_element_type=jnp.float32)
    grad_hidden = jnp.einsum("td,fd->tf", cot_back, down_back, preferred_element_type=jnp.float32)
    grad_gate, grad_up = swiglu_pull(grad_hidden)
    gate_low = grad_gate.astype(jnp.bfloat16)
    up_low = grad_up.astype(jnp.bfloat16)
    grad_feed = jnp.stack(
        [
            jnp.einsum("td,tf->df", normed_b, gate_low, preferred_element_type=jnp.float32),
            jnp.einsum("td,tf->df", normed_b, up_low, preferred_element_type=jnp.float32),
        ]
    )
    grad_normed_b = jnp.einsum(
        "tf,df->td", gate_low, in_back[0], preferred_element_type=jnp.float32
    ) + jnp.einsum("tf,df->td", up_low, in_back[1], preferred_element_type=jnp.float32)
    grad_middle_norm, grad_scale_two = norm_two_pull(grad_normed_b)
    grad_middle = cot_rows + grad_middle_norm
    feed_sum, down_sum = (
        lax.psum_scatter(grad_feed, "fsdp", scatter_dimension=1, tiled=True),
        lax.psum_scatter(grad_down, "fsdp", scatter_dimension=0, tiled=True),
    )
    mix_back = lax.all_gather(mix_part, "fsdp", axis=1, tiled=True)
    mix_low = grad_middle.astype(jnp.bfloat16)
    grad_out_proj = jnp.einsum("td,te->de", head_out, mix_low, preferred_element_type=jnp.float32)
    grad_head_out = jnp.einsum(
        "te,de->td", mix_low, mix_back[3], preferred_element_type=jnp.float32
    )
    recurrence_gradient, grad_scale_head = head_pull(grad_head_out)
    local_backward = jnp.einsum(
        "gxu,gxa->xua", reach_decay, recurrence_gradient, precision=highest_precision
    )
    carried_state = carried_in((decay_total, local_backward), "fsdp", combine, identity, True)[1]

    def from_incoming(query_rows, decay_rows, key_rows, value_rows):
        return recurrence(query_rows, decay_rows, key_rows, value_rows, incoming_state)

    unused_out, rec_pull = jax.vjp(from_incoming, query_heads, decay_heads, key_heads, value_heads)
    grad_query, grad_decay, grad_keys, grad_values = rec_pull((recurrence_gradient, carried_state))
    grad_query_pre, grad_forget_pre, grad_bias = gate_pull(
        (flatten_heads(grad_query), flatten_heads(grad_decay), flatten_heads(grad_keys))
    )
    query_low = grad_query_pre.astype(jnp.bfloat16)
    forget_low = grad_forget_pre.astype(jnp.bfloat16)
    value_low = flatten_heads(grad_values).astype(jnp.bfloat16)
    grad_mix = jnp.stack(
        [
            jnp.einsum("td,te->de", normed_a, query_low, preferred_element_type=jnp.float32),
            jnp.einsum("td,te->de", normed_a, forget_low, preferred_element_type=jnp.float32),
            jnp.einsum("td,te->de", normed_a, value_low, preferred_element_type=jnp.float32),
            grad_out_proj,
        ]
    )
    grad_normed_a = (
        jnp.einsum("te,de->td", query_low, mix_back[0], preferred_element_type=jnp.float32)
        + jnp.einsum("te,de->td", forget_low, mix_back[1], preferred_element_type=jnp.float32)
        + jnp.einsum("te,de->td", value_low, mix_back[2], preferred_element_type=jnp.float32)
    )
    grad_input_norm, grad_scale_one = norm_one_pull(grad_normed_a)
    token_grad = grad_middle + grad_input_norm
    grad_gains = jnp.stack([grad_scale_one, grad_scale_two, grad_scale_head, grad_bias])
    mix_sum, gain_sum = (
        lax.psum_scatter(grad_mix, "fsdp", scatter_dimension=1, tiled=True),
        lax.psum_scatter(grad_gains, "fsdp", scatter_dimension=1, tiled=True),
    )
    gain_owned = lax.psum(gain_sum, "rep")
    mix_owned, feed_owned, down_owned = (
        lax.psum_scatter(mix_sum, "rep", scatter_dimension=2, tiled=True),
        lax.psum_scatter(feed_sum, "rep", scatter_dimension=2, tiled=True),
        lax.psum_scatter(down_sum, "rep", scatter_dimension=1, tiled=True),
    )
    new_mix, first_mix, second_mix = adam(w_mix, m_mix, v_mix, mix_owned, rate_matrix, decay_matrix)
    new_in, first_in, second_in = adam(w_in, m_in, v_in, feed_owned, rate_matrix, decay_matrix)
    new_down, first_down, second_down = adam(
        w_down, m_down, v_down, down_owned, rate_matrix, decay_matrix
    )
    new_gains, first_gains, second_gains = adam(gains, m_gain, v_gain, gain_owned, rate_gain, 0.0)
    return (
        mixed[None],
        token_grad[None],
        new_mix,
        new_in,
        new_down,
        new_gains,
        first_mix,
        first_in,
        first_down,
        first_gains,
        second_mix,
        second_in,
        second_down,
        second_gains,
        new_mix.astype(jnp.bfloat16),
        new_in.astype(jnp.bfloat16),
        new_down.astype(jnp.bfloat16),
    )


def solution(mesh):
    placed = (
        P("rep", "fsdp", None),
        P("rep", "fsdp", None),
        P("rep"),
        P(None, "fsdp", "rep"),
        P(None, "fsdp", "rep"),
        P("fsdp", "rep"),
        P(None, "fsdp"),
        P(None, "fsdp", "rep"),
        P(None, "fsdp", "rep"),
        P("fsdp", "rep"),
        P(None, "fsdp"),
        P(None, "fsdp", "rep"),
        P(None, "fsdp", "rep"),
        P("fsdp", "rep"),
        P(None, "fsdp"),
    )
    return jax.shard_map(
        shards,
        mesh=mesh,
        in_specs=placed,
        out_specs=(
            P("rep", "fsdp", None),
            P("rep", "fsdp", None),
            P(None, "fsdp", "rep"),
            P(None, "fsdp", "rep"),
            P("fsdp", "rep"),
            P(None, "fsdp"),
            P(None, "fsdp", "rep"),
            P(None, "fsdp", "rep"),
            P("fsdp", "rep"),
            P(None, "fsdp"),
            P(None, "fsdp", "rep"),
            P(None, "fsdp", "rep"),
            P("fsdp", "rep"),
            P(None, "fsdp"),
            P(None, "fsdp", "rep"),
            P(None, "fsdp", "rep"),
            P("fsdp", "rep"),
        ),
        check_vma=False,
    )
```

profile of v0, /device:TPU:0, one launch (start us, length us, event | category | flops | bytes accessed | tf_op | source)
XLA Modules:
  0.0 6178.9 jit_solution(800314356457106440)
XLA Ops:
  10.0 59.2 all-gather.11.cloned.1.call-done
  74.7 13.2 all_gather.42
  88.8 543.4 %all-gather.13.cloned.1.call-done = bf16[4,2048,2048]{2,1,0:T(8,128)(2,1)} async-done(((bf16[4,512,2048]{2,1,0:T(8,128)(2,1)}), bf16[4,2048,2048]{2,1,0:T(8,128)(2,1)}) %all-gather.13.cloned.1.call-update) | async-done | bytes 33554448 | tf_op jit(solution)/shard_map/all_gather | solution.py:144
  642.8 11.9 fusion.164
  654.7 12.5 copy.203
  683.8 204.2 %while.77 = (s32[]{:T(128)}, f32[16,128,128]{2,1,0:T(8,128)S(1)}, f32[8,32,16,128]{3,2,1,0:T(8,128)}, f32[8,32,16,128]{3,2,1,0:T(8,128)}, f32[8,32,16,128]{3,2,1...) while((s32[]{:T(128)}, f32[16,128,128]{2,1,0:T(8,128)S(1)}, ...), condition=%wide.region_3.4_spmd.clone, body=%wide.region_1.3_spmd.clone.sunk | while | flops 263390208 | bytes 25610372 | solution.py:88
  692.6 14.7 fusion.288
  718.1 14.7 fusion.288
  743.6 14.7 fusion.288
  769.0 14.7 fusion.288
  794.5 14.7 fusion.288
  819.9 14.7 fusion.288
  845.4 14.7 fusion.288
  870.9 14.7 fusion.288
  898.5 13.3 all_gather.45
  911.8 59.2 all-gather.23.cloned.1.call-done
  977.9 8.8 multiply_reduce_fusion.5
  988.4 750.4 %all-gather.17.cloned.1.call-done = bf16[2,2048,5632]{1,2,0:T(8,128)(2,1)} async-done(((bf16[2,512,5632]{1,2,0:T(8,128)(2,1)}), bf16[2,2048,5632]{1,2,0:T(8,128)(2,1)}) %all-gather.17.cloned.1.call-update) | async-done | bytes 46137360 | tf_op jit(solution)/shard_map/all_gather | solution.py:189
  1738.7 13.7 fusion.67
  1752.5 14.6 fusion.69
  1767.1 362.5 %all-gather.21.cloned.1.call-done = bf16[5632,2048]{1,0:T(8,128)(2,1)} async-done(((bf16[1408,2048]{1,0:T(8,128)(2,1)}), bf16[5632,2048]{1,0:T(8,128)(2,1)}) %all-gather.21.cloned.1.call-update) | async-done | bytes 23068688 | tf_op jit(solution)/shard_map/all_gather | solution.py:190
  2129.6 25.0 multiply_convert_fusion
  2154.7 12.8 fusion.66
  2167.5 13.5 multiply_reduce_fusion.2
  2182.6 7.0 multiply_reduce_fusion.1
  2197.2 20.8 fusion.141
  2218.1 49.7 while.75
  2271.0 8.1 convolution_bitcast_fusion.6
  2279.2 7.6 while.74
  2292.6 518.7 %while.76 = (s32[]{:T(128)}, f32[16,128,128]{2,1,0:T(8,128)S(1)}, f32[8,32,16,128]{3,2,1,0:T(8,128)}, f32[8,32,16,128]{3,2,1,0:T(8,128)}, f32[8,32,16,128]{3,2,1...) while((s32[]{:T(128)}, f32[16,128,128]{2,1,0:T(8,128)S(1)}, ...), condition=%wide.region_24.25_spmd, body=%wide.region_17.24_spmd.sunk | while | flops 545391616 | bytes 56880456 | solution.py:88
  2347.1 9.0 fusion.272
  2360.2 14.9 fusion.275
  2408.2 9.0 fusion.272
  2421.2 14.9 fusion.275
  2469.3 9.0 fusion.272
  2482.3 14.9 fusion.275
  2530.3 9.0 fusion.272
  2543.3 14.9 fusion.275
  2591.4 9.0 fusion.272
  2604.4 14.9 fusion.275
  2652.4 9.0 fusion.272
  2665.4 14.9 fusion.275
  2713.5 9.0 fusion.272
  2726.5 14.9 fusion.275
  2774.7 9.0 fusion.272
  2787.7 14.9 fusion.275
  2814.5 8.3 convolution_bitcast_fusion.7
  2826.6 8.3 convolution_bitcast_fusion.8
  2837.0 8.5 convolution_bitcast_fusion.9
  2845.5 44.8 pad_maximum_fusion.1
  2891.6 20.2 convolution_bitcast_fusion.4
  2911.7 18.6 convolution_bitcast_fusion.5
  2930.3 61.3 pad_maximum_fusion
  3004.7 7.7 fusion.102
  3013.8 17.0 reduce-scatter.15.cloned.1.call-done
  3030.9 1098.7 %reduce-scatter.9.cloned.1.call-done = f32[4,512,2048]{2,1,0:T(8,128)} async-done(((f32[4,2048,2048]{2,1,0:T(8,128)}), f32[4,512,2048]{2,1,0:T(8,128)}) %reduce-scatter.9.cloned.1.call-update) | async-done | bytes 16777232 | tf_op jit(solution)/shard_map/reduce_scatter | solution.py:263
  4129.6 1503.0 %reduce-scatter.13.cloned.1.call-done = f32[2,512,5632]{2,1,0:T(8,128)} async-done(((f32[2,2048,5632]{2,1,0:T(8,128)}), f32[2,512,5632]{2,1,0:T(8,128)}) %reduce-scatter.13.cloned.1.call-update) | async-done | bytes 23068688 | tf_op jit(solution)/shard_map/reduce_scatter | solution.py:220
  5632.6 33.8 copy.223
  5668.4 16.4 fusion.100
  5687.9 13.9 psum.7
  5702.5 51.3 reduce-scatter.17.cloned.1.call-done
  5759.0 114.1 %reduce-scatter.11.cloned.1.call-done = f32[4,512,256]{2,1,0:T(8,128)} async-done(((f32[4,512,2048]{2,1,0:T(8,128)}), f32[4,512,256]{2,1,0:T(8,128)}) %reduce-scatter.11.cloned.1.call-update) | async-done | bytes 2097168 | tf_op jit(solution)/shard_map/reduce_scatter | solution.py:268
  5873.1 7.0 fusion.159
  5880.1 282.6 %all-reduce.4.cloned.1.call-done = f32[2,512,5632]{1,0,2:T(2,128)} async-done(((f32[2,512,5632]{1,0,2:T(2,128)}), f32[2,512,5632]{1,0,2:T(2,128)}) %all-reduce.4.cloned.1.call-update) | async-done | bytes 23068688
  (684 shorter events, 555.3 us)
Async XLA Ops:
  7.2 62.0 %all-gather.11.cloned.1.call-start = ((), (), s32[]{:S(2)}) async-start(), calls=%async_computation.6 | async-start | bytes 9437184 | tf_op jit(solution)/shard_map/all_gather | solution.py:139
  9.9 622.3 %all-gather.13.cloned.1.call-start = ((), (), s32[]{:S(2)}) async-start(), calls=%async_computation.7 | async-start | bytes 41943040 | tf_op jit(solution)/shard_map/all_gather | solution.py:144
  69.2 819.9 %all-gather.15.cloned.1.call-start = ((), (), s32[]{:S(2)}) async-start(), calls=%async_computation.8 | async-start | bytes 12976128 | tf_op jit(solution)/shard_map/all_gather | solution.py:140
  72.3 15.6 copy-start.3
  72.3 817.4 %all-gather.19.cloned.1.call-start = ((), (), s32[]{:S(2)}) async-start(), calls=%async_computation.10 | async-start | bytes 6488064 | tf_op jit(solution)/shard_map/all_gather | solution.py:141
  74.6 896.4 %all-gather.23.cloned.1.call-start = ((), (), s32[]{:S(2)}) async-start(), calls=%async_computation.17 | async-start | bytes 5242880 | tf_op jit(solution)/shard_map/all_gather | solution.py:26
  88.2 549.7 %copy-start.61 = (f32[256]{0:T(256)}, f32[256]{0:T(256)S(1)}, u32[]{:S(2)}) copy-start(f32[256]{0:T(256)S(1)} %fusion.103) | copy-start | bytes 3076
  88.2 549.7 %copy-start.55 = (f32[256]{0:T(256)}, f32[256]{0:T(256)S(1)}, u32[]{:S(2)}) copy-start(f32[256]{0:T(256)S(1)} %fusion.152) | copy-start | bytes 3076
  88.8 587.9 %copy-start.42 = (bf16[1,256,2048]{2,1,0:T(8,128)(2,1)}, bf16[1,256,2048]{2,1,0:T(8,128)(2,1)S(1)}, u32[]{:S(2)}) copy-start(bf16[1,256,2048]{2,1,0:T(8,128)(2,1)S(1)} %fusion.106) | copy-start | bytes 3145732
  889.0 849.7 %all-gather.17.cloned.1.call-start = ((), (), s32[]{:S(2)}) async-start(), calls=%async_computation.9 | async-start | bytes 57671680 | tf_op jit(solution)/shard_map/all_gather | solution.py:189
  889.6 1240.1 %all-gather.21.cloned.1.call-start = ((), (), s32[]{:S(2)}) async-start(), calls=%async_computation.11 | async-start | bytes 28835840 | tf_op jit(solution)/shard_map/all_gather | solution.py:190
  890.3 1388.8 %all-gather.25.cloned.1.call-start = ((), (), s32[]{:S(2)}) async-start(), calls=%async_computation.18 | async-start | bytes 5242880 | tf_op jit(solution)/shard_map/all_gather | solution.py:26
  977.9 8.8 copy-start.36
  988.4 764.1 %copy-start.16 = (bf16[256,2048]{1,0:T(8,128)(2,1)}, bf16[256,2048]{1,0:T(8,128)(2,1)S(1)}, u32[]{:S(2)}) copy-start(bf16[256,2048]{1,0:T(8,128)(2,1)S(1)} %multiply_convert_fusion.2) | copy-start | bytes 3145732
  1752.5 377.2 %copy-start.34 = (bf16[1,256,2048]{2,1,0:T(8,128)(2,1)S(1)}, bf16[1,256,2048]{2,1,0:T(8,128)(2,1)}, u32[]{:S(2)}) copy-start(bf16[1,256,2048]{2,1,0:T(8,128)(2,1)} %param.26) | copy-start | bytes 3145732
  2154.6 12.8 copy-start.48
  2154.6 12.8 copy-start.24
  2167.5 13.5 copy-start.35
  2181.7 89.3 %copy-start.10 = (f32[256,2048]{1,0:T(8,128)}, f32[256,2048]{1,0:T(8,128)S(1)}, u32[]{:S(2)}) copy-start(f32[256,2048]{1,0:T(8,128)S(1)} %fusion.108) | copy-start | bytes 6291460
  2197.2 833.6 %reduce-scatter.15.cloned.1.call-start = ((), (), s32[]{:S(2)}) async-start(), calls=%async_computation.15 | async-start | bytes 57671680 | tf_op jit(solution)/shard_map/reduce_scatter | solution.py:221
  2218.1 1911.5 %reduce-scatter.9.cloned.1.call-start = ((), (), s32[]{:S(2)}) async-start(), calls=%async_computation.12 | async-start | bytes 83886080 | tf_op jit(solution)/shard_map/reduce_scatter | solution.py:263
  2334.8 6.6 copy-start.6
  2360.2 15.0 copy-start.7
  2421.2 15.0 copy-start.7
  2456.9 6.6 copy-start.2
  2456.9 6.6 copy-start.6
  2482.3 15.0 copy-start.7
  2543.3 15.0 copy-start.7
  2579.1 6.6 copy-start.2
  2579.1 6.6 copy-start.6
  2604.4 15.0 copy-start.7
  2640.1 6.6 copy-start.2
  2640.1 6.6 copy-start.6
  2665.4 15.0 copy-start.7
  2701.1 6.6 copy-start.2
  2701.1 6.6 copy-start.6
  2726.5 15.0 copy-start.7
  2762.3 6.6 copy-start.6
  2787.7 15.0 copy-start.7
  2813.8 9.1 copy-start.40
  2814.5 8.3 copy-start.28
  2814.5 8.3 copy-start.30
  2826.5 8.3 copy-start.44
  2826.5 8.3 copy-start.22
  2826.6 8.3 copy-start.29
  2890.4 2742.3 %reduce-scatter.13.cloned.1.call-start = ((), (), s32[]{:S(2)}) async-start(), calls=%async_computation.14 | async-start | bytes 115343360 | tf_op jit(solution)/shard_map/reduce_scatter | solution.py:220
  2891.6 20.2 copy-start.49
  2991.7 6.9 copy-start.39
  2991.7 2695.1 %reduce-scatter.19.cloned.1.call-start = ((), (), s32[]{:S(2)}) async-start(), calls=%async_computation.19 | async-start | bytes 1310720
  3004.6 7.7 copy-start.60
  3004.6 7.7 copy-start.65
  3004.7 7.7 copy-start.66
  3013.8 2739.9 %reduce-scatter.17.cloned.1.call-start = ((), (), s32[]{:S(2)}) async-start(), calls=%async_computation.16 | async-start | bytes 12976128 | tf_op jit(solution)/shard_map/reduce_scatter | solution.py:270
  3030.8 2842.3 %reduce-scatter.11.cloned.1.call-start = ((), (), s32[]{:S(2)}) async-start(), calls=%async_computation.13 | async-start | bytes 18874368 | tf_op jit(solution)/shard_map/reduce_scatter | solution.py:268
  4129.6 2033.1 %all-reduce.4.cloned.1.call-start = ((), (), s32[]{:S(2)}) async-start(), calls=%async_computation.20 | async-start | bytes 46137344
  5668.4 16.4 copy-start.62
  5668.4 16.4 copy-start.11
  5668.4 16.4 copy-start.50
  5684.9 16.9 copy-start.59
  5684.9 16.9 copy-start.63
  5684.9 16.9 copy-start.64
  5684.9 68.8 %copy-start.33 = (f32[1408,256]{1,0:T(8,128)S(1)}, f32[1408,256]{1,0:T(8,128)}, u32[]{:S(2)}) copy-start(f32[1408,256]{1,0:T(8,128)} %param.30) | copy-start | bytes 4325380
  5702.5 170.7 %copy-start.20 = (f32[4,512,256]{2,1,0:T(8,128)S(1)}, f32[4,512,256]{2,1,0:T(8,128)}, u32[]{:S(2)}) copy-start(f32[4,512,256]{2,1,0:T(8,128)} %param.28) | copy-start | bytes 6291460
  5880.1 285.6 %copy-start.19 = (f32[2,512,704]{1,2,0:T(8,128)S(1)}, f32[2,512,704]{1,2,0:T(8,128)}, u32[]{:S(2)}) copy-start(f32[2,512,704]{1,2,0:T(8,128)} %param.29) | copy-start | bytes 8650756
  (54 other events, 174.5 us)
Sparse Core Ops, SparseCore 0:
  10.5 58.6 all-gather.10
  70.7 561.3 all-gather.12
  634.7 65.8 all-gather.14
  702.9 44.3 all-gather.18
  889.1 81.7 all-gather.22
  972.4 766.3 all-gather.16
  1740.3 389.2 all-gather.20
  2197.3 79.0 all-gather.24
  2278.8 751.9 reduce-scatter.14
  3033.1 1096.4 reduce-scatter.8
  4131.9 1500.6 reduce-scatter.12
  5635.5 28.9 reduce-scatter.18
  5667.9 85.7 reduce-scatter.16
  5757.1 115.9 reduce-scatter.10
  5876.7 285.9 all-reduce.3
where the time goes:
time: 6190 us; the launch traced here: 6180 us
  waiting for transfers between devices  4840 us (78%)
  matrix products  709 us (11%)
  other arithmetic  324 us (5%)
  local copies, waits for them, and re-layouts  213 us (3%)
    reduce_scatter x1, waiting for transfers between devices, shards(): lax.psum_scatter(grad_feed, 'fsdp', scatter_dimension=1, tiled=True)  1500 us
    reduce_scatter x1, waiting for transfers between devices, shards(): lax.psum_scatter(grad_mix, 'fsdp', scatter_dimension=1, tiled=True)  1100 us
    all_gather x1, waiting for transfers between devices, shards(): lax.all_gather(in_part, 'fsdp', axis=1, tiled=True)  750 us
    all_gather x1, waiting for transfers between devices, shards(): lax.all_gather(mix_part, 'fsdp', axis=1, tiled=True)  543 us
    all_gather x1, waiting for transfers between devices, shards(): lax.all_gather(down_part, 'fsdp', axis=0, tiled=True)  363 us
    dot_general x24, matrix products, stretch_step(): jnp.einsum('thk,tshk,shk->tsh', query_input, weights, input_keys, precisi...  309 us
    unnamed x17, waiting for transfers between devices  284 us
  transfers between devices with their start and end apart: 15, of which 11 were waited for; matrix products, arithmetic and copies ran while one was open for 19% of the time, Pallas kernels for 0%

commit v1 on v0

v1 whole, which is shorter than its diff:
```python
import functools
import math

import jax
import jax.numpy as jnp
import numpy as np
from jax import lax
from jax.experimental import pallas as pl
from jax.experimental.pallas import tpu as pltpu
from jax.sharding import PartitionSpec as P

D = 2048
HEAD = 128
STEP = 10
PACK = HEAD + 32

epsilon = 1e-06
adam_epsilon = 1e-08
beta_first = 0.5
beta_second = 0.5
rate_matrix = 0.04
rate_gain = 0.3
decay_matrix = 0.1
bf16 = jnp.bfloat16
f32 = jnp.float32


def swap(x, axis, d):
    n = lax.axis_size(axis)
    return lax.ppermute(x, axis, [(i, i ^ d) for i in range(n)])


def block_of(x, index):
    return lax.dynamic_index_in_dim(x, index, 0, False)


def low_bit(j):
    return j & -j


def z_pieces(x, *lands):
    n = lax.axis_size("fsdp")
    pieces, landed = {0: x}, ()
    for hop in range(1, n.bit_length()):
        now = [j for j in range(n) if j.bit_count() == hop]
        got = {j: swap(after(pieces[j & (j - 1)], *landed), "fsdp", low_bit(j)) for j in now}
        if hop <= len(lands):
            got = {j: after(piece, *lands[hop - 1]) for j, piece in got.items()}
        pieces.update(got)
        landed = tuple(got.values())
    return [pieces[j] for j in range(n)]


def kernel_call(body, grid, in_specs, out_specs, out_shape, name, us, prefetch=(), aliases=None):
    return pl.pallas_call(
        body,
        grid_spec=pltpu.PrefetchScalarGridSpec(
            num_scalar_prefetch=len(prefetch), grid=grid, in_specs=in_specs, out_specs=out_specs
        ),
        out_shape=out_shape,
        name=name,
        input_output_aliases=aliases or {},
        cost_estimate=pl.CostEstimate(flops=0, bytes_accessed=int(us * 5e4), transcendentals=0),
        compiler_params=pltpu.CompilerParams(
            dimension_semantics=("arbitrary",) * len(grid), vmem_limit_bytes=52 * 1024 * 1024
        ),
    )


def whole_spec(x, buffers=2):
    return pl.BlockSpec(x.shape, lambda *_: (0,) * x.ndim, pipeline_mode=pl.Buffered(buffers))


def layer_spec(x, at):
    return pl.BlockSpec((None,) + x.shape[1:], lambda *_: (at, 0, 0), pipeline_mode=pl.Buffered(1))


def index_of(axis):
    return lax.axis_index(axis).astype(jnp.int32).reshape(1)


class ZReduce:
    def __init__(self, sums):
        self.sums = list(sums)
        self.left = list(range(len(self.sums) - 1, 0, -1))
        self.flying = []
        self.send()

    def send(self, *others):
        most = max(j.bit_count() for j in self.left)
        now = [j for j in self.left if j.bit_count() == most]
        self.left = [j for j in self.left if j.bit_count() < most]
        self.sent = [after(self.sums[j].astype(bf16), *others) for j in now]
        self.flying += [(j, swap(x, "fsdp", low_bit(j))) for j, x in zip(now, self.sent)]

    def advance(self, *others):
        first = not self.left
        landed, self.flying = self.flying, []
        self.landed = [got for _, got in landed]
        for j, got in landed:
            got = after(got, *others)
            self.sums[j & (j - 1)] = self.sums[j & (j - 1)].astype(f32) + got.astype(f32)
        if not first:
            self.send(*self.landed, *others)
        return self.sums[0]

    def flying_now(self):
        return [got for _, got in self.flying]

    def finish(self, *others):
        while self.flying:
            total = self.advance(*others)
        return total


def after(x, *others):
    return lax.optimization_barrier((x,) + others)[0]


def chip_masks():
    masks = []
    while 2 << len(masks) < lax.axis_size("rep"):
        masks.append(2 << len(masks))
    return masks


def rep_gather(x, sends=(), lands=(), before_far=()):
    rows = x.shape[0] // 2
    masks = chip_masks()
    upper, lower = x[None, :rows], x[None, rows:]
    for step in range(len(masks)):
        if step < len(sends):
            upper, lower = after(upper, *sends[step]), after(lower, *sends[step])
        got = swap(upper, "rep", masks[step])
        other = swap(lower, "rep", masks[-1 - step])
        got, other = lax.optimization_barrier((got, other) + tuple(lands[step] if step < len(lands) else ()))[:2]
        upper = jnp.concatenate([upper, got])
        lower = jnp.stack([lower, other], axis=1).reshape((2 * lower.shape[0],) + lower.shape[1:])
    near = after(jnp.stack([upper, lower]), *before_far)
    return near, swap(near, "rep", 1)


class RepReduce:
    def __init__(self, far):
        self.got = swap(far, "rep", 1)
        self.masks = chip_masks()

    def begin(self, send_upper, send_lower, keep_upper, keep_lower):
        self.upper, self.lower = keep_upper, keep_lower
        self.sent = (send_upper, send_lower)
        self.fly(0)

    def fly(self, step):
        self.flying = (
            swap(self.sent[0], "rep", self.masks[-1 - step]),
            swap(self.sent[1], "rep", self.masks[step]),
        )

    def advance(self, *others):
        self.landed = self.flying
        upper, lower = lax.optimization_barrier(tuple(self.flying) + others)[:2]
        self.flying = None
        if self.upper.shape[0] == 1:
            self.last = (upper[0], lower[0])
            return
        half = self.upper.shape[0] // 2
        *sent, self.upper, self.lower = step_sums(self.upper, upper, self.lower, lower)
        self.sent = sent
        self.fly(len(self.masks) - half.bit_length())

    def finish(self, *others):
        while self.flying is not None:
            self.advance(*others)
        return self.upper[0], self.lower[0], *self.last


def step_kernel(keep_upper_ref, got_upper_ref, keep_lower_ref, got_lower_ref, *outs):
    half = keep_upper_ref.shape[0] // 2
    for i in range(half):
        upper = keep_upper_ref[i] + got_upper_ref[i].astype(f32)
        outs[2][i] = upper
        outs[0][i] = (keep_upper_ref[half + i] + got_upper_ref[half + i].astype(f32)).astype(bf16)
        outs[3][i] = keep_lower_ref[2 * i] + got_lower_ref[2 * i].astype(f32)
        outs[1][i] = (keep_lower_ref[2 * i + 1] + got_lower_ref[2 * i + 1].astype(f32)).astype(bf16)


def step_sums(keep_upper, got_upper, keep_lower, got_lower):
    count, rows, d = keep_upper.shape
    block = 32
    whole = pl.BlockSpec((count, block, d), lambda i: (0, i, 0))
    half = pl.BlockSpec((count // 2, block, d), lambda i: (0, i, 0))
    shape = (count // 2, rows, d)
    return kernel_call(
        step_kernel,
        (rows // block,),
        [whole] * 4,
        [half] * 4,
        [jax.ShapeDtypeStruct(shape, bf16)] * 2 + [jax.ShapeDtypeStruct(shape, f32)] * 2,
        "step_sums",
        3,
    )(keep_upper, got_upper, keep_lower, got_lower)


def place_kernel(me_ref, near_ref, far_ref, out_ref):
    rows = near_ref.shape[2]
    near = pl.program_id(0) < pl.num_programs(0) // 2
    out_ref[:rows] = jnp.where(near, near_ref[0, 0], far_ref[0, 0])
    out_ref[rows:] = jnp.where(near, near_ref[1, 0], far_ref[1, 0])


def place_columns(near, far):
    _, chips, rows, width = near.shape
    return kernel_call(
        place_kernel,
        (2 * chips,),
        [
            pl.BlockSpec((2, 1, rows, width), lambda p, me: (0, jnp.minimum(p, chips - 1), 0, 0)),
            pl.BlockSpec((2, 1, rows, width), lambda p, me: (0, jnp.maximum(p - chips, 0), 0, 0)),
        ],
        pl.BlockSpec((2 * rows, width), lambda p, me: (0, me[0] ^ (2 * lax.rem(p, chips) + p // chips))),
        jax.ShapeDtypeStruct((2 * rows, 2 * chips * width), near.dtype),
        "place_columns",
        7,
        (index_of("rep"),),
    )(index_of("rep"), near, far)


def rep_exchange(x):
    return lax.all_to_all(x, "rep", 0, 0)


def all_sum(x, axis):
    d = 1
    while d < lax.axis_size(axis):
        x = x + swap(x, axis, d)
        d *= 2
    return x


def split(x):
    high = x.astype(bf16)
    return high, (x - high.astype(f32)).astype(bf16)


def dot3(a, b, ca, cb):
    left = jnp.concatenate([a[0], a[0], a[1]], axis=ca)
    right = jnp.concatenate([b[0], b[1], b[0]], axis=cb)
    return lax.dot_general(left, right, (((ca,), (cb,)), ((), ())), preferred_element_type=f32)


def dot3_wide(a, b):
    both = jnp.dot(a[0], jnp.concatenate(b, axis=1), preferred_element_type=f32)
    return both[:, :HEAD] + both[:, HEAD:] + jnp.dot(a[1], b[0], preferred_element_type=f32)


def range_sums(matrix, x):
    width = x.shape[1]
    both = jnp.dot(matrix, jnp.concatenate(split(x), axis=1), preferred_element_type=f32)
    return both[:, :width] + both[:, width:]


def log_decay_of(z):
    return jnp.minimum(z, 0.0) - jnp.log1p(jnp.exp(-jnp.abs(z)))


def head_slice(h):
    return slice(h * HEAD, (h + 1) * HEAD)


def pack_store(ref, h, state, decay):
    ref[0, h, :HEAD, :] = state.astype(bf16)
    high, low = split(jnp.broadcast_to(decay, (16, HEAD)))
    ref[0, h, HEAD : HEAD + 16, :] = high
    ref[0, h, HEAD + 16 :, :] = low


def entry_kernel(me_ref, after_ref, x_ref, *refs):
    *pieces, scale_ref, a_ref, qfi_ref, weight_ref, last_ref, state_ref, out_ref, fb_ref = refs
    rows, wide = pieces[0].shape[0] - 16, weight_ref.shape[1]
    width = fb_ref.shape[1]

    @pl.when(pl.program_id(0) == 0)
    def _():
        for j, piece in enumerate(pieces):
            at = pl.ds(pl.multiple_of((me_ref[0] ^ j) * rows, rows), rows)
            weight_ref[at, :] = piece[:rows, :wide]
            last_ref[at, :] = piece[:rows, wide:]
            scale_ref[:, at] = piece[rows:, :rows].astype(f32)
        fb_ref[...] = scale_ref[3:4, pl.ds(pl.multiple_of(me_ref[1] * width, width), width)]

    x = x_ref[...].astype(f32)
    size = lax.rsqrt(jnp.mean(x * x, axis=1, keepdims=True) + epsilon)
    a_ref[...] = (x * size * scale_ref[0:1, :]).astype(bf16)
    qfi_ref[...] = jnp.dot(a_ref[...], weight_ref[...], preferred_element_type=f32)
    z = qfi_ref[:, width : 2 * width] + fb_ref[...]
    log_decay = log_decay_of(z)
    to_end = range_sums(after_ref[...], log_decay)
    keys = jax.nn.sigmoid(-z) * jnp.exp(to_end)
    decay = jnp.exp(jnp.sum(log_decay, axis=0, keepdims=True))
    for h in range(width // HEAD):
        at = head_slice(h)
        value = qfi_ref[:, 2 * width + h * HEAD : 2 * width + (h + 1) * HEAD]
        state = dot3(split(value), split(keys[:, at]), 0, 0)
        state_ref[0, h] = state
        pack_store(out_ref, h, state, decay[:, at])


def level_masks(size):
    row = lax.broadcasted_iota(jnp.int32, (size, size), 0)
    col = lax.broadcasted_iota(jnp.int32, (size, size), 1)
    return row, col, row ^ col


def inside_kernel(levels_ref, fb_ref, q_ref, f_ref, i_ref, *refs):
    out_ref, high_ref, low_ref = refs[-3:]
    size = q_ref.shape[0]
    count = levels_ref.shape[0] // size
    z = f_ref[...] + fb_ref[...]
    weights = jnp.exp(range_sums(levels_ref[...], log_decay_of(z)))
    keys = jax.nn.sigmoid(-z)
    q = q_ref[...]
    query = q * jax.nn.sigmoid(q)
    row, col, differ = level_masks(size)
    later = row > col
    for h in range(q_ref.shape[1] // HEAD):
        at = head_slice(h)
        hq, hk = query[:, at], keys[:, at]
        scores = jnp.where(row == col, jnp.sum(hq * hk, axis=1, keepdims=True), 0.0)
        for l in range(count):
            w = weights[l * size : (l + 1) * size, at]
            part = dot3(split(hq * w), split(hk * w), 1, 1)
            scores = jnp.where(later & ((differ >> l) == 1), part, scores)
        high, low = split(scores)
        high_ref[0, h] = high
        low_ref[0, h] = low
        out_ref[:, at] = dot3((high, low), split(i_ref[:, at]), 1, 0)


def output_kernel(upto_ref, fb_ref, scale_ref, q_ref, f_ref, inside_ref, state_ref, out_ref, u_ref):
    q = q_ref[...]
    reach = q * jax.nn.sigmoid(q) * jnp.exp(range_sums(upto_ref[...], log_decay_of(f_ref[...] + fb_ref[...])))
    for h in range(q_ref.shape[1] // HEAD):
        at = head_slice(h)
        o = inside_ref[:, at] + dot3(split(reach[:, at]), split(state_ref[0, h]), 1, 1)
        out_ref[:, at] = o
        size = lax.rsqrt(jnp.mean(o * o, axis=1, keepdims=True) + epsilon)
        u_ref[:, at] = (o * size * scale_ref[:, at]).astype(bf16)


def back_state_kernel(upto_ref, fb_ref, scale_ref, q_ref, f_ref, o_ref, du_ref, do_ref, out_ref, dscale_ref):
    @pl.when(pl.program_id(0) == 0)
    def _():
        dscale_ref[...] = jnp.zeros_like(dscale_ref)

    q = q_ref[...]
    log_decay = log_decay_of(f_ref[...] + fb_ref[...])
    reach = q * jax.nn.sigmoid(q) * jnp.exp(range_sums(upto_ref[...], log_decay))
    decay = jnp.exp(jnp.sum(log_decay, axis=0, keepdims=True))
    for h in range(q_ref.shape[1] // HEAD):
        at = head_slice(h)
        o, du = o_ref[:, at], du_ref[:, at]
        size = lax.rsqrt(jnp.mean(o * o, axis=1, keepdims=True) + epsilon)
        normed = o * size
        dscale_ref[:, at] += jnp.sum(du * normed, axis=0, keepdims=True)
        scaled = du * scale_ref[:, at]
        do = size * (scaled - normed * jnp.mean(scaled * normed, axis=1, keepdims=True))
        do_ref[:, at] = do
        pack_store(out_ref, h, dot3(split(do), split(reach[:, at]), 0, 0), decay[:, at])


def back_inside_kernel(levels_ref, fb_ref, q_ref, f_ref, i_ref, do_ref, high_ref, low_ref, *refs):
    dq_ref, dk_ref, di_ref = refs[-3:]
    size = q_ref.shape[0]
    count = levels_ref.shape[0] // size
    z = f_ref[...] + fb_ref[...]
    weights = jnp.exp(range_sums(levels_ref[...], log_decay_of(z)))
    keys = jax.nn.sigmoid(-z)
    q = q_ref[...]
    query = q * jax.nn.sigmoid(q)
    row, col, differ = level_masks(size)
    for h in range(q_ref.shape[1] // HEAD):
        at = head_slice(h)
        hq, hk = query[:, at], keys[:, at]
        value, do = i_ref[:, at], do_ref[:, at]
        value2, do2 = split(value), split(do)
        di_ref[:, at] = dot3((high_ref[0, h], low_ref[0, h]), do2, 0, 0)
        forth = dot3(do2, value2, 1, 1)
        back = dot3(value2, do2, 1, 1)
        diagonal = jnp.sum(do * value, axis=1, keepdims=True)
        dq, dk = diagonal * hk, diagonal * hq
        for l in range(count):
            w = weights[l * size : (l + 1) * size, at]
            here = (differ >> l) == 1
            forth2 = split(jnp.where(here & (row > col), forth, 0.0))
            back2 = split(jnp.where(here & (row < col), back, 0.0))
            dq += w * dot3_wide(forth2, split(hk * w))
            dk += w * dot3_wide(back2, split(hq * w))
        dq_ref[:, at] = dq
        dk_ref[:, at] = dk


def back_output_kernel(
    me_ref,
    upto_ref,
    after_ref,
    from_ref,
    fb_ref,
    q_ref,
    f_ref,
    i_ref,
    do_ref,
    dq_ref,
    dk_ref,
    di_ref,
    first_ref,
    end_ref,
    grad_ref,
    out_ref,
    again_ref,
    dbias_ref,
):
    @pl.when(pl.program_id(0) == 0)
    def _():
        dbias_ref[...] = jnp.zeros_like(dbias_ref)

    width = q_ref.shape[1]
    z = f_ref[...] + fb_ref[...]
    log_decay = log_decay_of(z)
    begin = jnp.exp(range_sums(upto_ref[...], log_decay))
    finish = jnp.exp(range_sums(after_ref[...], log_decay))
    keys = jax.nn.sigmoid(-z)
    q = q_ref[...]
    gate = jax.nn.sigmoid(q)
    query = q * gate
    for h in range(width // HEAD):
        at = head_slice(h)
        hk, hq = keys[:, at], query[:, at]
        grad = split(grad_ref[0, h])
        value, do = split(i_ref[:, at]), split(do_ref[:, at])
        dq = dq_ref[:, at] + begin[:, at] * dot3(do, split(first_ref[0, h]), 1, 0)
        dk = dk_ref[:, at] + finish[:, at] * dot3(value, grad, 1, 0)
        di = di_ref[:, at] + dot3(split(hk * finish[:, at]), grad, 1, 1)
        last = jnp.sum(grad_ref[0, h] * end_ref[0, h], axis=0, keepdims=True)
        dlog = range_sums(from_ref[...], hq * dq - hk * dk) + last
        dz = dlog * hk - dk * hk * (1.0 - hk)
        dbias_ref[:, at] += jnp.sum(dz, axis=0, keepdims=True)
        g = gate[:, at]
        out_ref[:, at] = (dq * (g * (1.0 + q[:, at] * (1.0 - g)))).astype(bf16)
        out_ref[:, slice(width + h * HEAD, width + (h + 1) * HEAD)] = dz.astype(bf16)
        out_ref[:, slice(2 * width + h * HEAD, 2 * width + (h + 1) * HEAD)] = di.astype(bf16)
    rows = out_ref.shape[0] // 2
    again_ref[0, 0, 0] = out_ref[:rows]
    again_ref[0, 1, 0] = out_ref[rows:]


def range_matrices(size):
    at = np.arange(size)
    row, col = at[:, None], at[None, :]
    upto = col <= row
    after = col > row
    since = col >= row
    levels = []
    for l in range(int(math.log2(size))):
        middle = (row >> (l + 1) << (l + 1)) + (1 << l)
        levels.append(np.where(row >= middle, (col >= middle) & (col <= row), (col > row) & (col < middle)))
    return [jnp.asarray(m, bf16) for m in (upto, after, since, np.concatenate(levels, axis=0))]


class Recurrence:
    def __init__(self, rows, width, size):
        self.size, self.width = size, width
        self.count, self.heads = rows // size, self.width // HEAD
        self.upto, self.after, self.since, self.levels = range_matrices(size)

    def whole(self, x):
        return pl.BlockSpec(x.shape, lambda s, *_: (0,) * x.ndim)

    def rows(self, column=0, wide=1, at=0):
        return pl.BlockSpec((self.size, self.width * wide), lambda s, *_: (s + at, column))

    def heads_spec(self, *tail, at=0):
        return pl.BlockSpec((1, self.heads) + tail, lambda s, *_: (s + at,) + (0,) * (1 + len(tail)))

    def rows_shape(self, dtype=f32, wide=1):
        return jax.ShapeDtypeStruct((self.count * self.size, self.width * wide), dtype)

    def heads_shape(self, *tail, dtype=f32):
        return jax.ShapeDtypeStruct((self.count, self.heads) + tail, dtype)

    def call(self, body, args, in_specs, out_specs, out_shape, name, us, prefetch=(), count=None, onto=None):
        aliases = None
        if onto is not None:
            aliases = {len(args) + k: k for k in range(len(onto))}
            args = args + tuple(onto)
            in_specs = in_specs + [pl.BlockSpec(memory_space=pl.ANY)] * len(onto)
        return kernel_call(
            body, (count or self.count,), in_specs, out_specs, out_shape, name, us, prefetch, aliases
        )(*prefetch, *args)

    def entry(self, x, pieces):
        d, wide = x.shape[1], 3 * self.width
        weight = jax.ShapeDtypeStruct((d, wide), bf16)
        last = jax.ShapeDtypeStruct((d, self.width), bf16)
        scales = jax.ShapeDtypeStruct((16, d), f32)
        row = pl.BlockSpec((self.size, d), lambda s, *_: (s, 0))
        one = jax.ShapeDtypeStruct((1, self.width), f32)
        outs = self.call(
            entry_kernel,
            (self.after, x) + tuple(pieces),
            [self.whole(self.after), row] + [self.whole(p) for p in pieces],
            [self.whole(scales), row, self.rows(0, 3), self.whole(weight), self.whole(last)]
            + [self.heads_spec(HEAD, HEAD), self.heads_spec(PACK, HEAD), self.whole(one)],
            [
                scales,
                jax.ShapeDtypeStruct(x.shape, bf16),
                self.rows_shape(f32, 3),
                weight,
                last,
                self.heads_shape(HEAD, HEAD),
                self.heads_shape(PACK, HEAD, dtype=bf16),
                one,
            ],
            "entry",
            17,
            (jnp.stack([lax.axis_index("fsdp"), lax.axis_index("rep")]).astype(jnp.int32),),
        )
        self.qfi, self.fb = outs[2], outs[7]
        return outs[:7]

    def inside(self, half, onto=None):
        x, fb, at = self.qfi, self.fb, half * (self.count // 2)
        square = self.heads_spec(self.size, self.size, at=at)
        return self.call(
            inside_kernel,
            (self.levels, fb, x, x, x),
            [self.whole(self.levels), self.whole(fb)] + [self.rows(k, at=at) for k in range(3)],
            [self.rows(at=at), square, square],
            [
                self.rows_shape(),
                self.heads_shape(self.size, self.size, dtype=bf16),
                self.heads_shape(self.size, self.size, dtype=bf16),
            ],
            "inside",
            15,
            count=self.count // 2,
            onto=onto,
        )

    def output(self, inside, first):
        x = self.qfi
        return self.call(
            output_kernel,
            (self.upto, self.fb, self.scale, x, x, inside, first),
            [self.whole(self.upto), self.whole(self.fb), self.whole(self.scale), self.rows(0), self.rows(1)]
            + [self.rows(), self.heads_spec(HEAD, HEAD)],
            [self.rows(), self.rows()],
            [self.rows_shape(), self.rows_shape(bf16)],
            "output",
            8,
        )

    def back_state(self, o, du):
        x = self.qfi
        row = jax.ShapeDtypeStruct((1, self.width), f32)
        return self.call(
            back_state_kernel,
            (self.upto, self.fb, self.scale, x, x, o, du),
            [self.whole(self.upto), self.whole(self.fb), self.whole(self.scale), self.rows(0), self.rows(1)]
            + [self.rows(), self.rows()],
            [self.rows(), self.heads_spec(PACK, HEAD), self.whole(row)],
            [self.rows_shape(), self.heads_shape(PACK, HEAD, dtype=bf16), row],
            "back_state",
            9,
        )

    def back_inside(self, do, high, low, half, onto=None):
        x, at = self.qfi, half * (self.count // 2)
        square = self.heads_spec(self.size, self.size, at=at)
        return self.call(
            back_inside_kernel,
            (self.levels, self.fb, x, x, x, do, high, low),
            [self.whole(self.levels), self.whole(self.fb)]
            + [self.rows(k, at=at) for k in range(3)]
            + [self.rows(at=at), square, square],
            [self.rows(at=at)] * 3,
            [self.rows_shape()] * 3,
            "back_inside",
            24,
            count=self.count // 2,
            onto=onto,
        )

    def back_output(self, do, dq, dk, di, first, end, grad):
        x = self.qfi
        row = jax.ShapeDtypeStruct((1, self.width), f32)
        state = self.heads_spec(HEAD, HEAD)
        half = self.count // 2

        def place(s, me):
            return (lax.rem(me[0] ^ s, 2), 0, (me[0] ^ s) // 2, 0, 0)

        return self.call(
            back_output_kernel,
            (self.upto, self.after, self.since, self.fb, x, x, x, do, dq, dk, di, first, end, grad),
            [self.whole(self.upto), self.whole(self.after), self.whole(self.since), self.whole(self.fb)]
            + [self.rows(0), self.rows(1), self.rows(2)]
            + [self.rows()] * 4
            + [state] * 3,
            [
                self.rows(0, 3),
                pl.BlockSpec((1, 2, 1, self.size // 2, self.width * 3), place),
                self.whole(row),
            ],
            [
                self.rows_shape(bf16, 3),
                jax.ShapeDtypeStruct((2, 2, half, self.size // 2, self.width * 3), bf16),
                row,
            ],
            "back_output",
            13,
            (index_of("rep"),),
        )


def parts_of(packed):
    wide = packed.astype(f32)
    return wide[:, :, :HEAD], wide[:, :, HEAD : HEAD + 1] + wide[:, :, HEAD + 16 : HEAD + 17]


def pack(state, decay):
    high, low = split(jnp.broadcast_to(decay, decay.shape[:2] + (16, HEAD)))
    return jnp.concatenate([state.astype(bf16), high, low], axis=2)


class Carry:
    def __init__(self, packed, reverse):
        self.reverse, self.shift, self.packed = reverse, 1, packed
        self.border, self.window = 0.0, 1.0
        self.send()

    def send(self):
        n, d = lax.axis_size("fsdp"), self.shift
        pairs = [(i, i - d) for i in range(d, n)] if self.reverse else [(i, i + d) for i in range(n - d)]
        self.flying = lax.ppermute(self.packed, "fsdp", pairs)
        self.sent = (self.packed,)

    def advance(self, *others):
        state, decay = parts_of(after(self.flying, *others))
        self.border = self.border + self.window * state
        self.window = self.window * decay
        self.shift *= 2
        self.flying = None
        if self.shift < lax.axis_size("fsdp"):
            own_state, own_decay = parts_of(self.packed)
            self.packed = pack(own_state + own_decay * state, own_decay * decay)
            self.send()

    def finish(self, *others):
        while self.flying is not None:
            self.advance(*others)
        return self.border


def nt(left, right):
    return lax.dot_general(left, right, (((1,), (1,)), ((), ())), preferred_element_type=f32)


def tn(left, right):
    return lax.dot_general(left, right, (((0,), (0,)), ((), ())), preferred_element_type=f32)


def middle_kernel(u_ref, weight_ref, x_ref, scale_ref, h_ref, b_ref):
    step, width = pl.program_id(0), weight_ref.shape[1]
    total = jnp.dot(u_ref[0], weight_ref[: u_ref.shape[2], :], preferred_element_type=f32)
    for r in range(1, u_ref.shape[0]):
        rows = slice(r * u_ref.shape[2], (r + 1) * u_ref.shape[2])
        total += jnp.dot(u_ref[r], weight_ref[rows, :], preferred_element_type=f32)
    at = pl.ds(pl.multiple_of(step * width, width), width)
    h_ref[:, at] = x_ref[:, at].astype(f32) + total

    @pl.when(step == pl.num_programs(0) - 1)
    def _():
        h = h_ref[...]
        size = lax.rsqrt(jnp.mean(h * h, axis=1, keepdims=True) + epsilon)
        b_ref[...] = (h * size * scale_ref[1:2, :]).astype(bf16)


def middle(u, weight, x, scales):
    rows, d = x.shape
    block = 512
    return kernel_call(
        middle_kernel,
        (d // block,),
        [whole_spec(u), pl.BlockSpec((d, block), lambda i: (0, i)), whole_spec(x), whole_spec(scales)],
        [whole_spec(x), whole_spec(x)],
        [jax.ShapeDtypeStruct(x.shape, f32), jax.ShapeDtypeStruct(x.shape, bf16)],
        "middle",
        6,
    )(u, weight, x, scales)


def back_middle_kernel(upper_ref, lower_ref, got_upper_ref, got_lower_ref, h_ref, dy_ref, scale_ref, weight_ref, *outs):
    dh_ref, dmo_ref, du_ref, dscale_ref = outs

    @pl.when(pl.program_id(0) == 0)
    def _():
        db = jnp.concatenate(
            [upper_ref[...] + got_upper_ref[...].astype(f32), lower_ref[...] + got_lower_ref[...].astype(f32)], axis=0
        )
        h = h_ref[...]
        size = lax.rsqrt(jnp.mean(h * h, axis=1, keepdims=True) + epsilon)
        normed = h * size
        dscale_ref[...] = jnp.sum(db * normed, axis=0, keepdims=True)
        scaled = db * scale_ref[1:2, :]
        dh = size * (scaled - normed * jnp.mean(scaled * normed, axis=1, keepdims=True)) + dy_ref[...].astype(f32)
        dh_ref[...] = dh
        dmo_ref[...] = dh.astype(bf16)

    total = nt(dmo_ref[...], weight_ref[...])
    width = du_ref.shape[2]
    for r in range(du_ref.shape[0]):
        du_ref[r] = total[:, r * width : (r + 1) * width]


def back_middle(parts, h, dy, scales, weight, width):
    rows, d = h.shape
    block = 512
    row = jax.ShapeDtypeStruct((1, d), f32)
    return kernel_call(
        back_middle_kernel,
        (d // block,),
        [whole_spec(x, 1) for x in parts]
        + [whole_spec(h, 1), whole_spec(dy, 1), whole_spec(scales), pl.BlockSpec((block, d), lambda i: (i, 0))],
        [whole_spec(h), whole_spec(dy), pl.BlockSpec((block // width, rows, width), lambda i: (i, 0, 0)), whole_spec(row)],
        [
            jax.ShapeDtypeStruct(h.shape, f32),
            jax.ShapeDtypeStruct(h.shape, bf16),
            jax.ShapeDtypeStruct((d // width, rows, width), f32),
            row,
        ],
        "back_middle",
        7,
    )(*parts, h, dy, scales, weight)


def joined(upper, lower, got_upper, got_lower):
    return jnp.concatenate([upper + got_upper.astype(f32), lower + got_lower.astype(f32)])


def feed_kernel(first, chunks, me_ref, b_ref, *refs):
    dy_refs, refs = refs[:chunks], refs[chunks:]
    if first:
        pieces_ref, down_ref, hidden_ref, gate_low_ref, up_low_ref, d_ref, gate_up_ref, rows_ref = refs

        @pl.when(pl.program_id(0) == 0)
        def _():
            width = pieces_ref.shape[3]
            for z in range(pieces_ref.shape[0]):
                gate_up_ref[:, :, z * width : (z + 1) * width] = pieces_ref[z]
            width = down_ref.shape[2]
            for r in range(down_ref.shape[0]):
                rows_ref[:, r * width : (r + 1) * width] = down_ref[r]
    else:
        gate_up_ref, rows_ref, hidden_ref, gate_low_ref, up_low_ref, d_ref, db_ref = refs
    d_ref[...] = jnp.concatenate([ref[...] for ref in dy_refs], axis=0)
    b = b_ref[...]
    gate = nt(b, gate_up_ref[0])
    up = nt(b, gate_up_ref[1])
    back = nt(d_ref[...], rows_ref[...])
    sigmoid = jax.nn.sigmoid(gate)
    silu = gate * sigmoid
    hidden_ref[...] = (silu * up).astype(bf16)
    gate_low_ref[...] = (back * up * (sigmoid * (1.0 + gate * (1.0 - sigmoid)))).astype(bf16)
    up_low_ref[...] = (back * silu).astype(bf16)
    if not first:
        total = jnp.dot(gate_low_ref[...], gate_up_ref[0], preferred_element_type=f32)
        total += jnp.dot(up_low_ref[...], gate_up_ref[1], preferred_element_type=f32)
        db_ref[...] = total.astype(bf16)


def feed(b, dy, weights, first):
    rows, d = b.shape
    ff = weights[-1].shape[-2]
    chips = lax.axis_size("rep") // 2
    half = dy.shape[0] // (4 * chips)
    chunks = 4

    def at(chunk):
        def block(i, me):
            q = chunks * i + chunk
            device = me[0] ^ (2 * lax.rem(q, chips) + (0 if first else 1))
            return (2 * device + q // chips, 0)

        return pl.BlockSpec((half, d), block)

    wide = pl.BlockSpec((chunks * half, d), lambda i, me: (i, 0))
    thin = pl.BlockSpec((chunks * half, ff), lambda i, me: (i, 0))
    outs, specs = [jax.ShapeDtypeStruct((rows, ff), bf16)] * 3 + [jax.ShapeDtypeStruct(b.shape, bf16)], [thin] * 3 + [wide]
    if first:
        whole = [jax.ShapeDtypeStruct((2, ff, d), bf16), jax.ShapeDtypeStruct((ff, d), bf16)]
        outs, specs = outs + whole, specs + [whole_spec(x) for x in whole]
    else:
        outs, specs = outs + [jax.ShapeDtypeStruct(b.shape, bf16)], specs + [wide]
    return kernel_call(
        functools.partial(feed_kernel, first, chunks),
        (rows // (chunks * half),),
        [wide] + [at(k) for k in range(chunks)] + [whole_spec(w, 1) for w in weights],
        specs,
        outs,
        "feed",
        20 if first else 27,
        (index_of("rep"),),
    )(index_of("rep"), b, *[dy] * chunks, *weights)


def source_kernel(count, turned, *refs):
    lefts, weights, refs = refs[: 4 * count], refs[4 * count : 5 * count], refs[5 * count :]
    got, outs = refs[:4], refs[4:]
    total = jnp.concatenate([ref[...] for ref in got], axis=0).astype(f32)
    for k in range(count):
        left = jnp.concatenate([ref[...] for ref in lefts[4 * k : 4 * k + 4]], axis=0)
        total += nt(left, weights[k][...]) if turned else jnp.dot(left, weights[k][...], preferred_element_type=f32)
    half = total.shape[0] // 2
    for q in range(2):

        @pl.when(pl.program_id(0) // (pl.num_programs(0) // 2) == q)
        def _(q=q):
            outs[2 * q][...] = total[:half].astype(outs[2 * q].dtype)
            outs[2 * q + 1][...] = total[half:].astype(outs[2 * q + 1].dtype)


def source(lefts, weights, got, rows, turned=False):
    chips = lax.axis_size("rep") // 2
    d = got.shape[1]
    steps = chips // 4

    def at(part):
        def block(s, *_):
            q, k = s // steps, 2 * lax.rem(s, steps) + part % 2
            upper = k + jnp.where(q == 0, chips // 2, 0)
            lower = chips + 2 * k + jnp.where(q == 0, 1, 0)
            return lower if part >= 2 else upper

        return block

    specs, args = [], []
    for left in lefts:
        for part in range(4):
            block = at(part)
            if left.ndim == 3:
                specs.append(pl.BlockSpec((None, rows, left.shape[2]), lambda s, block=block: (0, block(s), 0)))
            else:
                specs.append(pl.BlockSpec((rows, left.shape[1]), lambda s, block=block: (block(s), 0)))
            args.append(left)
    out = jax.ShapeDtypeStruct((chips // 2 * rows, d), bf16)
    kept = jax.ShapeDtypeStruct((chips // 2 * rows, d), f32)
    outs = kernel_call(
        functools.partial(source_kernel, len(lefts), turned),
        (2 * steps,),
        specs
        + [layer_spec(weights, k) for k in range(len(lefts))]
        + [pl.BlockSpec((rows, d), lambda s, block=at(part): (block(s), 0)) for part in range(4)],
        [pl.BlockSpec((2 * rows, d), lambda s, q=q: (jnp.clip(s - q * steps, 0, steps - 1), 0)) for q in (0, 0, 1, 1)],
        [out, out, kept, kept],
        "source",
        4 + 3 * len(lefts),
    )(*args, *[weights] * len(lefts), *[got] * 4)
    return [x.reshape(chips // 2, rows, d) for x in outs]


def grad_kernel(count, blocks, me_ref, *refs):
    lefts, rights, outs = refs[:count], refs[count : 2 * count], refs[2 * count :]
    total = tn(lefts[0][...], rights[0][...])
    for k in range(1, count):
        total += tn(lefts[k][...], rights[k][...])
    for j in range(blocks):

        @pl.when(pl.program_id(0) == blocks - 1 - j)
        def _(j=j):
            outs[j][...] = total.astype(outs[j].dtype)


def grad_blocks(lefts, rights, of_left):
    blocks = lax.axis_size("fsdp")

    def cut(x):
        width = x.shape[1] // blocks
        return pl.BlockSpec((x.shape[0], width), lambda s, me: (0, me[0] ^ (blocks - 1 - s)))

    specs = [cut(x) if of_left else whole_spec(x) for x in lefts]
    specs += [whole_spec(x) if of_left else cut(x) for x in rights]
    shape = (specs[0].block_shape[1], specs[-1].block_shape[1])
    return kernel_call(
        functools.partial(grad_kernel, len(lefts), blocks),
        (blocks,),
        specs,
        [pl.BlockSpec(shape, lambda s, me: (0, 0))] * blocks,
        [jax.ShapeDtypeStruct(shape, f32 if j == 0 else bf16) for j in range(blocks)],
        "grad",
        10,
        (index_of("fsdp"),),
    )(index_of("fsdp"), *lefts, *rights)


def grad_plain_kernel(count, *refs):
    total = tn(refs[0][...], refs[count][...])
    for k in range(1, count):
        total += tn(refs[k][...], refs[count + k][...])
    refs[-1][0] = total.astype(bf16)


def grad_plain(lefts, rights, width):
    rows, count = lefts[0].shape[1], rights[0].shape[1] // width
    return kernel_call(
        functools.partial(grad_plain_kernel, len(lefts)),
        (count,),
        [whole_spec(x) for x in lefts] + [pl.BlockSpec((x.shape[0], width), lambda s: (0, s)) for x in rights],
        pl.BlockSpec((1, rows, width), lambda s: (s, 0, 0)),
        jax.ShapeDtypeStruct((count, rows, width), bf16),
        "grad_plain",
        11,
    )(*lefts, *rights)


def grad_out_kernel(blocks, me_ref, u_ref, dmo_ref, *outs):
    total = jnp.concatenate([tn(u_ref[r], dmo_ref[...]) for r in range(u_ref.shape[0])], axis=0)
    for j in range(blocks):

        @pl.when(pl.program_id(0) == blocks - 1 - j)
        def _(j=j):
            outs[j][...] = total.astype(outs[j].dtype)


def grad_out_blocks(u, dmo):
    blocks = lax.axis_size("fsdp")
    each = u.shape[0] // blocks
    shape = (each * u.shape[2], dmo.shape[1])
    return kernel_call(
        functools.partial(grad_out_kernel, blocks),
        (blocks,),
        [pl.BlockSpec((each,) + u.shape[1:], lambda s, me: (me[0] ^ (blocks - 1 - s), 0, 0)), whole_spec(dmo)],
        [pl.BlockSpec(shape, lambda s, me: (0, 0))] * blocks,
        [jax.ShapeDtypeStruct(shape, f32 if j == 0 else bf16) for j in range(blocks)],
        "grad_out",
        6,
        (index_of("fsdp"),),
    )(index_of("fsdp"), u, dmo)


def rms_scale(value_input, scales):
    return (
        value_input
        * lax.rsqrt(jnp.mean(value_input * value_input, axis=-1, keepdims=True) + epsilon)
        * scales
    )


def product(left, right):
    return jnp.dot(left, right, preferred_element_type=f32)


def product_nt(left, right):
    return lax.dot_general(left, right, (((1,), (1,)), ((), ())), preferred_element_type=f32)


def adam(weight, first, second, gradient, step_rate, decay_on):
    first_new = beta_first * first + (1.0 - beta_first) * gradient
    second_new = beta_second * second + (1.0 - beta_second) * gradient * gradient
    first_fix = 1.0 - beta_first**STEP
    second_fix = 1.0 - beta_second**STEP
    weight_new = weight - step_rate * (
        first_new / first_fix / (jnp.sqrt(second_new / second_fix) + adam_epsilon)
        + decay_on * weight
    )
    return (weight_new, first_new, second_new)


def shards(
    tokens,
    cotangent,
    lengths,
    w_mix,
    w_in,
    w_down,
    gains,
    m_mix,
    m_in,
    m_down,
    m_gain,
    v_mix,
    v_in,
    v_down,
    v_gain,
):
    reps, planes = lax.axis_size("rep"), lax.axis_size("fsdp")
    rep, plane = lax.axis_index("rep"), lax.axis_index("fsdp")
    size = tokens.shape[1]
    width = w_mix.shape[2]
    rows = reps * size

    gain_rows = jnp.pad(gains.astype(bf16), ((0, 12), (0, 4 * width - gains.shape[1])))
    block = jnp.concatenate([w_mix[j].astype(bf16) for j in range(4)], axis=1)
    pieces = z_pieces(jnp.concatenate([block, gain_rows]))
    x_all = lax.all_gather(tokens[0], "rep", axis=0, tiled=True)
    turned = w_in.astype(bf16).transpose(0, 2, 1)
    position = plane * size + jnp.arange(size)
    valid = (position < lengths[0])[:, None]
    dy = jnp.where(valid, cotangent[0], jnp.zeros_like(cotangent[0]))
    dy_all = lax.all_gather(dy, "rep", axis=0, tiled=True)
    mixer = Recurrence(rows, width, size)
    pieces[-1] = after(pieces[-1], dy, turned)
    scales, a_all, qfi, qfi_cols, out_cols, local, packed = mixer.entry(x_all, pieces)
    mixer.scale = lax.dynamic_slice(scales, (2, rep * width), (1, width))
    ff = w_in.shape[2]
    carry = Carry(packed, False)
    part = mixer.inside(0)
    state_landed = carry.flying
    carry.advance(part[0])
    more_landed = carry.flying
    own_fb = mixer.fb
    mixer.fb = after(own_fb, carry.packed)
    inside, score_high, score_low = mixer.inside(1, part)
    mixer.fb = own_fb
    first = carry.finish(inside)
    end = local + parts_of(packed)[1] * first
    down_cols = lax.all_gather(after(w_down.astype(bf16), more_landed), "fsdp", axis=0, tiled=True)
    turned, dy_all = lax.optimization_barrier((after(turned, more_landed), dy_all))
    gate_up = lax.all_gather(turned, "fsdp", axis=0)
    o, u = mixer.output(after(inside, dy_all), first)
    u_got = rep_exchange(u.reshape(reps, size, width))
    out_full = place_columns(*rep_gather(after(out_cols, state_landed), lands=((more_landed, inside), (u_got,))))
    down_rows = rep_exchange(after(down_cols, u_got).reshape(reps, ff, width))
    h, b_own = middle(after(u_got, down_rows), out_full, tokens[0], scales)
    b_halves = rep_gather(b_own, before_far=(gate_up,))
    u_all = lax.all_gather(after(u, b_halves[1]), "rep", axis=0)

    b_halves = [half.reshape(rows // 2, D) for half in b_halves]
    hidden_near, gate_near, up_near, d_near, gate_up, down_rows = feed(b_halves[0], dy_all, (gate_up, down_rows), True)
    hidden_far, gate_far, up_far, d_far, db_far = feed(b_halves[1], dy_all, (gate_up, down_rows), False)
    db = RepReduce(db_far)
    gate_part = grad_plain([gate_near, gate_far], [after(b, db_far) for b in b_halves], D // planes)
    grad_gate = lax.psum_scatter(gate_part, "fsdp", scatter_dimension=0)
    db.begin(*source([after(gate_near, gate_part), up_near], gate_up, db.got, size // 2))
    up_part = grad_plain([up_near, up_far], [after(b, *db.sent) for b in b_halves], D // planes)
    db.advance(up_part)
    grad_up = lax.psum_scatter(after(up_part, *db.landed), "fsdp", scatter_dimension=0)
    mixed_far = product(after(hidden_far, *db.sent), down_rows).astype(bf16)
    mixed_sum = RepReduce(mixed_far)
    db_parts = db.finish(mixed_far, u_all)

    dh, dmo, du_own, grad_scale_two = back_middle(db_parts, h, dy, scales, out_full, width)
    du = rep_exchange(du_own).reshape(rows, width)
    down_part = grad_plain([after(hidden_near, du_own), hidden_far], [d_near, d_far], width)
    mixed_parts = source([after(hidden_near, down_part)], down_rows[None], mixed_sum.got, size // 2)
    do, back_packed, grad_scale_head = mixer.back_state(o, after(du, *mixed_parts))
    carry = Carry(back_packed, True)
    part = mixer.back_inside(do, score_high, score_low, 0)
    down_part = rep_exchange(after(down_part, back_packed))
    carry.advance(part[0])
    mixed_sum.begin(*lax.optimization_barrier((*mixed_parts, back_packed))[:4])
    dq, dk, di = mixer.back_inside(after(do, carry.packed, grad_gate), score_high, score_low, 1, part)
    down_part = after(down_part, dq).reshape(planes, -1, width)
    down_sum = ZReduce([block_of(down_part, plane ^ j) for j in range(planes)])
    grad_state = carry.finish(dq)
    grad_state = after(grad_state, grad_up, *mixed_sum.flying)
    dqfi, dqfi_again, grad_bias = mixer.back_output(do, dq, dk, di, first, end, grad_state)
    dqfi_again = dqfi_again.reshape(2, rows // 2, 3 * width)
    down_sum.advance(dqfi)
    qfi_sum = ZReduce(grad_blocks([a_all], [after(dqfi, *down_sum.landed)], True))
    again = after(dqfi_again, *qfi_sum.sent)
    da = RepReduce(product_nt(again[1], qfi_cols).astype(bf16))
    da.begin(*source([dqfi_again], qfi_cols[None], da.got, size // 2, True))
    gate_total, up_total = after(grad_gate, *da.sent).astype(f32), after(grad_up, *da.sent).astype(f32)
    dmo_cols = rep_exchange(after(dmo, *da.sent).reshape(size, reps, width).transpose(1, 0, 2)).reshape(rows, width)
    qfi_sum.advance(*da.sent)
    down_total = down_sum.finish(*da.sent)
    da.advance(*down_sum.landed)
    out_sum = ZReduce(grad_out_blocks(u_all, after(dmo_cols, *da.sent)))
    da_own = joined(*da.finish())
    grad_qfi_w = qfi_sum.finish(*da.landed)
    out_sum.advance(*da.landed)
    mixed_sum.advance(*da.landed)
    mixed = (h + joined(*mixed_sum.finish())).astype(bf16)
    norm_one, norm_one_pull = jax.vjp(rms_scale, tokens[0].astype(f32), scales[0])
    dx_norm, grad_scale_one = norm_one_pull(da_own)
    token_grad = dh + dx_norm
    grad_in = jnp.stack([gate_total, up_total]).transpose(0, 2, 1)
    grad_out_w = out_sum.finish()

    def spread(own):
        return lax.dynamic_update_slice_in_dim(jnp.zeros((1, D), f32), own, rep * width, 1)

    grad_gains = jnp.concatenate(
        [grad_scale_one[None], grad_scale_two, spread(grad_scale_head), spread(grad_bias)]
    )
    grad_gains = all_sum(after(all_sum(grad_gains, "rep"), *qfi_sum.landed), "fsdp")
    gain_owned = lax.dynamic_slice_in_dim(grad_gains, plane * gains.shape[1], gains.shape[1], 1)

    grad_mix = jnp.stack([grad_qfi_w[:, j * width : (j + 1) * width] for j in range(3)] + [grad_out_w])
    new_mix, first_mix, second_mix = adam(w_mix, m_mix, v_mix, grad_mix, rate_matrix, decay_matrix)
    new_in, first_in, second_in = adam(w_in, m_in, v_in, grad_in, rate_matrix, decay_matrix)
    new_down, first_down, second_down = adam(
        w_down, m_down, v_down, down_total, rate_matrix, decay_matrix
    )
    new_gains, first_gains, second_gains = adam(gains, m_gain, v_gain, gain_owned, rate_gain, 0.0)
    return (
        mixed[None],
        token_grad[None],
        new_mix,
        new_in,
        new_down,
        new_gains,
        first_mix,
        first_in,
        first_down,
        first_gains,
        second_mix,
        second_in,
        second_down,
        second_gains,
        new_mix.astype(bf16),
        new_in.astype(bf16),
        new_down.astype(bf16),
    )


def solution(mesh):
    rows = P("rep", "fsdp", None)
    stack = P(None, "fsdp", "rep")
    flat = P("fsdp", "rep")
    gain = P(None, "fsdp")
    weights = (stack, stack, flat, gain)
    return jax.shard_map(
        shards,
        mesh=mesh,
        in_specs=(rows, rows, P("rep")) + weights * 3,
        out_specs=(rows, rows) + weights * 3 + (stack, stack, flat),
        check_vma=False,
    )
```

time: 6190 us -> 750 us (0.12)
  waiting for transfers between devices: 4840 us -> 286 us
  matrix products: 709 us -> 10.1 us
  Pallas kernels: 0 us -> 298 us
  other arithmetic: 324 us -> 50.9 us
  local copies, waits for them, and re-layouts: 213 us -> 12 us
  starting transfers between devices: 0.86 us -> 65.8 us
    reduce_scatter x5 -> x2, waiting for transfers between devices: 2780 us -> 0.02 us  [the longest x1 0.02 us: shards(): grad_gate = lax.psum_scatter(gate_part, 'fsdp', scatter_dimension=0)]
    all_gather x8 -> x5, waiting for transfers between devices: 1770 us -> 28.6 us  [the longest x1 17.9 us: shards(): gate_up = lax.all_gather(turned, 'fsdp', axis=0)]
    dot_general x127 -> x2, matrix products: 709 us -> 10.1 us  [the longest x1 5.04 us: product_nt(): lax.dot_general(left, right, (((1,), (1,)), ((), ())), preferred_element_...]
    pallas_call x0 -> x24, Pallas kernels: none -> 298 us  [the longest x8 123 us: call(): kernel_call(body, (count or self.count,), in_specs, out_specs, out_shape,...]
    unnamed x17 -> x7, waiting for transfers between devices: 284 us -> 1.11 us
    ppermute x0 -> x46, waiting for transfers between devices: none -> 209 us  [the longest x42 191 us: swap(): return lax.ppermute(x, axis, [(i, i ^ d) for i in range(n)])]
    another operation x38 -> x11, other arithmetic: 146 us -> 9.84 us  [the longest x4 6.36 us: rep_gather(): near = after(jnp.stack([upper, lower]), *before_far)]
  transfers between devices with their start and end apart: 15 -> 58, of which waited for: 11 -> 30; matrix products, arithmetic and copies ran while one was open for 19% -> 8% of each run, Pallas kernels for 0% -> 39%
where the time goes in v1:
time: 750 us; the launch traced here: 739 us
  Pallas kernels  298 us (40%)
  waiting for transfers between devices  286 us (38%)
  starting transfers between devices  65.8 us (9%)
  other arithmetic  50.9 us (7%)
  between operations  16 us (2%)
  local copies, waits for them, and re-layouts  12 us (2%)
  matrix products  10.1 us (1%)
    ppermute x42, waiting for transfers between devices, swap(): return lax.ppermute(x, axis, [(i, i ^ d) for i in range(n)])  191 us
    pallas_call x8, Pallas kernels, call(): kernel_call(body, (count or self.count,), in_specs, out_specs, out_shape,...  123 us
    all_to_all x5, waiting for transfers between devices, rep_exchange(): return lax.all_to_all(x, 'rep', 0, 0)  47.4 us
    pallas_call x2, Pallas kernels, feed(): kernel_call(functools.partial(feed_kernel, first, chunks), (rows // (chun...  47.1 us
    pallas_call x3, Pallas kernels, source(): kernel_call(functools.partial(source_kernel, len(lefts), turned), (2 * st...  33.5 us
    ppermute x42, starting transfers between devices, swap(): return lax.ppermute(x, axis, [(i, i ^ d) for i in range(n)])  33.1 us
    pallas_call x3, Pallas kernels, grad_plain(): kernel_call(functools.partial(grad_plain_kernel, len(lefts)), (count,), [...  32.1 us
    all_to_all x5, starting transfers between devices, rep_exchange(): return lax.all_to_all(x, 'rep', 0, 0)  20.7 us
  transfers between devices with their start and end apart: 58, of which 30 were waited for; matrix products, arithmetic and copies ran while one was open for 8% of the time, Pallas kernels for 39%

profile of v1, /device:TPU:0, one launch (start us, length us, event | category | flops | bytes accessed | tf_op | source)
XLA Modules:
  0.0 739.0 jit_solution(10687551980414026900)
XLA Ops:
  8.7 2.3 bitcast_select_fusion.dy_ref
  11.5 3.1 collective-permute-start
  14.5 2.6 collective-permute-start.1
  17.1 44.3 %collective-permute-done.refs_1_ = bf16[528,1024]{1,0:T(8,128)(2,1)S(1)} collective-permute-done((bf16[528,1024]{1,0:T(8,128)(2,1)S(1)}, bf16[528,1024]{1,0:T(8,128)(2,1)S(1)}, u32[]{:S(2)}, u32[]{:S(2)}) %collective-permute-start) | collective-permute-done | bytes 1081376 | tf_op jit(solution)/shard_map/ppermute | solution.py:30
  61.5 2.6 collective-permute-done.1.refs_2_
  65.9 22.0 %collective-permute-done.2.refs_3_ = bf16[528,1024]{1,0:T(8,128)(2,1)} collective-permute-done((bf16[528,1024]{1,0:T(8,128)(2,1)}, bf16[528,1024]{1,0:T(8,128)(2,1)}, u32[]{:S(2)}, u32[]{:S(2)}) %collective-permute-start.2) | collective-permute-done | bytes 1081376 | tf_op jit(solution)/shard_map/ppermute | solution.py:30
  87.9 19.7 %entry.1 = (f32[16,2048]{1,0:T(8,128)S(1)}, bf16[2048,2048]{1,0:T(8,128)(2,1)}, f32[2048,768]{1,0:T(8,128)}, bf16[2048,768]{1,0:T(8,128)(2,1)}, bf16[2048,256]{1...) custom-call(s32[2]{0:T(128)S(1)} %pad_add_fusion.me_ref, ...), custom_call_target="tpu_custom_call" | custom-call | bytes 850000 | tf_op jit(solution)/shard_map/entry/pallas_call | solution.py:496
  107.6 3.7 collective-permute-start.3
  111.5 14.8 %inside.2 = (f32[2048,256]{1,0:T(8,128)}, bf16[8,2,256,256]{3,2,1,0:T(8,128)(2,1)}, bf16[8,2,256,256]{3,2,1,0:T(8,128)(2,1)}) custom-call(bf16[2048,256]{1,0:T(8,128)(2,1)S(1)} %copy-done.3, f32[1,256]{1,0:T(1,128)S(1)} %get-tuple-element.177.fb_ref, f32[2048,768]{1,0:T(8,128)} %get-tuple-element.173.q_ref.f_ref.i_ref, ...), custom_call_target="tpu_custom_call" | custom-call | bytes 750000 | tf_op jit(solution)/shard_map/inside/pallas_call | solution.py:496
  128.6 5.2 collective-permute-start.4
  134.8 11.5 %collective-permute-done.4 = bf16[8,2,160,128]{3,2,1,0:T(8,128)(2,1)S(1)} collective-permute-done((bf16[8,2,160,128]{3,2,1,0:T(8,128)(2,1)}, bf16[8,2,160,128]{3,2,1,0:T(8,128)(2,1)S(1)}, u32[]{:S(2)}, u32[]{:S(2)}) %collective-permute-start.4) | collective-permute-done | bytes 655392 | tf_op jit(solution)/shard_map/ppermute | solution.py:644
  150.9 14.8 %inside.3 = (f32[2048,256]{1,0:T(8,128)}, bf16[8,2,256,256]{3,2,1,0:T(8,128)(2,1)}, bf16[8,2,256,256]{3,2,1,0:T(8,128)(2,1)}) custom-call(bf16[2048,256]{1,0:T(8,128)(2,1)S(1)} %copy-done.3, f32[1,256]{1,0:T(1,128)S(1)} %get-tuple-element.177.fb_ref, ...), custom_call_target="tpu_custom_call", output_to_operand_aliasing={{0}: (5, {}), {1}: (6, {}), {2}: (7, {})} | custom-call | bytes 750000 | tf_op jit(solution)/shard_map/inside/pallas_call | solution.py:496
  170.9 9.4 %output.1 = (f32[2048,256]{1,0:T(8,128)}, bf16[2048,256]{1,0:T(8,128)(2,1)}) custom-call(bf16[256,256]{1,0:T(8,128)(2,1)S(1)} %copy-done.8, f32[1,256]{1,0:T(1,128)S(1)} %get-tuple-element.177.fb_ref, f32[1,256]{1,0:T(1,128)S(1)} %constant_dynamic-slice_fusion.scale_ref, f32[2048,768]{1,0:T(8,128)} %get-tuple-element.173.q_ref.f_ref.i_ref, ...), custom_call_target="tpu_custom_call" | custom-call | bytes 400000 | tf_op jit(solution)/shard_map/output/pallas_call | solution.py:496
  180.3 3.6 all-to-all-start
  184.4 17.7 %all-to-all-done.u_ref = bf16[8,256,256]{2,1,0:T(8,128)(2,1)S(1)} async-done(((bf16[8,256,256]{2,1,0:T(8,128)(2,1)}), bf16[8,256,256]{2,1,0:T(8,128)(2,1)S(1)}, u32[]{:S(2)}, u32[]{:S(2)}) %all-to-all-start) | async-done | bytes 1048608 | tf_op jit(solution)/shard_map/all_to_all | solution.py:229
  206.4 2.4 pad_maximum_fusion.near_ref
  208.8 10.7 %all-gather.11.cloned.1.call-done = bf16[5632,256]{1,0:T(8,128)(2,1)} async-done(((bf16[1408,256]{1,0:T(8,128)(2,1)}), bf16[5632,256]{1,0:T(8,128)(2,1)}) %all-gather.11.cloned.1.call-update) | async-done | bytes 2883600 | tf_op jit(solution)/shard_map/all_gather | solution.py:1026
  219.5 3.7 all-to-all-start.1
  223.2 10.1 %place_columns.1.weight_ref = bf16[2048,2048]{1,0:T(8,128)(2,1)} custom-call(s32[1]{0:T(128)} %bitcast.1.me_ref, bf16[2,4,1024,256]{3,2,1,0:T(8,128)(2,1)} %pad_maximum_fusion.near_ref, bf16[2,4,1024,256]{3,2,1,0:T(8,128)(2,1)} %collective-permute-done.9.far_ref), custom_call_target="tpu_custom_call" | custom-call | bytes 350000 | tf_op jit(solution)/shard_map/place_columns/pallas_call | solution.py:213
  233.3 25.0 %all-to-all-done.1.refs_5_ = bf16[8,704,256]{2,1,0:T(8,128)(2,1)S(1)} async-done(((bf16[8,704,256]{2,1,0:T(8,128)(2,1)}), bf16[8,704,256]{2,1,0:T(8,128)(2,1)S(1)}, u32[]{:S(2)}, u32[]{:S(2)}) %all-to-all-start.1) | async-done | bytes 2883616 | tf_op jit(solution)/shard_map/all_to_all | solution.py:229
  258.2 8.9 %middle.1 = (f32[256,2048]{1,0:T(8,128)}, bf16[256,2048]{1,0:T(8,128)(2,1)S(1)}) custom-call(bf16[8,256,256]{2,1,0:T(8,128)(2,1)} %copy-done.27, bf16[2048,2048]{1,0:T(8,128)(2,1)} %place_columns.1.weight_ref, bf16[256,2048]{1,0:T(8,128)(2,1)} %bitcast.156, f32[16,2048]{1,0:T(8,128)S(1)} %get-tuple-element.172.scale_ref), custom_call_target="tpu_custom_call" | custom-call | bytes 300000 | tf_op jit(solution)/shard_map/middle/pallas_call | solution.py:691
  268.5 11.6 %collective-permute-done.10 = bf16[1,128,2048]{2,1,0:T(8,128)(2,1)S(1)} collective-permute-done((bf16[1,128,2048]{2,1,0:T(8,128)(2,1)S(1)}, bf16[1,128,2048]{2,1,0:T(8,128)(2,1)S(1)}, u32[]{:S(2)}, u32[]{:S(2)}) %collective-permute-start.10) | collective-permute-done | bytes 524320 | tf_op jit(solution)/shard_map/ppermute | solution.py:30
  282.6 23.3 %collective-permute-done.12 = bf16[2,128,2048]{2,1,0:T(8,128)(2,1)S(1)} collective-permute-done((bf16[2,128,2048]{2,1,0:T(8,128)(2,1)S(1)}, bf16[2,128,2048]{2,1,0:T(8,128)(2,1)S(1)}, u32[]{:S(2)}, u32[]{:S(2)}) %collective-permute-start.12) | collective-permute-done | bytes 1048608 | tf_op jit(solution)/shard_map/ppermute | solution.py:30
  309.0 17.9 %all-gather.15.cloned.1.call-done = bf16[8,704,512]{2,1,0:T(8,128)(2,1)} async-done(((bf16[2,704,512]{2,1,0:T(8,128)(2,1)}), bf16[8,704,512]{2,1,0:T(8,128)(2,1)}) %all-gather.15.cloned.1.call-update) | async-done | bytes 5767184 | tf_op jit(solution)/shard_map/all_gather | solution.py:1028
  327.0 7.4 %collective-permute-done.14 = bf16[2,4,128,2048]{3,2,1,0:T(8,128)(2,1)} collective-permute-done((bf16[2,4,128,2048]{3,2,1,0:T(8,128)(2,1)}, bf16[2,4,128,2048]{3,2,1,0:T(8,128)(2,1)}, u32[]{:S(2)}, u32[]{:S(2)}) %collective-permute-start.14) | collective-permute-done | bytes 4194336 | tf_op jit(solution)/shard_map/ppermute | solution.py:30
  334.5 19.9 %feed.2 = (bf16[1024,704]{1,0:T(8,128)(2,1)S(1)}, bf16[1024,704]{1,0:T(8,128)(2,1)}, bf16[1024,704]{1,0:T(8,128)(2,1)}, bf16[1024,2048]{1,0:T(8,128)(2,1)}, bf16...) custom-call(s32[1]{0:T(128)} %bitcast.1.me_ref, bf16[1024,2048]{1,0:T(8,128)(2,1)} %bitcast.148, ...), custom_call_target="tpu_custom_call" | custom-call | bytes 1000000 | tf_op jit(solution)/shard_map/feed/pallas_call | solution.py:804
  354.4 27.2 %feed.3 = (bf16[1024,704]{1,0:T(8,128)(2,1)S(1)}, bf16[1024,704]{1,0:T(8,128)(2,1)}, bf16[1024,704]{1,0:T(8,128)(2,1)}, bf16[1024,2048]{1,0:T(8,128)(2,1)}, bf16[1024,2048]{1,0:T(8,128)(2,1)}) custom-call(s32[1]{0:T(128)} %bitcast.1.me_ref, bf16[1024,2048]{1,0:T(8,128)(2,1)} %bitcast.36.b_ref.refs_3_, ...), custom_call_target="tpu_custom_call" | custom-call | bytes 1350000 | tf_op jit(solution)/shard_map/feed/pallas_call | solution.py:804
  382.8 10.1 %grad_plain.3 = bf16[4,704,512]{2,1,0:T(8,128)(2,1)} custom-call(bf16[1024,704]{1,0:T(8,128)(2,1)S(1)} %copy-done.1, bf16[1024,704]{1,0:T(8,128)(2,1)} %get-tuple-element.207.refs_1_, bf16[1024,2048]{1,0:T(8,128)(2,1)} %bitcast.149, bf16[1024,2048]{1,0:T(8,128)(2,1)} %bitcast.36.b_ref.refs_3_), custom_call_target="tpu_custom_call" | custom-call | bytes 550000 | tf_op jit(solution)/shard_map/grad_plain/pallas_call | solution.py:914
  393.0 13.8 %source.3 = (bf16[256,2048]{1,0:T(8,128)(2,1)S(1)}, bf16[256,2048]{1,0:T(8,128)(2,1)}, f32[256,2048]{1,0:T(8,128)}, f32[256,2048]{1,0:T(8,128)}) custom-call(bf16[1024,704]{1,0:T(8,128)(2,1)} %get-tuple-element.211.refs_0_.refs_1_.refs_2_.refs_3_, bf16[1024,704]{1,0:T(8,128)(2,1)} %get-tuple-element.211.refs_0_.refs_1_.refs_2_.refs_3_, ...), custom_call_target="tpu_custom_call" | custom-call | bytes 500000 | tf_op jit(solution)/shard_map/source/pallas_call | solution.py:857
  409.7 9.8 %grad_plain.4 = bf16[4,704,512]{2,1,0:T(8,128)(2,1)} custom-call(bf16[1024,704]{1,0:T(8,128)(2,1)S(1)} %copy-done, bf16[1024,704]{1,0:T(8,128)(2,1)} %get-tuple-element.216.refs_1_, bf16[1024,2048]{1,0:T(8,128)(2,1)} %bitcast.150, bf16[1024,2048]{1,0:T(8,128)(2,1)} %bitcast.36.b_ref.refs_3_), custom_call_target="tpu_custom_call" | custom-call | bytes 550000 | tf_op jit(solution)/shard_map/grad_plain/pallas_call | solution.py:914
  419.6 12.9 %collective-permute-done.16.got_upper_ref = bf16[2,128,2048]{2,1,0:T(8,128)(2,1)} collective-permute-done((bf16[2,128,2048]{2,1,0:T(8,128)(2,1)S(1)}, bf16[2,128,2048]{2,1,0:T(8,128)(2,1)}, u32[]{:S(2)}, u32[]{:S(2)}) %collective-permute-start.16) | collective-permute-done | bytes 1048608 | tf_op jit(solution)/shard_map/ppermute | solution.py:30
  433.8 5.6 step_sums.3
  439.4 5.0 convolution_convert_fusion
  446.5 12.5 %collective-permute-done.18 = bf16[1,128,2048]{2,1,0:T(8,128)(2,1)S(1)} collective-permute-done((bf16[1,128,2048]{2,1,0:T(8,128)(2,1)}, bf16[1,128,2048]{2,1,0:T(8,128)(2,1)S(1)}, u32[]{:S(2)}, u32[]{:S(2)}) %collective-permute-start.18) | collective-permute-done | bytes 524320 | tf_op jit(solution)/shard_map/ppermute | solution.py:30
  460.2 10.3 %back_middle.1 = (f32[256,2048]{1,0:T(8,128)}, bf16[256,2048]{1,0:T(8,128)(2,1)}, f32[8,256,256]{2,1,0:T(8,128)}, f32[1,2048]{1,0:T(1,128)S(1)}) custom-call(f32[128,2048]{1,0:T(8,128)} %bitcast.172, f32[128,2048]{1,0:T(8,128)} %bitcast.173, bf16[128,2048]{1,0:T(8,128)(2,1)S(1)} %bitcast.143, bf16[128,2048]{1,0:T(8,128)(2,1)S(1)} %bitcast.144, ...), custom_call_target="tpu_custom_call" | custom-call | bytes 350000 | tf_op jit(solution)/shard_map/back_middle/pallas_call | solution.py:729
  470.5 4.8 all-to-all-start.2
  475.3 12.2 %grad_plain.5 = bf16[8,704,256]{2,1,0:T(8,128)(2,1)} custom-call(bf16[1024,704]{1,0:T(8,128)(2,1)S(1)} %get-tuple-element.235.refs_0_.refs_1_.refs_2_.refs_3_, bf16[1024,704]{1,0:T(8,128)(2,1)} %copy-done.6, bf16[1024,2048]{1,0:T(8,128)(2,1)} %get-tuple-element.233.refs_2_, bf16[1024,2048]{1,0:T(8,128)(2,1)} %get-tuple-element.234.refs_3_), custom_call_target="tpu_custom_call" | custom-call | bytes 550000 | tf_op jit(solution)/shard_map/grad_plain/pallas_call | solution.py:914
  487.5 9.7 %source.4 = (bf16[256,2048]{1,0:T(8,128)(2,1)S(1)}, bf16[256,2048]{1,0:T(8,128)(2,1)}, f32[256,2048]{1,0:T(8,128)}, f32[256,2048]{1,0:T(8,128)}) custom-call(bf16[1024,704]{1,0:T(8,128)(2,1)} %copy-done.2, bf16[1024,704]{1,0:T(8,128)(2,1)} %copy-done.2, bf16[1024,704]{1,0:T(8,128)(2,1)} %copy-done.2, bf16[1024,704]{1,0:T(8,128)(2,1)} %copy-done.2, ...), custom_call_target="tpu_custom_call" | custom-call | bytes 350000 | tf_op jit(solution)/shard_map/source/pallas_call | solution.py:857
  497.2 4.7 all-to-all-done.2
  501.9 9.2 %back_state.1 = (f32[2048,256]{1,0:T(8,128)}, bf16[8,2,160,128]{3,2,1,0:T(8,128)(2,1)S(1)}, f32[1,256]{1,0:T(1,128)S(1)}) custom-call(bf16[256,256]{1,0:T(8,128)(2,1)S(1)} %copy-done.8, f32[1,256]{1,0:T(1,128)S(1)} %get-tuple-element.177.fb_ref, f32[1,256]{1,0:T(1,128)S(1)} %constant_dynamic-slice_fusion.scale_ref, ...), custom_call_target="tpu_custom_call" | custom-call | bytes 450000 | tf_op jit(solution)/shard_map/back_state/pallas_call | solution.py:496
  511.1 4.4 all-to-all-start.3
  520.6 20.6 %back_inside.2 = (f32[2048,256]{1,0:T(8,128)}, f32[2048,256]{1,0:T(8,128)}, f32[2048,256]{1,0:T(8,128)}) custom-call(bf16[2048,256]{1,0:T(8,128)(2,1)S(1)} %copy-done.4, f32[1,256]{1,0:T(1,128)S(1)} %get-tuple-element.177.fb_ref, f32[2048,768]{1,0:T(8,128)} %get-tuple-element.173.q_ref.f_ref.i_ref, f32[2048,768]{1,0:T(8,128)} %get-tuple-element.173.q_ref.f_ref.i_ref, ...), custom_call_target="tpu_custom_call" | custom-call | bytes 1200000 | tf_op jit(solution)/shard_map/back_inside/pallas_call | solution.py:496
  545.8 20.7 %back_inside.3 = (f32[2048,256]{1,0:T(8,128)}, f32[2048,256]{1,0:T(8,128)}, f32[2048,256]{1,0:T(8,128)}) custom-call(bf16[2048,256]{1,0:T(8,128)(2,1)S(1)} %copy-done.4, f32[1,256]{1,0:T(1,128)S(1)} %get-tuple-element.177.fb_ref, f32[2048,768]{1,0:T(8,128)} %get-tuple-element.173.q_ref.f_ref.i_ref, ...), custom_call_target="tpu_custom_call", output_to_operand_aliasing={{0}: (8, {}), {1}: (9, {}), {2}: (10, {})} | custom-call | bytes 1200000 | tf_op jit(solution)/shard_map/back_inside/pallas_call | solution.py:496
  566.6 2.7 dynamic-slice_bitcast_fusion
  569.3 2.6 collective-permute-start.25
  572.0 5.9 collective-permute-done.24
  579.1 13.9 %back_output.1 = (bf16[2048,768]{1,0:T(8,128)(2,1)}, bf16[2,2,4,128,768]{4,3,2,1,0:T(8,128)(2,1)}, f32[1,256]{1,0:T(1,128)S(1)}) custom-call(s32[1]{0:T(128)} %bitcast.1.me_ref, bf16[256,256]{1,0:T(8,128)(2,1)S(1)} %copy-done.8, bf16[256,256]{1,0:T(8,128)(2,1)S(1)} %copy-done.9, bf16[256,256]{1,0:T(8,128)(2,1)S(1)} %copy-done.10, ...), custom_call_target="tpu_custom_call" | custom-call | bytes 650000 | tf_op jit(solution)/shard_map/back_output/pallas_call | solution.py:496
  593.3 11.8 %grad.1 = (f32[512,768]{1,0:T(8,128)}, bf16[512,768]{1,0:T(8,128)(2,1)S(1)}, bf16[512,768]{1,0:T(8,128)(2,1)S(1)}, bf16[512,768]{1,0:T(8,128)(2,1)}) custom-call(s32[1]{0:T(128)} %bitcast.me_ref, bf16[2048,2048]{1,0:T(8,128)(2,1)} %get-tuple-element.263.refs_0_, bf16[2048,768]{1,0:T(8,128)(2,1)} %get-tuple-element.267.refs_1_), custom_call_target="tpu_custom_call" | custom-call | bytes 500000 | tf_op jit(solution)/shard_map/grad/pallas_call | solution.py:893
  605.2 5.0 convolution_convert_fusion.1
  610.7 2.4 fusion.14
  615.1 2.7 collective-permute-done.26.refs_5_.refs_6_.refs_7_.refs_8_
  617.7 10.0 %source.5 = (bf16[256,2048]{1,0:T(8,128)(2,1)S(1)}, bf16[256,2048]{1,0:T(8,128)(2,1)}, f32[256,2048]{1,0:T(8,128)}, f32[256,2048]{1,0:T(8,128)}) custom-call(bf16[2,1024,768]{2,1,0:T(8,128)(2,1)} %bitcast.151, bf16[2,1024,768]{2,1,0:T(8,128)(2,1)} %bitcast.152, bf16[2,1024,768]{2,1,0:T(8,128)(2,1)} %bitcast.153, bf16[2,1024,768]{2,1,0:T(8,128)(2,1)} %bitcast.154, ...), custom_call_target="tpu_custom_call" | custom-call | bytes 350000 | tf_op jit(solution)/shard_map/source/pallas_call | solution.py:857
  629.8 4.3 all-to-all-start.4
  634.0 9.4 %collective-permute-done.35 = bf16[512,768]{1,0:T(8,128)(2,1)} collective-permute-done((bf16[512,768]{1,0:T(8,128)(2,1)}, bf16[512,768]{1,0:T(8,128)(2,1)}, u32[]{:S(2)}, u32[]{:S(2)}) %collective-permute-start.35) | collective-permute-done | bytes 786464 | tf_op jit(solution)/shard_map/ppermute | solution.py:30
  643.5 7.4 fusion.28
  653.1 9.1 %collective-permute-done.30 = bf16[1408,256]{1,0:T(8,128)(2,1)} collective-permute-done((bf16[1408,256]{1,0:T(8,128)(2,1)}, bf16[1408,256]{1,0:T(8,128)(2,1)}, u32[]{:S(2)}, u32[]{:S(2)}) %collective-permute-start.30) | collective-permute-done | bytes 720928 | tf_op jit(solution)/shard_map/ppermute | solution.py:30
  662.2 5.3 step_sums.4
  668.4 4.9 fusion.26
  673.3 6.0 grad_out.1
  680.9 4.6 step_sums.5
  692.8 8.2 %collective-permute-done.38 = bf16[512,256]{1,0:T(8,128)(2,1)S(1)} collective-permute-done((bf16[512,256]{1,0:T(8,128)(2,1)S(1)}, bf16[512,256]{1,0:T(8,128)(2,1)S(1)}, u32[]{:S(2)}, u32[]{:S(2)}) %collective-permute-start.38) | collective-permute-done | bytes 262176 | tf_op jit(solution)/shard_map/ppermute | solution.py:30
  703.7 11.6 %collective-permute-done.43 = f32[4,2048]{1,0:T(4,128)S(1)} collective-permute-done((f32[4,2048]{1,0:T(4,128)S(1)}, f32[4,2048]{1,0:T(4,128)S(1)}, u32[]{:S(2)}, u32[]{:S(2)}) %collective-permute-start.43) | collective-permute-done | bytes 32800 | tf_op jit(solution)/shard_map/ppermute | solution.py:30
  719.5 5.0 collective-permute-done.45
  725.3 3.8 fusion.30
  (263 shorter events, 74.7 us)
Async XLA Ops:
  7.2 80.7 %all-gather.13.cloned.1.call-start = ((), (), s32[]{:S(2)}) async-start(), calls=%async_computation.11 | async-start | bytes 9437184 | tf_op jit(solution)/shard_map/all_gather | solution.py:1004
  7.9 163.0 %all-gather.9.cloned.1.call-start = ((), (), s32[]{:S(2)}) async-start(), calls=%async_computation.7 | async-start | bytes 9437184 | tf_op jit(solution)/shard_map/all_gather | solution.py:1009
  11.0 208.5 %all-gather.11.cloned.1.call-start = ((), (), s32[]{:S(2)}) async-start(), calls=%async_computation.8 | async-start | bytes 3604480 | tf_op jit(solution)/shard_map/all_gather | solution.py:1026
  11.2 53.4 %copy-start.14 = (f32[2,512,704]{1,2,0:T(8,128)S(1)}, f32[2,512,704]{1,2,0:T(8,128)}, u32[]{:S(2)}) copy-start(f32[2,512,704]{1,2,0:T(8,128)} %param.23) | copy-start | bytes 8650756
  11.5 50.0 %collective-permute-start = (bf16[528,1024]{1,0:T(8,128)(2,1)S(1)}, bf16[528,1024]{1,0:T(8,128)(2,1)S(1)}, u32[]{:S(2)}, u32[]{:S(2)}) collective-permute-start(bf16[528,1024]{1,0:T(8,128)(2,1)S(1)} %fusion.15.refs_0_), channel_id=1, source_target_pairs={{0,1},{1,0},{2,3},{3,2},{4,5},{5,4},{6,7},{7,6},{8,9},{9,8},{10,11... | collective-permute-start | bytes 3244040 | tf_op jit(solution)/shard_map/ppermute | solution.py:30
  14.5 49.5 %collective-permute-start.1 = (bf16[528,1024]{1,0:T(8,128)(2,1)S(1)}, bf16[528,1024]{1,0:T(8,128)(2,1)}, u32[]{:S(2)}, u32[]{:S(2)}) collective-permute-start(bf16[528,1024]{1,0:T(8,128)(2,1)S(1)} %fusion.15.refs_0_), channel_id=1, source_target_pairs={{0,2},{1,3},{2,0},{3,1},{4,6},{5,7},{6,4},{7,5},{8,10},{9,11},{10,... | collective-permute-start | bytes 3244040 | tf_op jit(solution)/shard_map/ppermute | solution.py:30
  64.1 23.8 %collective-permute-start.2 = (bf16[528,1024]{1,0:T(8,128)(2,1)}, bf16[528,1024]{1,0:T(8,128)(2,1)}, u32[]{:S(2)}, u32[]{:S(2)}) collective-permute-start(bf16[528,1024]{1,0:T(8,128)(2,1)} %collective-permute-done.1.refs_2_), channel_id=1, source_target_pairs={{0,1},{1,0},{2,3},{3,2},{4,5},{5,4},{6,7},{7,6},{8,9},{9,8},{10,11... | collective-permute-start | bytes 3244040 | tf_op jit(solution)/shard_map/ppermute | solution.py:30
  64.6 23.3 %copy-start.9 = (bf16[256,256]{1,0:T(8,128)(2,1)S(1)}, bf16[256,256]{1,0:T(8,128)(2,1)}, u32[]{:S(2)}) copy-start(bf16[256,256]{1,0:T(8,128)(2,1)} %constant.91.clone.after_ref) | copy-start | bytes 393220
  107.6 18.7 %collective-permute-start.3 = (bf16[8,2,160,128]{3,2,1,0:T(8,128)(2,1)S(1)}, bf16[8,2,160,128]{3,2,1,0:T(8,128)(2,1)S(1)}, u32[]{:S(2)}, u32[]{:S(2)}) collective-permute-start(bf16[8,2,160,128]{3,2,1,0:T(8,128)(2,1)S(1)} %get-tuple-element.174), channel_id=1, source_target_pairs={{0,1},{1,2},{2,3},{4,5},{5,6},{6,7},{8,9},{9,10},{10,11},{12,13},{... | collective-permute-start | bytes 1966088 | tf_op jit(solution)/shard_map/ppermute | solution.py:644
  128.6 17.7 %collective-permute-start.4 = (bf16[8,2,160,128]{3,2,1,0:T(8,128)(2,1)}, bf16[8,2,160,128]{3,2,1,0:T(8,128)(2,1)S(1)}, u32[]{:S(2)}, u32[]{:S(2)}) collective-permute-start(bf16[8,2,160,128]{3,2,1,0:T(8,128)(2,1)} %pad_maximum_fusion.11), channel_id=1, source_target_pairs={{0,2},{1,3},{4,6},{5,7},{8,10},{9,11},{12,14},{13,15},{16,18},{17,... | collective-permute-start | bytes 1966088 | tf_op jit(solution)/shard_map/ppermute | solution.py:644
  148.0 17.8 %collective-permute-start.5 = (bf16[1,1024,256]{2,1,0:T(8,128)(2,1)S(1)}, bf16[1,1024,256]{2,1,0:T(8,128)(2,1)S(1)}, u32[]{:S(2)}, u32[]{:S(2)}) collective-permute-start(bf16[1,1024,256]{2,1,0:T(8,128)(2,1)S(1)} %get-tuple-element.364), channel_id=1, source_target_pairs={{0,8},{4,12},{8,0},{12,4},{16,24},{20,28},{24,16},{28,20},{1,9},{5... | collective-permute-start | bytes 1572872 | tf_op jit(solution)/shard_map/ppermute | solution.py:30
  149.5 16.2 %collective-permute-start.6 = (bf16[1,1024,256]{2,1,0:T(8,128)(2,1)}, bf16[1,1024,256]{2,1,0:T(8,128)(2,1)S(1)}, u32[]{:S(2)}, u32[]{:S(2)}) collective-permute-start(bf16[1,1024,256]{2,1,0:T(8,128)(2,1)} %get-tuple-element.363), channel_id=1, source_target_pairs={{0,16},{4,20},{8,24},{12,28},{16,0},{20,4},{24,8},{28,12},{1,17},{... | collective-permute-start | bytes 1572872 | tf_op jit(solution)/shard_map/ppermute | solution.py:30
  166.9 35.2 %collective-permute-start.7 = (bf16[2,1024,256]{2,1,0:T(8,128)(2,1)}, bf16[2,1024,256]{2,1,0:T(8,128)(2,1)}, u32[]{:S(2)}, u32[]{:S(2)}) collective-permute-start(bf16[2,1024,256]{2,1,0:T(8,128)(2,1)} %pad_maximum_fusion.7), channel_id=1, source_target_pairs={{0,16},{4,20},{8,24},{12,28},{16,0},{20,4},{24,8},{28,12},{1,17},{... | collective-permute-start | bytes 3145736 | tf_op jit(solution)/shard_map/ppermute | solution.py:30
  168.8 33.3 %collective-permute-start.8 = (bf16[2,1024,256]{2,1,0:T(8,128)(2,1)}, bf16[2,1024,256]{2,1,0:T(8,128)(2,1)}, u32[]{:S(2)}, u32[]{:S(2)}) collective-permute-start(bf16[2,1024,256]{2,1,0:T(8,128)(2,1)} %get-tuple-element.361), channel_id=1, source_target_pairs={{0,8},{4,12},{8,0},{12,4},{16,24},{20,28},{24,16},{28,20},{1,9},{5... | collective-permute-start | bytes 3145736 | tf_op jit(solution)/shard_map/ppermute | solution.py:30
  180.3 21.8 %all-to-all-start = ((bf16[8,256,256]{2,1,0:T(8,128)(2,1)}), bf16[8,256,256]{2,1,0:T(8,128)(2,1)S(1)}, u32[]{:S(2)}, u32[]{:S(2)}) async-start(bf16[8,256,256]{2,1,0:T(8,128)(2,1)} %bitcast.13), calls=%async_computation | async-start | bytes 2097152 | tf_op jit(solution)/shard_map/all_to_all | solution.py:229
  183.9 143.1 %all-gather.15.cloned.1.call-start = ((), (), s32[]{:S(2)}) async-start(), calls=%async_computation.12 | async-start | bytes 7208960 | tf_op jit(solution)/shard_map/all_gather | solution.py:1028
  208.8 14.4 %collective-permute-start.9 = (bf16[2,4,1024,256]{3,2,1,0:T(8,128)(2,1)}, bf16[2,4,1024,256]{3,2,1,0:T(8,128)(2,1)}, u32[]{:S(2)}, u32[]{:S(2)}) collective-permute-start(bf16[2,4,1024,256]{3,2,1,0:T(8,128)(2,1)} %pad_maximum_fusion.near_ref), channel_id=1, source_target_pairs={{0,4},{4,0},{8,12},{12,8},{16,20},{20,16},{24,28},{28,24},{1,5},{5... | collective-permute-start | bytes 12582920 | tf_op jit(solution)/shard_map/ppermute | solution.py:30
  219.5 38.7 %all-to-all-start.1 = ((bf16[8,704,256]{2,1,0:T(8,128)(2,1)}), bf16[8,704,256]{2,1,0:T(8,128)(2,1)S(1)}, u32[]{:S(2)}, u32[]{:S(2)}) async-start(bf16[8,704,256]{2,1,0:T(8,128)(2,1)} %bitcast.165), calls=%async_computation.1 | async-start | bytes 5767168 | tf_op jit(solution)/shard_map/all_to_all | solution.py:229
  223.2 237.0 %all-gather.17.cloned.1.call-start = ((), (), s32[]{:S(2)}) async-start(), calls=%async_computation.13 | async-start | bytes 9437184 | tf_op jit(solution)/shard_map/all_gather | solution.py:1035
  267.2 12.8 %collective-permute-start.10 = (bf16[1,128,2048]{2,1,0:T(8,128)(2,1)S(1)}, bf16[1,128,2048]{2,1,0:T(8,128)(2,1)S(1)}, u32[]{:S(2)}, u32[]{:S(2)}) collective-permute-start(bf16[1,128,2048]{2,1,0:T(8,128)(2,1)S(1)} %get-tuple-element.359), channel_id=1, source_target_pairs={{0,8},{4,12},{8,0},{12,4},{16,24},{20,28},{24,16},{28,20},{1,9},{5... | collective-permute-start | bytes 1572872 | tf_op jit(solution)/shard_map/ppermute | solution.py:30
  267.8 13.7 %collective-permute-start.11 = (bf16[1,128,2048]{2,1,0:T(8,128)(2,1)S(1)}, bf16[1,128,2048]{2,1,0:T(8,128)(2,1)S(1)}, u32[]{:S(2)}, u32[]{:S(2)}) collective-permute-start(bf16[1,128,2048]{2,1,0:T(8,128)(2,1)S(1)} %get-tuple-element.358), channel_id=1, source_target_pairs={{0,16},{4,20},{8,24},{12,28},{16,0},{20,4},{24,8},{28,12},{1,17},{... | collective-permute-start | bytes 1572872 | tf_op jit(solution)/shard_map/ppermute | solution.py:30
  281.6 24.3 %collective-permute-start.12 = (bf16[2,128,2048]{2,1,0:T(8,128)(2,1)S(1)}, bf16[2,128,2048]{2,1,0:T(8,128)(2,1)S(1)}, u32[]{:S(2)}, u32[]{:S(2)}) collective-permute-start(bf16[2,128,2048]{2,1,0:T(8,128)(2,1)S(1)} %pad_maximum_fusion.9), channel_id=1, source_target_pairs={{0,16},{4,20},{8,24},{12,28},{16,0},{20,4},{24,8},{28,12},{1,17},{... | collective-permute-start | bytes 3145736 | tf_op jit(solution)/shard_map/ppermute | solution.py:30
  282.2 24.0 %collective-permute-start.13 = (bf16[2,128,2048]{2,1,0:T(8,128)(2,1)S(1)}, bf16[2,128,2048]{2,1,0:T(8,128)(2,1)S(1)}, u32[]{:S(2)}, u32[]{:S(2)}) collective-permute-start(bf16[2,128,2048]{2,1,0:T(8,128)(2,1)S(1)} %get-tuple-element.356), channel_id=1, source_target_pairs={{0,8},{4,12},{8,0},{12,4},{16,24},{20,28},{24,16},{28,20},{1,9},{5... | collective-permute-start | bytes 3145736 | tf_op jit(solution)/shard_map/ppermute | solution.py:30
  326.9 7.5 %collective-permute-start.14 = (bf16[2,4,128,2048]{3,2,1,0:T(8,128)(2,1)}, bf16[2,4,128,2048]{3,2,1,0:T(8,128)(2,1)}, u32[]{:S(2)}, u32[]{:S(2)}) collective-permute-start(bf16[2,4,128,2048]{3,2,1,0:T(8,128)(2,1)} %pad_maximum_fusion.1), channel_id=1, source_target_pairs={{0,4},{4,0},{8,12},{12,8},{16,20},{20,16},{24,28},{28,24},{1,5},{5... | collective-permute-start | bytes 12582920 | tf_op jit(solution)/shard_map/ppermute | solution.py:30
  334.4 211.4 %reduce-scatter.3.cloned.1.call-start = ((), (), s32[]{:S(2)}) async-start(), calls=%async_computation.9 | async-start | bytes 3604480 | tf_op jit(solution)/shard_map/reduce_scatter | solution.py:1042
  354.4 120.9 %copy-start.2 = (bf16[1024,704]{1,0:T(8,128)(2,1)}, bf16[1024,704]{1,0:T(8,128)(2,1)S(1)}, u32[]{:S(2)}) copy-start(bf16[1024,704]{1,0:T(8,128)(2,1)S(1)} %get-tuple-element.235.refs_0_.refs_1_.refs_2_.refs_3_) | copy-start | bytes 4325380
  354.4 28.4 %copy-start.1 = (bf16[1024,704]{1,0:T(8,128)(2,1)S(1)}, bf16[1024,704]{1,0:T(8,128)(2,1)}, u32[]{:S(2)}) copy-start(bf16[1024,704]{1,0:T(8,128)(2,1)} %get-tuple-element.211.refs_0_.refs_1_.refs_2_.refs_3_) | copy-start | bytes 4325380
  382.7 10.2 %collective-permute-start.15 = (bf16[1024,2048]{1,0:T(8,128)(2,1)}, bf16[1024,2048]{1,0:T(8,128)(2,1)}, u32[]{:S(2)}, u32[]{:S(2)}) collective-permute-start(bf16[1024,2048]{1,0:T(8,128)(2,1)} %get-tuple-element.208), channel_id=1, source_target_pairs={{0,4},{4,0},{8,12},{12,8},{16,20},{20,16},{24,28},{28,24},{1,5},{5... | collective-permute-start | bytes 12582920 | tf_op jit(solution)/shard_map/ppermute | solution.py:30
  392.9 186.1 %reduce-scatter.5.cloned.1.call-start = ((), (), s32[]{:S(2)}) async-start(), calls=%async_computation.10 | async-start | bytes 3604480 | tf_op jit(solution)/shard_map/reduce_scatter | solution.py:1046
  393.0 16.8 %copy-start = (bf16[1024,704]{1,0:T(8,128)(2,1)S(1)}, bf16[1024,704]{1,0:T(8,128)(2,1)}, u32[]{:S(2)}) copy-start(bf16[1024,704]{1,0:T(8,128)(2,1)} %get-tuple-element.212.refs_4_.refs_5_.refs_6_.refs_7_.refs_0_) | copy-start | bytes 4325380
  406.8 25.7 %collective-permute-start.16 = (bf16[2,128,2048]{2,1,0:T(8,128)(2,1)S(1)}, bf16[2,128,2048]{2,1,0:T(8,128)(2,1)}, u32[]{:S(2)}, u32[]{:S(2)}) collective-permute-start(bf16[2,128,2048]{2,1,0:T(8,128)(2,1)S(1)} %bitcast.147), channel_id=1, source_target_pairs={{0,16},{4,20},{8,24},{12,28},{16,0},{20,4},{24,8},{28,12},{1,17},{... | collective-permute-start | bytes 3145736 | tf_op jit(solution)/shard_map/ppermute | solution.py:30
  408.3 25.4 %collective-permute-start.17 = (bf16[2,128,2048]{2,1,0:T(8,128)(2,1)}, bf16[2,128,2048]{2,1,0:T(8,128)(2,1)}, u32[]{:S(2)}, u32[]{:S(2)}) collective-permute-start(bf16[2,128,2048]{2,1,0:T(8,128)(2,1)} %bitcast.192), channel_id=1, source_target_pairs={{0,8},{4,12},{8,0},{12,4},{16,24},{20,28},{24,16},{28,20},{1,9},{5... | collective-permute-start | bytes 3145736 | tf_op jit(solution)/shard_map/ppermute | solution.py:30
  444.5 43.1 %collective-permute-start.20 = (bf16[1024,2048]{1,0:T(8,128)(2,1)}, bf16[1024,2048]{1,0:T(8,128)(2,1)}, u32[]{:S(2)}, u32[]{:S(2)}) collective-permute-start(bf16[1024,2048]{1,0:T(8,128)(2,1)} %convolution_convert_fusion), channel_id=1, source_target_pairs={{0,4},{4,0},{8,12},{12,8},{16,20},{20,16},{24,28},{28,24},{1,5},{5... | collective-permute-start | bytes 12582920 | tf_op jit(solution)/shard_map/ppermute | solution.py:30
  444.5 14.5 %collective-permute-start.18 = (bf16[1,128,2048]{2,1,0:T(8,128)(2,1)}, bf16[1,128,2048]{2,1,0:T(8,128)(2,1)S(1)}, u32[]{:S(2)}, u32[]{:S(2)}) collective-permute-start(bf16[1,128,2048]{2,1,0:T(8,128)(2,1)} %get-tuple-element.224), channel_id=1, source_target_pairs={{0,8},{4,12},{8,0},{12,4},{16,24},{20,28},{24,16},{28,20},{1,9},{5... | collective-permute-start | bytes 1572872 | tf_op jit(solution)/shard_map/ppermute | solution.py:30
  445.9 14.3 %collective-permute-start.19 = (bf16[1,128,2048]{2,1,0:T(8,128)(2,1)}, bf16[1,128,2048]{2,1,0:T(8,128)(2,1)S(1)}, u32[]{:S(2)}, u32[]{:S(2)}) collective-permute-start(bf16[1,128,2048]{2,1,0:T(8,128)(2,1)} %get-tuple-element.225), channel_id=1, source_target_pairs={{0,16},{4,20},{8,24},{12,28},{16,0},{20,4},{24,8},{28,12},{1,17},{... | collective-permute-start | bytes 1572872 | tf_op jit(solution)/shard_map/ppermute | solution.py:30
  470.5 31.4 %all-to-all-start.2 = ((f32[8,256,256]{2,1,0:T(8,128)}), f32[8,256,256]{2,1,0:T(8,128)}, u32[]{:S(2)}, u32[]{:S(2)}) async-start(f32[8,256,256]{2,1,0:T(8,128)} %get-tuple-element.231), calls=%async_computation.2 | async-start | bytes 4194304 | tf_op jit(solution)/shard_map/all_to_all | solution.py:229
  511.1 55.5 %all-to-all-start.3 = ((bf16[8,704,256]{2,1,0:T(8,128)(2,1)}), bf16[8,704,256]{2,1,0:T(8,128)(2,1)}, u32[]{:S(2)}, u32[]{:S(2)}) async-start(bf16[8,704,256]{2,1,0:T(8,128)(2,1)} %grad_plain.5), calls=%async_computation.5 | async-start | bytes 5767168 | tf_op jit(solution)/shard_map/all_to_all | solution.py:229
  515.6 25.6 %collective-permute-start.23 = (bf16[8,2,160,128]{3,2,1,0:T(8,128)(2,1)S(1)}, bf16[8,2,160,128]{3,2,1,0:T(8,128)(2,1)}, u32[]{:S(2)}, u32[]{:S(2)}) collective-permute-start(bf16[8,2,160,128]{3,2,1,0:T(8,128)(2,1)S(1)} %get-tuple-element.242), channel_id=1, source_target_pairs={{1,0},{2,1},{3,2},{5,4},{6,5},{7,6},{9,8},{10,9},{11,10},{13,12},{... | collective-permute-start | bytes 1966088 | tf_op jit(solution)/shard_map/ppermute | solution.py:644
  517.1 61.9 %collective-permute-start.21 = (bf16[2,128,2048]{2,1,0:T(8,128)(2,1)S(1)}, bf16[2,128,2048]{2,1,0:T(8,128)(2,1)}, u32[]{:S(2)}, u32[]{:S(2)}) collective-permute-start(bf16[2,128,2048]{2,1,0:T(8,128)(2,1)S(1)} %bitcast.145), channel_id=1, source_target_pairs={{0,16},{4,20},{8,24},{12,28},{16,0},{20,4},{24,8},{28,12},{1,17},{... | collective-permute-start | bytes 3145736 | tf_op jit(solution)/shard_map/ppermute | solution.py:30
  519.1 59.9 %collective-permute-start.22 = (bf16[2,128,2048]{2,1,0:T(8,128)(2,1)}, bf16[2,128,2048]{2,1,0:T(8,128)(2,1)}, u32[]{:S(2)}, u32[]{:S(2)}) collective-permute-start(bf16[2,128,2048]{2,1,0:T(8,128)(2,1)} %bitcast.190), channel_id=1, source_target_pairs={{0,8},{4,12},{8,0},{12,4},{16,24},{20,28},{24,16},{28,20},{1,9},{5... | collective-permute-start | bytes 3145736 | tf_op jit(solution)/shard_map/ppermute | solution.py:30
  544.5 33.4 %collective-permute-start.24 = (bf16[8,2,160,128]{3,2,1,0:T(8,128)(2,1)}, bf16[8,2,160,128]{3,2,1,0:T(8,128)(2,1)S(1)}, u32[]{:S(2)}, u32[]{:S(2)}) collective-permute-start(bf16[8,2,160,128]{3,2,1,0:T(8,128)(2,1)} %pad_maximum_fusion.12), channel_id=1, source_target_pairs={{2,0},{3,1},{6,4},{7,5},{10,8},{11,9},{14,12},{15,13},{18,16},{19,... | collective-permute-start | bytes 1966088 | tf_op jit(solution)/shard_map/ppermute | solution.py:644
  569.3 24.0 %collective-permute-start.25 = (bf16[1408,256]{1,0:T(8,128)(2,1)}, bf16[1408,256]{1,0:T(8,128)(2,1)}, u32[]{:S(2)}, u32[]{:S(2)}) collective-permute-start(bf16[1408,256]{1,0:T(8,128)(2,1)} %get-tuple-element.351), channel_id=1, source_target_pairs={{0,1},{1,0},{2,3},{3,2},{4,5},{5,4},{6,7},{7,6},{8,9},{9,8},{10,11... | collective-permute-start | bytes 2162696 | tf_op jit(solution)/shard_map/ppermute | solution.py:30
  610.2 7.5 %collective-permute-start.26 = (bf16[1024,2048]{1,0:T(8,128)(2,1)}, bf16[1024,2048]{1,0:T(8,128)(2,1)}, u32[]{:S(2)}, u32[]{:S(2)}) collective-permute-start(bf16[1024,2048]{1,0:T(8,128)(2,1)} %convolution_convert_fusion.1), channel_id=1, source_target_pairs={{0,4},{4,0},{8,12},{12,8},{16,20},{20,16},{24,28},{28,24},{1,5},{5... | collective-permute-start | bytes 12582920 | tf_op jit(solution)/shard_map/ppermute | solution.py:30
  610.5 32.9 %collective-permute-start.35 = (bf16[512,768]{1,0:T(8,128)(2,1)}, bf16[512,768]{1,0:T(8,128)(2,1)}, u32[]{:S(2)}, u32[]{:S(2)}) collective-permute-start(bf16[512,768]{1,0:T(8,128)(2,1)} %get-tuple-element.268), channel_id=1, source_target_pairs={{0,1},{1,0},{2,3},{3,2},{4,5},{5,4},{6,7},{7,6},{8,9},{9,8},{10,11... | collective-permute-start | bytes 2359304 | tf_op jit(solution)/shard_map/ppermute | solution.py:30
  613.1 49.1 %collective-permute-start.29 = (bf16[1408,256]{1,0:T(8,128)(2,1)}, bf16[1408,256]{1,0:T(8,128)(2,1)}, u32[]{:S(2)}, u32[]{:S(2)}) collective-permute-start(bf16[1408,256]{1,0:T(8,128)(2,1)} %fusion.14), channel_id=1, source_target_pairs={{0,2},{1,3},{2,0},{3,1},{4,6},{5,7},{6,4},{7,5},{8,10},{9,11},{10,... | collective-permute-start | bytes 2162696 | tf_op jit(solution)/shard_map/ppermute | solution.py:30
  613.1 49.1 %collective-permute-start.30 = (bf16[1408,256]{1,0:T(8,128)(2,1)}, bf16[1408,256]{1,0:T(8,128)(2,1)}, u32[]{:S(2)}, u32[]{:S(2)}) collective-permute-start(bf16[1408,256]{1,0:T(8,128)(2,1)} %get-tuple-element.275), channel_id=1, source_target_pairs={{0,1},{1,0},{2,3},{3,2},{4,5},{5,4},{6,7},{7,6},{8,9},{9,8},{10,11... | collective-permute-start | bytes 2162696 | tf_op jit(solution)/shard_map/ppermute | solution.py:30
  627.8 34.4 %collective-permute-start.27 = (bf16[2,128,2048]{2,1,0:T(8,128)(2,1)S(1)}, bf16[2,128,2048]{2,1,0:T(8,128)(2,1)}, u32[]{:S(2)}, u32[]{:S(2)}) collective-permute-start(bf16[2,128,2048]{2,1,0:T(8,128)(2,1)S(1)} %bitcast.146), channel_id=1, source_target_pairs={{0,16},{4,20},{8,24},{12,28},{16,0},{20,4},{24,8},{28,12},{1,17},{... | collective-permute-start | bytes 3145736 | tf_op jit(solution)/shard_map/ppermute | solution.py:30
  628.4 33.8 %collective-permute-start.28 = (bf16[2,128,2048]{2,1,0:T(8,128)(2,1)}, bf16[2,128,2048]{2,1,0:T(8,128)(2,1)}, u32[]{:S(2)}, u32[]{:S(2)}) collective-permute-start(bf16[2,128,2048]{2,1,0:T(8,128)(2,1)} %bitcast.191), channel_id=1, source_target_pairs={{0,8},{4,12},{8,0},{12,4},{16,24},{20,28},{24,16},{28,20},{1,9},{5... | collective-permute-start | bytes 3145736 | tf_op jit(solution)/shard_map/ppermute | solution.py:30
  629.8 43.5 %all-to-all-start.4 = ((bf16[8,256,256]{2,1,0:T(8,128)(2,1)}), bf16[8,256,256]{2,1,0:T(8,128)(2,1)}, u32[]{:S(2)}, u32[]{:S(2)}) async-start(bf16[8,256,256]{2,1,0:T(8,128)(2,1)} %bitcast.163), calls=%async_computation.6 | async-start | bytes 2097152 | tf_op jit(solution)/shard_map/all_to_all | solution.py:229
  643.5 59.7 %collective-permute-start.37 = (bf16[512,768]{1,0:T(8,128)(2,1)S(1)}, bf16[512,768]{1,0:T(8,128)(2,1)}, u32[]{:S(2)}, u32[]{:S(2)}) collective-permute-start(bf16[512,768]{1,0:T(8,128)(2,1)S(1)} %get-tuple-element.301), channel_id=1, source_target_pairs={{0,1},{1,0},{2,3},{3,2},{4,5},{5,4},{6,7},{7,6},{8,9},{9,8},{10,11... | collective-permute-start | bytes 2359304 | tf_op jit(solution)/shard_map/ppermute | solution.py:30
  662.2 41.5 %collective-permute-start.36 = (bf16[512,768]{1,0:T(8,128)(2,1)}, bf16[512,768]{1,0:T(8,128)(2,1)}, u32[]{:S(2)}, u32[]{:S(2)}) collective-permute-start(bf16[512,768]{1,0:T(8,128)(2,1)} %add_convert_fusion), channel_id=1, source_target_pairs={{0,2},{1,3},{2,0},{3,1},{4,6},{5,7},{6,4},{7,5},{8,10},{9,11},{10,... | collective-permute-start | bytes 2359304 | tf_op jit(solution)/shard_map/ppermute | solution.py:30
  667.5 13.1 %collective-permute-start.31 = (bf16[1,128,2048]{2,1,0:T(8,128)(2,1)S(1)}, bf16[1,128,2048]{2,1,0:T(8,128)(2,1)S(1)}, u32[]{:S(2)}, u32[]{:S(2)}) collective-permute-start(bf16[1,128,2048]{2,1,0:T(8,128)(2,1)S(1)} %get-tuple-element.279), channel_id=1, source_target_pairs={{0,8},{4,12},{8,0},{12,4},{16,24},{20,28},{24,16},{28,20},{1,9},{5... | collective-permute-start | bytes 1572872 | tf_op jit(solution)/shard_map/ppermute | solution.py:30
  668.0 12.9 %collective-permute-start.32 = (bf16[1,128,2048]{2,1,0:T(8,128)(2,1)S(1)}, bf16[1,128,2048]{2,1,0:T(8,128)(2,1)S(1)}, u32[]{:S(2)}, u32[]{:S(2)}) collective-permute-start(bf16[1,128,2048]{2,1,0:T(8,128)(2,1)S(1)} %get-tuple-element.280), channel_id=1, source_target_pairs={{0,16},{4,20},{8,24},{12,28},{16,0},{20,4},{24,8},{28,12},{1,17},{... | collective-permute-start | bytes 1572872 | tf_op jit(solution)/shard_map/ppermute | solution.py:30
  679.3 21.6 %collective-permute-start.38 = (bf16[512,256]{1,0:T(8,128)(2,1)S(1)}, bf16[512,256]{1,0:T(8,128)(2,1)S(1)}, u32[]{:S(2)}, u32[]{:S(2)}) collective-permute-start(bf16[512,256]{1,0:T(8,128)(2,1)S(1)} %get-tuple-element.308), channel_id=1, source_target_pairs={{0,1},{1,0},{2,3},{3,2},{4,5},{5,4},{6,7},{7,6},{8,9},{9,8},{10,11... | collective-permute-start | bytes 786440 | tf_op jit(solution)/shard_map/ppermute | solution.py:30
  685.5 43.6 %collective-permute-start.33 = (bf16[1,128,2048]{2,1,0:T(8,128)(2,1)S(1)}, bf16[1,128,2048]{2,1,0:T(8,128)(2,1)S(1)}, u32[]{:S(2)}, u32[]{:S(2)}) collective-permute-start(bf16[1,128,2048]{2,1,0:T(8,128)(2,1)S(1)} %get-tuple-element.285), channel_id=1, source_target_pairs={{0,8},{4,12},{8,0},{12,4},{16,24},{20,28},{24,16},{28,20},{1,9},{5... | collective-permute-start | bytes 1572872 | tf_op jit(solution)/shard_map/ppermute | solution.py:30
  689.0 1.3 collective-permute-start.41
  690.3 11.2 %collective-permute-start.42 = (f32[4,2048]{1,0:T(4,128)S(1)}, f32[4,2048]{1,0:T(4,128)S(1)}, u32[]{:S(2)}, u32[]{:S(2)}) collective-permute-start(f32[4,2048]{1,0:T(4,128)S(1)} %fusion.25), channel_id=1, source_target_pairs={{0,8},{4,12},{8,0},{12,4},{16,24},{20,28},{24,16},{28,20},{1,9},{5... | collective-permute-start | bytes 98312 | tf_op jit(solution)/shard_map/ppermute | solution.py:30
  690.9 25.0 %copy-start.34 = (f32[512,768]{1,0:T(8,128)S(1)}, f32[512,768]{1,0:T(8,128)}, u32[]{:S(2)}) copy-start(f32[512,768]{1,0:T(8,128)} %get-tuple-element.295) | copy-start | bytes 4718596
  701.0 28.1 %collective-permute-start.34 = (bf16[1,128,2048]{2,1,0:T(8,128)(2,1)S(1)}, bf16[1,128,2048]{2,1,0:T(8,128)(2,1)S(1)}, u32[]{:S(2)}, u32[]{:S(2)}) collective-permute-start(bf16[1,128,2048]{2,1,0:T(8,128)(2,1)S(1)} %get-tuple-element.286), channel_id=1, source_target_pairs={{0,16},{4,20},{8,24},{12,28},{16,0},{20,4},{24,8},{28,12},{1,17},{... | collective-permute-start | bytes 1572872 | tf_op jit(solution)/shard_map/ppermute | solution.py:30
  701.6 13.7 %collective-permute-start.43 = (f32[4,2048]{1,0:T(4,128)S(1)}, f32[4,2048]{1,0:T(4,128)S(1)}, u32[]{:S(2)}, u32[]{:S(2)}) collective-permute-start(f32[4,2048]{1,0:T(4,128)S(1)} %fusion.38), channel_id=1, source_target_pairs={{0,16},{4,20},{8,24},{12,28},{16,0},{20,4},{24,8},{28,12},{1,17},{... | collective-permute-start | bytes 98312 | tf_op jit(solution)/shard_map/ppermute | solution.py:30
  703.2 21.9 %collective-permute-start.40 = (bf16[512,256]{1,0:T(8,128)(2,1)S(1)}, bf16[512,256]{1,0:T(8,128)(2,1)S(1)}, u32[]{:S(2)}, u32[]{:S(2)}) collective-permute-start(bf16[512,256]{1,0:T(8,128)(2,1)S(1)} %get-tuple-element.312), channel_id=1, source_target_pairs={{0,1},{1,0},{2,3},{3,2},{4,5},{5,4},{6,7},{7,6},{8,9},{9,8},{10,11... | collective-permute-start | bytes 786440 | tf_op jit(solution)/shard_map/ppermute | solution.py:30
  703.7 21.5 %collective-permute-start.39 = (bf16[512,256]{1,0:T(8,128)(2,1)S(1)}, bf16[512,256]{1,0:T(8,128)(2,1)S(1)}, u32[]{:S(2)}, u32[]{:S(2)}) collective-permute-start(bf16[512,256]{1,0:T(8,128)(2,1)S(1)} %add_convert_fusion.1), channel_id=1, source_target_pairs={{0,2},{1,3},{2,0},{3,1},{4,6},{5,7},{6,4},{7,5},{8,10},{9,11},{10,... | collective-permute-start | bytes 786440 | tf_op jit(solution)/shard_map/ppermute | solution.py:30
  715.2 4.0 collective-permute-start.44
  719.3 5.2 collective-permute-start.45
  (47 other events, 240.0 us)
Sparse Core Ops, SparseCore 0:
  9.9 57.0 all-gather.12
  68.9 54.3 all-gather.8
  146.4 73.0 all-gather.10
  221.5 105.3 all-gather.14
  334.6 55.9 all-gather.16
  393.3 54.4 reduce-scatter.2
  450.7 56.0 reduce-scatter.4

commit v2 on v1

--- a/solution.py
+++ b/solution.py
@@ -1062,11 +1062,12 @@
     down_part = after(down_part, dq).reshape(planes, -1, width)
     down_sum = ZReduce([block_of(down_part, plane ^ j) for j in range(planes)])
     grad_state = carry.finish(dq)
-    grad_state = after(grad_state, grad_up, *mixed_sum.flying)
+    mixed_sum.advance(dq)
+    grad_state = after(grad_state, grad_up, *mixed_sum.sent)
     dqfi, dqfi_again, grad_bias = mixer.back_output(do, dq, dk, di, first, end, grad_state)
     dqfi_again = dqfi_again.reshape(2, rows // 2, 3 * width)
     down_sum.advance(dqfi)
-    qfi_sum = ZReduce(grad_blocks([a_all], [after(dqfi, *down_sum.landed)], True))
+    qfi_sum = ZReduce(grad_blocks([a_all], [after(dqfi, *down_sum.landed, *mixed_sum.flying)], True))
     again = after(dqfi_again, *qfi_sum.sent)
     da = RepReduce(product_nt(again[1], qfi_cols).astype(bf16))
     da.begin(*source([dqfi_again], qfi_cols[None], da.got, size // 2, True))
@@ -1079,8 +1080,7 @@
     da_own = joined(*da.finish())
     grad_qfi_w = qfi_sum.finish(*da.landed)
     out_sum.advance(*da.landed)
-    mixed_sum.advance(*da.landed)
-    mixed = (h + joined(*mixed_sum.finish())).astype(bf16)
+    mixed = (h + joined(*mixed_sum.finish(*da.landed))).astype(bf16)
     norm_one, norm_one_pull = jax.vjp(rms_scale, tokens[0].astype(f32), scales[0])
     dx_norm, grad_scale_one = norm_one_pull(da_own)
     token_grad = dh + dx_norm

time: 750 us -> 747 us (level)
  waiting for transfers between devices: 286 us -> 266 us
  starting transfers between devices: 65.8 us -> 81.9 us
    ppermute x42, starting transfers between devices: 33.1 us -> 49.1 us  [swap(): return lax.ppermute(x, axis, [(i, i ^ d) for i in range(n)])]
    ppermute x42, waiting for transfers between devices: 191 us -> 177 us  [swap(): return lax.ppermute(x, axis, [(i, i ^ d) for i in range(n)])]
  transfers between devices with their start and end apart: 58 -> 58, of which waited for: 30 -> 28; matrix products, arithmetic and copies ran while one was open for 8% -> 8% of each run, Pallas kernels for 39% -> 39%
where the time goes in v2:
time: 747 us; the launch traced here: 736 us
  Pallas kernels  299 us (40%)
  waiting for transfers between devices  266 us (36%)
  starting transfers between devices  81.9 us (11%)
  other arithmetic  53.4 us (7%)
  between operations  16 us (2%)
  local copies, waits for them, and re-layouts  10.6 us (1%)
  matrix products  10 us (1%)
    ppermute x42, waiting for transfers between devices, swap(): return lax.ppermute(x, axis, [(i, i ^ d) for i in range(n)])  177 us
    pallas_call x8, Pallas kernels, call(): kernel_call(body, (count or self.count,), in_specs, out_specs, out_shape,...  123 us
    ppermute x42, starting transfers between devices, swap(): return lax.ppermute(x, axis, [(i, i ^ d) for i in range(n)])  49.1 us
    all_to_all x5, waiting for transfers between devices, rep_exchange(): return lax.all_to_all(x, 'rep', 0, 0)  47.3 us
    pallas_call x2, Pallas kernels, feed(): kernel_call(functools.partial(feed_kernel, first, chunks), (rows // (chun...  47 us
    pallas_call x3, Pallas kernels, source(): kernel_call(functools.partial(source_kernel, len(lefts), turned), (2 * st...  33.6 us
    pallas_call x3, Pallas kernels, grad_plain(): kernel_call(functools.partial(grad_plain_kernel, len(lefts)), (count,), [...  32.2 us
    all_to_all x5, starting transfers between devices, rep_exchange(): return lax.all_to_all(x, 'rep', 0, 0)  20.6 us
  transfers between devices with their start and end apart: 58, of which 28 were waited for; matrix products, arithmetic and copies ran while one was open for 8% of the time, Pallas kernels for 39%

profile of v2, /device:TPU:0, one launch (start us, length us, event | category | flops | bytes accessed | tf_op | source)
XLA Modules:
  0.0 736.2 jit_solution(12513482772542817721)
XLA Ops:
  8.7 2.4 bitcast_select_fusion.dy_ref
  11.5 3.1 collective-permute-start
  14.6 2.6 collective-permute-start.1
  17.2 44.3 %collective-permute-done.refs_1_ = bf16[528,1024]{1,0:T(8,128)(2,1)S(1)} collective-permute-done((bf16[528,1024]{1,0:T(8,128)(2,1)S(1)}, bf16[528,1024]{1,0:T(8,128)(2,1)S(1)}, u32[]{:S(2)}, u32[]{:S(2)}) %collective-permute-start) | collective-permute-done | bytes 1081376 | tf_op jit(solution)/shard_map/ppermute | solution.py:30
  61.5 2.6 collective-permute-done.1.refs_2_
  65.9 22.0 %collective-permute-done.2.refs_3_ = bf16[528,1024]{1,0:T(8,128)(2,1)} collective-permute-done((bf16[528,1024]{1,0:T(8,128)(2,1)}, bf16[528,1024]{1,0:T(8,128)(2,1)}, u32[]{:S(2)}, u32[]{:S(2)}) %collective-permute-start.2) | collective-permute-done | bytes 1081376 | tf_op jit(solution)/shard_map/ppermute | solution.py:30
  87.9 19.8 %entry.1 = (f32[16,2048]{1,0:T(8,128)S(1)}, bf16[2048,2048]{1,0:T(8,128)(2,1)}, f32[2048,768]{1,0:T(8,128)}, bf16[2048,768]{1,0:T(8,128)(2,1)}, bf16[2048,256]{1...) custom-call(s32[2]{0:T(128)S(1)} %pad_add_fusion.me_ref, ...), custom_call_target="tpu_custom_call" | custom-call | bytes 850000 | tf_op jit(solution)/shard_map/entry/pallas_call | solution.py:496
  107.7 3.7 collective-permute-start.3
  111.5 14.8 %inside.2 = (f32[2048,256]{1,0:T(8,128)}, bf16[8,2,256,256]{3,2,1,0:T(8,128)(2,1)}, bf16[8,2,256,256]{3,2,1,0:T(8,128)(2,1)}) custom-call(bf16[2048,256]{1,0:T(8,128)(2,1)S(1)} %copy-done.3, f32[1,256]{1,0:T(1,128)S(1)} %get-tuple-element.177.fb_ref, f32[2048,768]{1,0:T(8,128)} %get-tuple-element.173.q_ref.f_ref.i_ref, ...), custom_call_target="tpu_custom_call" | custom-call | bytes 750000 | tf_op jit(solution)/shard_map/inside/pallas_call | solution.py:496
  128.7 5.3 collective-permute-start.4
  134.9 11.5 %collective-permute-done.4 = bf16[8,2,160,128]{3,2,1,0:T(8,128)(2,1)S(1)} collective-permute-done((bf16[8,2,160,128]{3,2,1,0:T(8,128)(2,1)}, bf16[8,2,160,128]{3,2,1,0:T(8,128)(2,1)S(1)}, u32[]{:S(2)}, u32[]{:S(2)}) %collective-permute-start.4) | collective-permute-done | bytes 655392 | tf_op jit(solution)/shard_map/ppermute | solution.py:644
  151.0 14.8 %inside.3 = (f32[2048,256]{1,0:T(8,128)}, bf16[8,2,256,256]{3,2,1,0:T(8,128)(2,1)}, bf16[8,2,256,256]{3,2,1,0:T(8,128)(2,1)}) custom-call(bf16[2048,256]{1,0:T(8,128)(2,1)S(1)} %copy-done.3, f32[1,256]{1,0:T(1,128)S(1)} %get-tuple-element.177.fb_ref, ...), custom_call_target="tpu_custom_call", output_to_operand_aliasing={{0}: (5, {}), {1}: (6, {}), {2}: (7, {})} | custom-call | bytes 750000 | tf_op jit(solution)/shard_map/inside/pallas_call | solution.py:496
  171.0 9.4 %output.1 = (f32[2048,256]{1,0:T(8,128)}, bf16[2048,256]{1,0:T(8,128)(2,1)}) custom-call(bf16[256,256]{1,0:T(8,128)(2,1)S(1)} %copy-done.8, f32[1,256]{1,0:T(1,128)S(1)} %get-tuple-element.177.fb_ref, f32[1,256]{1,0:T(1,128)S(1)} %constant_dynamic-slice_fusion.scale_ref, f32[2048,768]{1,0:T(8,128)} %get-tuple-element.173.q_ref.f_ref.i_ref, ...), custom_call_target="tpu_custom_call" | custom-call | bytes 400000 | tf_op jit(solution)/shard_map/output/pallas_call | solution.py:496
  180.4 3.6 all-to-all-start
  184.6 17.6 %all-to-all-done.u_ref = bf16[8,256,256]{2,1,0:T(8,128)(2,1)S(1)} async-done(((bf16[8,256,256]{2,1,0:T(8,128)(2,1)}), bf16[8,256,256]{2,1,0:T(8,128)(2,1)S(1)}, u32[]{:S(2)}, u32[]{:S(2)}) %all-to-all-start) | async-done | bytes 1048608 | tf_op jit(solution)/shard_map/all_to_all | solution.py:229
  208.8 10.8 %all-gather.11.cloned.1.call-done = bf16[5632,256]{1,0:T(8,128)(2,1)} async-done(((bf16[1408,256]{1,0:T(8,128)(2,1)}), bf16[5632,256]{1,0:T(8,128)(2,1)}) %all-gather.11.cloned.1.call-update) | async-done | bytes 2883600 | tf_op jit(solution)/shard_map/all_gather | solution.py:1026
  219.6 3.7 all-to-all-start.1
  223.3 10.0 %place_columns.1.weight_ref = bf16[2048,2048]{1,0:T(8,128)(2,1)} custom-call(s32[1]{0:T(128)} %bitcast.1.me_ref, bf16[2,4,1024,256]{3,2,1,0:T(8,128)(2,1)} %pad_maximum_fusion.near_ref, bf16[2,4,1024,256]{3,2,1,0:T(8,128)(2,1)} %collective-permute-done.9.far_ref), custom_call_target="tpu_custom_call" | custom-call | bytes 350000 | tf_op jit(solution)/shard_map/place_columns/pallas_call | solution.py:213
  233.3 25.0 %all-to-all-done.1.refs_5_ = bf16[8,704,256]{2,1,0:T(8,128)(2,1)S(1)} async-done(((bf16[8,704,256]{2,1,0:T(8,128)(2,1)}), bf16[8,704,256]{2,1,0:T(8,128)(2,1)S(1)}, u32[]{:S(2)}, u32[]{:S(2)}) %all-to-all-start.1) | async-done | bytes 2883616 | tf_op jit(solution)/shard_map/all_to_all | solution.py:229
  258.3 8.8 %middle.1 = (f32[256,2048]{1,0:T(8,128)}, bf16[256,2048]{1,0:T(8,128)(2,1)S(1)}) custom-call(bf16[8,256,256]{2,1,0:T(8,128)(2,1)} %copy-done.27, bf16[2048,2048]{1,0:T(8,128)(2,1)} %place_columns.1.weight_ref, bf16[256,2048]{1,0:T(8,128)(2,1)} %bitcast.156, f32[16,2048]{1,0:T(8,128)S(1)} %get-tuple-element.172.scale_ref), custom_call_target="tpu_custom_call" | custom-call | bytes 300000 | tf_op jit(solution)/shard_map/middle/pallas_call | solution.py:691
  268.5 11.6 %collective-permute-done.10 = bf16[1,128,2048]{2,1,0:T(8,128)(2,1)S(1)} collective-permute-done((bf16[1,128,2048]{2,1,0:T(8,128)(2,1)S(1)}, bf16[1,128,2048]{2,1,0:T(8,128)(2,1)S(1)}, u32[]{:S(2)}, u32[]{:S(2)}) %collective-permute-start.10) | collective-permute-done | bytes 524320 | tf_op jit(solution)/shard_map/ppermute | solution.py:30
  282.6 23.3 %collective-permute-done.12 = bf16[2,128,2048]{2,1,0:T(8,128)(2,1)S(1)} collective-permute-done((bf16[2,128,2048]{2,1,0:T(8,128)(2,1)S(1)}, bf16[2,128,2048]{2,1,0:T(8,128)(2,1)S(1)}, u32[]{:S(2)}, u32[]{:S(2)}) %collective-permute-start.12) | collective-permute-done | bytes 1048608 | tf_op jit(solution)/shard_map/ppermute | solution.py:30
  306.7 2.4 pad_maximum_fusion.1
  309.1 17.9 %all-gather.15.cloned.1.call-done = bf16[8,704,512]{2,1,0:T(8,128)(2,1)} async-done(((bf16[2,704,512]{2,1,0:T(8,128)(2,1)}), bf16[8,704,512]{2,1,0:T(8,128)(2,1)}) %all-gather.15.cloned.1.call-update) | async-done | bytes 5767184 | tf_op jit(solution)/shard_map/all_gather | solution.py:1028
  327.1 7.4 %collective-permute-done.14 = bf16[2,4,128,2048]{3,2,1,0:T(8,128)(2,1)} collective-permute-done((bf16[2,4,128,2048]{3,2,1,0:T(8,128)(2,1)}, bf16[2,4,128,2048]{3,2,1,0:T(8,128)(2,1)}, u32[]{:S(2)}, u32[]{:S(2)}) %collective-permute-start.14) | collective-permute-done | bytes 4194336 | tf_op jit(solution)/shard_map/ppermute | solution.py:30
  334.6 19.8 %feed.2 = (bf16[1024,704]{1,0:T(8,128)(2,1)S(1)}, bf16[1024,704]{1,0:T(8,128)(2,1)}, bf16[1024,704]{1,0:T(8,128)(2,1)}, bf16[1024,2048]{1,0:T(8,128)(2,1)}, bf16...) custom-call(s32[1]{0:T(128)} %bitcast.1.me_ref, bf16[1024,2048]{1,0:T(8,128)(2,1)} %bitcast.148, ...), custom_call_target="tpu_custom_call" | custom-call | bytes 1000000 | tf_op jit(solution)/shard_map/feed/pallas_call | solution.py:804
  354.4 27.2 %feed.3 = (bf16[1024,704]{1,0:T(8,128)(2,1)S(1)}, bf16[1024,704]{1,0:T(8,128)(2,1)}, bf16[1024,704]{1,0:T(8,128)(2,1)}, bf16[1024,2048]{1,0:T(8,128)(2,1)}, bf16[1024,2048]{1,0:T(8,128)(2,1)}) custom-call(s32[1]{0:T(128)} %bitcast.1.me_ref, bf16[1024,2048]{1,0:T(8,128)(2,1)} %bitcast.36.b_ref.refs_3_, ...), custom_call_target="tpu_custom_call" | custom-call | bytes 1350000 | tf_op jit(solution)/shard_map/feed/pallas_call | solution.py:804
  382.8 10.1 %grad_plain.3 = bf16[4,704,512]{2,1,0:T(8,128)(2,1)} custom-call(bf16[1024,704]{1,0:T(8,128)(2,1)S(1)} %copy-done.1, bf16[1024,704]{1,0:T(8,128)(2,1)} %get-tuple-element.207.refs_1_, bf16[1024,2048]{1,0:T(8,128)(2,1)} %bitcast.149, bf16[1024,2048]{1,0:T(8,128)(2,1)} %bitcast.36.b_ref.refs_3_), custom_call_target="tpu_custom_call" | custom-call | bytes 550000 | tf_op jit(solution)/shard_map/grad_plain/pallas_call | solution.py:914
  393.0 13.8 %source.3 = (bf16[256,2048]{1,0:T(8,128)(2,1)S(1)}, bf16[256,2048]{1,0:T(8,128)(2,1)}, f32[256,2048]{1,0:T(8,128)}, f32[256,2048]{1,0:T(8,128)}) custom-call(bf16[1024,704]{1,0:T(8,128)(2,1)} %get-tuple-element.211.refs_0_.refs_1_.refs_2_.refs_3_, bf16[1024,704]{1,0:T(8,128)(2,1)} %get-tuple-element.211.refs_0_.refs_1_.refs_2_.refs_3_, ...), custom_call_target="tpu_custom_call" | custom-call | bytes 500000 | tf_op jit(solution)/shard_map/source/pallas_call | solution.py:857
  409.8 9.8 %grad_plain.4 = bf16[4,704,512]{2,1,0:T(8,128)(2,1)} custom-call(bf16[1024,704]{1,0:T(8,128)(2,1)S(1)} %copy-done, bf16[1024,704]{1,0:T(8,128)(2,1)} %get-tuple-element.216.refs_1_, bf16[1024,2048]{1,0:T(8,128)(2,1)} %bitcast.150, bf16[1024,2048]{1,0:T(8,128)(2,1)} %bitcast.36.b_ref.refs_3_), custom_call_target="tpu_custom_call" | custom-call | bytes 550000 | tf_op jit(solution)/shard_map/grad_plain/pallas_call | solution.py:914
  419.6 12.9 %collective-permute-done.16.got_upper_ref = bf16[2,128,2048]{2,1,0:T(8,128)(2,1)} collective-permute-done((bf16[2,128,2048]{2,1,0:T(8,128)(2,1)S(1)}, bf16[2,128,2048]{2,1,0:T(8,128)(2,1)}, u32[]{:S(2)}, u32[]{:S(2)}) %collective-permute-start.16) | collective-permute-done | bytes 1048608 | tf_op jit(solution)/shard_map/ppermute | solution.py:30
  433.8 5.6 step_sums.3
  439.4 5.0 convolution_convert_fusion
  446.5 12.5 %collective-permute-done.18 = bf16[1,128,2048]{2,1,0:T(8,128)(2,1)S(1)} collective-permute-done((bf16[1,128,2048]{2,1,0:T(8,128)(2,1)}, bf16[1,128,2048]{2,1,0:T(8,128)(2,1)S(1)}, u32[]{:S(2)}, u32[]{:S(2)}) %collective-permute-start.18) | collective-permute-done | bytes 524320 | tf_op jit(solution)/shard_map/ppermute | solution.py:30
  460.2 10.3 %back_middle.1 = (f32[256,2048]{1,0:T(8,128)}, bf16[256,2048]{1,0:T(8,128)(2,1)}, f32[8,256,256]{2,1,0:T(8,128)}, f32[1,2048]{1,0:T(1,128)S(1)}) custom-call(f32[128,2048]{1,0:T(8,128)} %bitcast.172, f32[128,2048]{1,0:T(8,128)} %bitcast.173, bf16[128,2048]{1,0:T(8,128)(2,1)S(1)} %bitcast.143, bf16[128,2048]{1,0:T(8,128)(2,1)S(1)} %bitcast.144, ...), custom_call_target="tpu_custom_call" | custom-call | bytes 350000 | tf_op jit(solution)/shard_map/back_middle/pallas_call | solution.py:729
  470.5 4.8 all-to-all-start.2
  475.3 12.3 %grad_plain.5 = bf16[8,704,256]{2,1,0:T(8,128)(2,1)} custom-call(bf16[1024,704]{1,0:T(8,128)(2,1)S(1)} %get-tuple-element.235.refs_0_.refs_1_.refs_2_.refs_3_, bf16[1024,704]{1,0:T(8,128)(2,1)} %copy-done.6, bf16[1024,2048]{1,0:T(8,128)(2,1)} %get-tuple-element.233.refs_2_, bf16[1024,2048]{1,0:T(8,128)(2,1)} %get-tuple-element.234.refs_3_), custom_call_target="tpu_custom_call" | custom-call | bytes 550000 | tf_op jit(solution)/shard_map/grad_plain/pallas_call | solution.py:914
  487.5 9.7 %source.4 = (bf16[256,2048]{1,0:T(8,128)(2,1)S(1)}, bf16[256,2048]{1,0:T(8,128)(2,1)}, f32[256,2048]{1,0:T(8,128)}, f32[256,2048]{1,0:T(8,128)}) custom-call(bf16[1024,704]{1,0:T(8,128)(2,1)} %copy-done.2, bf16[1024,704]{1,0:T(8,128)(2,1)} %copy-done.2, bf16[1024,704]{1,0:T(8,128)(2,1)} %copy-done.2, bf16[1024,704]{1,0:T(8,128)(2,1)} %copy-done.2, ...), custom_call_target="tpu_custom_call" | custom-call | bytes 350000 | tf_op jit(solution)/shard_map/source/pallas_call | solution.py:857
  497.3 4.6 all-to-all-done.2
  501.9 9.1 %back_state.1 = (f32[2048,256]{1,0:T(8,128)}, bf16[8,2,160,128]{3,2,1,0:T(8,128)(2,1)S(1)}, f32[1,256]{1,0:T(1,128)S(1)}) custom-call(bf16[256,256]{1,0:T(8,128)(2,1)S(1)} %copy-done.8, f32[1,256]{1,0:T(1,128)S(1)} %get-tuple-element.177.fb_ref, f32[1,256]{1,0:T(1,128)S(1)} %constant_dynamic-slice_fusion.scale_ref, ...), custom_call_target="tpu_custom_call" | custom-call | bytes 450000 | tf_op jit(solution)/shard_map/back_state/pallas_call | solution.py:496
  511.1 4.4 all-to-all-start.3
  520.5 20.6 %back_inside.2 = (f32[2048,256]{1,0:T(8,128)}, f32[2048,256]{1,0:T(8,128)}, f32[2048,256]{1,0:T(8,128)}) custom-call(bf16[2048,256]{1,0:T(8,128)(2,1)S(1)} %copy-done.4, f32[1,256]{1,0:T(1,128)S(1)} %get-tuple-element.177.fb_ref, f32[2048,768]{1,0:T(8,128)} %get-tuple-element.173.q_ref.f_ref.i_ref, f32[2048,768]{1,0:T(8,128)} %get-tuple-element.173.q_ref.f_ref.i_ref, ...), custom_call_target="tpu_custom_call" | custom-call | bytes 1200000 | tf_op jit(solution)/shard_map/back_inside/pallas_call | solution.py:496
  545.8 20.8 %back_inside.3 = (f32[2048,256]{1,0:T(8,128)}, f32[2048,256]{1,0:T(8,128)}, f32[2048,256]{1,0:T(8,128)}) custom-call(bf16[2048,256]{1,0:T(8,128)(2,1)S(1)} %copy-done.4, f32[1,256]{1,0:T(1,128)S(1)} %get-tuple-element.177.fb_ref, f32[2048,768]{1,0:T(8,128)} %get-tuple-element.173.q_ref.f_ref.i_ref, ...), custom_call_target="tpu_custom_call", output_to_operand_aliasing={{0}: (8, {}), {1}: (9, {}), {2}: (10, {})} | custom-call | bytes 1200000 | tf_op jit(solution)/shard_map/back_inside/pallas_call | solution.py:496
  566.6 2.5 dynamic-slice_bitcast_fusion
  569.1 2.6 collective-permute-start.27
  572.2 4.6 step_sums.4
  581.1 13.8 %back_output.1 = (bf16[2048,768]{1,0:T(8,128)(2,1)}, bf16[2,2,4,128,768]{4,3,2,1,0:T(8,128)(2,1)}, f32[1,256]{1,0:T(1,128)S(1)}) custom-call(s32[1]{0:T(128)} %bitcast.1.me_ref, bf16[256,256]{1,0:T(8,128)(2,1)S(1)} %copy-done.8, bf16[256,256]{1,0:T(8,128)(2,1)S(1)} %copy-done.9, bf16[256,256]{1,0:T(8,128)(2,1)S(1)} %copy-done.10, ...), custom_call_target="tpu_custom_call" | custom-call | bytes 650000 | tf_op jit(solution)/shard_map/back_output/pallas_call | solution.py:496
  594.9 11.9 %grad.1 = (f32[512,768]{1,0:T(8,128)}, bf16[512,768]{1,0:T(8,128)(2,1)S(1)}, bf16[512,768]{1,0:T(8,128)(2,1)S(1)}, bf16[512,768]{1,0:T(8,128)(2,1)}) custom-call(s32[1]{0:T(128)} %bitcast.me_ref, bf16[2048,2048]{1,0:T(8,128)(2,1)} %get-tuple-element.269.refs_0_, bf16[2048,768]{1,0:T(8,128)(2,1)} %get-tuple-element.273.refs_1_), custom_call_target="tpu_custom_call" | custom-call | bytes 500000 | tf_op jit(solution)/shard_map/grad/pallas_call | solution.py:893
  606.8 5.0 convolution_convert_fusion.1
  612.3 2.4 fusion.14
  614.7 2.7 collective-permute-start.31
  619.3 10.0 %source.5 = (bf16[256,2048]{1,0:T(8,128)(2,1)S(1)}, bf16[256,2048]{1,0:T(8,128)(2,1)}, f32[256,2048]{1,0:T(8,128)}, f32[256,2048]{1,0:T(8,128)}) custom-call(bf16[2,1024,768]{2,1,0:T(8,128)(2,1)} %bitcast.151, bf16[2,1024,768]{2,1,0:T(8,128)(2,1)} %bitcast.152, bf16[2,1024,768]{2,1,0:T(8,128)(2,1)} %bitcast.153, bf16[2,1024,768]{2,1,0:T(8,128)(2,1)} %bitcast.154, ...), custom_call_target="tpu_custom_call" | custom-call | bytes 350000 | tf_op jit(solution)/shard_map/source/pallas_call | solution.py:857
  633.8 4.2 all-to-all-start.4
  638.0 10.3 %collective-permute-done.35 = bf16[512,768]{1,0:T(8,128)(2,1)} collective-permute-done((bf16[512,768]{1,0:T(8,128)(2,1)}, bf16[512,768]{1,0:T(8,128)(2,1)}, u32[]{:S(2)}, u32[]{:S(2)}) %collective-permute-start.35) | collective-permute-done | bytes 786464 | tf_op jit(solution)/shard_map/ppermute | solution.py:30
  648.3 7.4 %fusion.28 = (bf16[2,512,704]{1,2,0:T(8,128)(2,1)}, f32[2,512,704]{1,2,0:T(8,128)}, f32[2,512,704]{1,2,0:T(8,128)}, f32[2,512,704]{1,2,0:T(8,128)}) fusion(f32[2,512,704]{1,2,0:T(8,128)} %param.23, bf16[1,704,512]{2,1,0:T(8,128)(2,1)} %reduce-scatter.5.cloned.1.call-done, bf16[1,704,512]{2,1,0:T(8,128)(2,1)} %reduce-scatter.3.cloned.1.call-done, ...), kind=kLoop, calls=%fused_computation.111 | loop fusion | flops 12255232 | bytes 20185088 | tf_op jit(solution)/shard_map/convert_element_type | solution.py:1122
  657.9 5.9 collective-permute-done.32
  663.8 2.6 collective-permute-start.36
  666.4 5.3 step_sums.5
  675.1 4.9 fusion.26
  680.0 6.2 grad_out.1
  688.5 14.1 %collective-permute-done.38 = bf16[512,256]{1,0:T(8,128)(2,1)S(1)} collective-permute-done((bf16[512,256]{1,0:T(8,128)(2,1)S(1)}, bf16[512,256]{1,0:T(8,128)(2,1)S(1)}, u32[]{:S(2)}, u32[]{:S(2)}) %collective-permute-start.38) | collective-permute-done | bytes 262176 | tf_op jit(solution)/shard_map/ppermute | solution.py:30
  703.0 2.6 collective-permute-start.39
  720.3 4.2 collective-permute-done.45
  725.3 3.8 fusion.30
  (263 shorter events, 81.5 us)
Async XLA Ops:
  7.2 80.7 %all-gather.13.cloned.1.call-start = ((), (), s32[]{:S(2)}) async-start(), calls=%async_computation.11 | async-start | bytes 9437184 | tf_op jit(solution)/shard_map/all_gather | solution.py:1004
  7.9 163.1 %all-gather.9.cloned.1.call-start = ((), (), s32[]{:S(2)}) async-start(), calls=%async_computation.7 | async-start | bytes 9437184 | tf_op jit(solution)/shard_map/all_gather | solution.py:1009
  11.0 208.5 %all-gather.11.cloned.1.call-start = ((), (), s32[]{:S(2)}) async-start(), calls=%async_computation.8 | async-start | bytes 3604480 | tf_op jit(solution)/shard_map/all_gather | solution.py:1026
  11.2 53.4 %copy-start.14 = (f32[2,512,704]{1,2,0:T(8,128)S(1)}, f32[2,512,704]{1,2,0:T(8,128)}, u32[]{:S(2)}) copy-start(f32[2,512,704]{1,2,0:T(8,128)} %param.23) | copy-start | bytes 8650756
  11.5 50.0 %collective-permute-start = (bf16[528,1024]{1,0:T(8,128)(2,1)S(1)}, bf16[528,1024]{1,0:T(8,128)(2,1)S(1)}, u32[]{:S(2)}, u32[]{:S(2)}) collective-permute-start(bf16[528,1024]{1,0:T(8,128)(2,1)S(1)} %fusion.15.refs_0_), channel_id=1, source_target_pairs={{0,1},{1,0},{2,3},{3,2},{4,5},{5,4},{6,7},{7,6},{8,9},{9,8},{10,11... | collective-permute-start | bytes 3244040 | tf_op jit(solution)/shard_map/ppermute | solution.py:30
  14.6 49.5 %collective-permute-start.1 = (bf16[528,1024]{1,0:T(8,128)(2,1)S(1)}, bf16[528,1024]{1,0:T(8,128)(2,1)}, u32[]{:S(2)}, u32[]{:S(2)}) collective-permute-start(bf16[528,1024]{1,0:T(8,128)(2,1)S(1)} %fusion.15.refs_0_), channel_id=1, source_target_pairs={{0,2},{1,3},{2,0},{3,1},{4,6},{5,7},{6,4},{7,5},{8,10},{9,11},{10,... | collective-permute-start | bytes 3244040 | tf_op jit(solution)/shard_map/ppermute | solution.py:30
  64.1 23.8 %collective-permute-start.2 = (bf16[528,1024]{1,0:T(8,128)(2,1)}, bf16[528,1024]{1,0:T(8,128)(2,1)}, u32[]{:S(2)}, u32[]{:S(2)}) collective-permute-start(bf16[528,1024]{1,0:T(8,128)(2,1)} %collective-permute-done.1.refs_2_), channel_id=1, source_target_pairs={{0,1},{1,0},{2,3},{3,2},{4,5},{5,4},{6,7},{7,6},{8,9},{9,8},{10,11... | collective-permute-start | bytes 3244040 | tf_op jit(solution)/shard_map/ppermute | solution.py:30
  64.6 23.3 %copy-start.9 = (bf16[256,256]{1,0:T(8,128)(2,1)S(1)}, bf16[256,256]{1,0:T(8,128)(2,1)}, u32[]{:S(2)}) copy-start(bf16[256,256]{1,0:T(8,128)(2,1)} %constant.91.clone.after_ref) | copy-start | bytes 393220
  107.7 18.7 %collective-permute-start.3 = (bf16[8,2,160,128]{3,2,1,0:T(8,128)(2,1)S(1)}, bf16[8,2,160,128]{3,2,1,0:T(8,128)(2,1)S(1)}, u32[]{:S(2)}, u32[]{:S(2)}) collective-permute-start(bf16[8,2,160,128]{3,2,1,0:T(8,128)(2,1)S(1)} %get-tuple-element.174), channel_id=1, source_target_pairs={{0,1},{1,2},{2,3},{4,5},{5,6},{6,7},{8,9},{9,10},{10,11},{12,13},{... | collective-permute-start | bytes 1966088 | tf_op jit(solution)/shard_map/ppermute | solution.py:644
  128.7 17.7 %collective-permute-start.4 = (bf16[8,2,160,128]{3,2,1,0:T(8,128)(2,1)}, bf16[8,2,160,128]{3,2,1,0:T(8,128)(2,1)S(1)}, u32[]{:S(2)}, u32[]{:S(2)}) collective-permute-start(bf16[8,2,160,128]{3,2,1,0:T(8,128)(2,1)} %pad_maximum_fusion.11), channel_id=1, source_target_pairs={{0,2},{1,3},{4,6},{5,7},{8,10},{9,11},{12,14},{13,15},{16,18},{17,... | collective-permute-start | bytes 1966088 | tf_op jit(solution)/shard_map/ppermute | solution.py:644
  148.1 17.7 %collective-permute-start.5 = (bf16[1,1024,256]{2,1,0:T(8,128)(2,1)S(1)}, bf16[1,1024,256]{2,1,0:T(8,128)(2,1)S(1)}, u32[]{:S(2)}, u32[]{:S(2)}) collective-permute-start(bf16[1,1024,256]{2,1,0:T(8,128)(2,1)S(1)} %get-tuple-element.364), channel_id=1, source_target_pairs={{0,8},{4,12},{8,0},{12,4},{16,24},{20,28},{24,16},{28,20},{1,9},{5... | collective-permute-start | bytes 1572872 | tf_op jit(solution)/shard_map/ppermute | solution.py:30
  149.6 16.2 %collective-permute-start.6 = (bf16[1,1024,256]{2,1,0:T(8,128)(2,1)}, bf16[1,1024,256]{2,1,0:T(8,128)(2,1)S(1)}, u32[]{:S(2)}, u32[]{:S(2)}) collective-permute-start(bf16[1,1024,256]{2,1,0:T(8,128)(2,1)} %get-tuple-element.363), channel_id=1, source_target_pairs={{0,16},{4,20},{8,24},{12,28},{16,0},{20,4},{24,8},{28,12},{1,17},{... | collective-permute-start | bytes 1572872 | tf_op jit(solution)/shard_map/ppermute | solution.py:30
  167.0 35.2 %collective-permute-start.7 = (bf16[2,1024,256]{2,1,0:T(8,128)(2,1)}, bf16[2,1024,256]{2,1,0:T(8,128)(2,1)}, u32[]{:S(2)}, u32[]{:S(2)}) collective-permute-start(bf16[2,1024,256]{2,1,0:T(8,128)(2,1)} %pad_maximum_fusion.7), channel_id=1, source_target_pairs={{0,16},{4,20},{8,24},{12,28},{16,0},{20,4},{24,8},{28,12},{1,17},{... | collective-permute-start | bytes 3145736 | tf_op jit(solution)/shard_map/ppermute | solution.py:30
  168.9 33.3 %collective-permute-start.8 = (bf16[2,1024,256]{2,1,0:T(8,128)(2,1)}, bf16[2,1024,256]{2,1,0:T(8,128)(2,1)}, u32[]{:S(2)}, u32[]{:S(2)}) collective-permute-start(bf16[2,1024,256]{2,1,0:T(8,128)(2,1)} %get-tuple-element.361), channel_id=1, source_target_pairs={{0,8},{4,12},{8,0},{12,4},{16,24},{20,28},{24,16},{28,20},{1,9},{5... | collective-permute-start | bytes 3145736 | tf_op jit(solution)/shard_map/ppermute | solution.py:30
  180.4 21.8 %all-to-all-start = ((bf16[8,256,256]{2,1,0:T(8,128)(2,1)}), bf16[8,256,256]{2,1,0:T(8,128)(2,1)S(1)}, u32[]{:S(2)}, u32[]{:S(2)}) async-start(bf16[8,256,256]{2,1,0:T(8,128)(2,1)} %bitcast.13), calls=%async_computation | async-start | bytes 2097152 | tf_op jit(solution)/shard_map/all_to_all | solution.py:229
  184.0 143.0 %all-gather.15.cloned.1.call-start = ((), (), s32[]{:S(2)}) async-start(), calls=%async_computation.12 | async-start | bytes 7208960 | tf_op jit(solution)/shard_map/all_gather | solution.py:1028
  208.8 14.5 %collective-permute-start.9 = (bf16[2,4,1024,256]{3,2,1,0:T(8,128)(2,1)}, bf16[2,4,1024,256]{3,2,1,0:T(8,128)(2,1)}, u32[]{:S(2)}, u32[]{:S(2)}) collective-permute-start(bf16[2,4,1024,256]{3,2,1,0:T(8,128)(2,1)} %pad_maximum_fusion.near_ref), channel_id=1, source_target_pairs={{0,4},{4,0},{8,12},{12,8},{16,20},{20,16},{24,28},{28,24},{1,5},{5... | collective-permute-start | bytes 12582920 | tf_op jit(solution)/shard_map/ppermute | solution.py:30
  219.6 38.7 %all-to-all-start.1 = ((bf16[8,704,256]{2,1,0:T(8,128)(2,1)}), bf16[8,704,256]{2,1,0:T(8,128)(2,1)S(1)}, u32[]{:S(2)}, u32[]{:S(2)}) async-start(bf16[8,704,256]{2,1,0:T(8,128)(2,1)} %bitcast.165), calls=%async_computation.1 | async-start | bytes 5767168 | tf_op jit(solution)/shard_map/all_to_all | solution.py:229
  223.2 237.0 %all-gather.17.cloned.1.call-start = ((), (), s32[]{:S(2)}) async-start(), calls=%async_computation.13 | async-start | bytes 9437184 | tf_op jit(solution)/shard_map/all_gather | solution.py:1035
  267.2 12.8 %collective-permute-start.10 = (bf16[1,128,2048]{2,1,0:T(8,128)(2,1)S(1)}, bf16[1,128,2048]{2,1,0:T(8,128)(2,1)S(1)}, u32[]{:S(2)}, u32[]{:S(2)}) collective-permute-start(bf16[1,128,2048]{2,1,0:T(8,128)(2,1)S(1)} %get-tuple-element.359), channel_id=1, source_target_pairs={{0,8},{4,12},{8,0},{12,4},{16,24},{20,28},{24,16},{28,20},{1,9},{5... | collective-permute-start | bytes 1572872 | tf_op jit(solution)/shard_map/ppermute | solution.py:30
  267.8 13.7 %collective-permute-start.11 = (bf16[1,128,2048]{2,1,0:T(8,128)(2,1)S(1)}, bf16[1,128,2048]{2,1,0:T(8,128)(2,1)S(1)}, u32[]{:S(2)}, u32[]{:S(2)}) collective-permute-start(bf16[1,128,2048]{2,1,0:T(8,128)(2,1)S(1)} %get-tuple-element.358), channel_id=1, source_target_pairs={{0,16},{4,20},{8,24},{12,28},{16,0},{20,4},{24,8},{28,12},{1,17},{... | collective-permute-start | bytes 1572872 | tf_op jit(solution)/shard_map/ppermute | solution.py:30
  281.6 24.3 %collective-permute-start.12 = (bf16[2,128,2048]{2,1,0:T(8,128)(2,1)S(1)}, bf16[2,128,2048]{2,1,0:T(8,128)(2,1)S(1)}, u32[]{:S(2)}, u32[]{:S(2)}) collective-permute-start(bf16[2,128,2048]{2,1,0:T(8,128)(2,1)S(1)} %pad_maximum_fusion.9), channel_id=1, source_target_pairs={{0,16},{4,20},{8,24},{12,28},{16,0},{20,4},{24,8},{28,12},{1,17},{... | collective-permute-start | bytes 3145736 | tf_op jit(solution)/shard_map/ppermute | solution.py:30
  282.2 23.9 %collective-permute-start.13 = (bf16[2,128,2048]{2,1,0:T(8,128)(2,1)S(1)}, bf16[2,128,2048]{2,1,0:T(8,128)(2,1)S(1)}, u32[]{:S(2)}, u32[]{:S(2)}) collective-permute-start(bf16[2,128,2048]{2,1,0:T(8,128)(2,1)S(1)} %get-tuple-element.356), channel_id=1, source_target_pairs={{0,8},{4,12},{8,0},{12,4},{16,24},{20,28},{24,16},{28,20},{1,9},{5... | collective-permute-start | bytes 3145736 | tf_op jit(solution)/shard_map/ppermute | solution.py:30
  327.0 7.5 %collective-permute-start.14 = (bf16[2,4,128,2048]{3,2,1,0:T(8,128)(2,1)}, bf16[2,4,128,2048]{3,2,1,0:T(8,128)(2,1)}, u32[]{:S(2)}, u32[]{:S(2)}) collective-permute-start(bf16[2,4,128,2048]{3,2,1,0:T(8,128)(2,1)} %pad_maximum_fusion.1), channel_id=1, source_target_pairs={{0,4},{4,0},{8,12},{12,8},{16,20},{20,16},{24,28},{28,24},{1,5},{5... | collective-permute-start | bytes 12582920 | tf_op jit(solution)/shard_map/ppermute | solution.py:30
  334.5 211.3 %reduce-scatter.3.cloned.1.call-start = ((), (), s32[]{:S(2)}) async-start(), calls=%async_computation.9 | async-start | bytes 3604480 | tf_op jit(solution)/shard_map/reduce_scatter | solution.py:1042
  354.4 120.9 %copy-start.2 = (bf16[1024,704]{1,0:T(8,128)(2,1)}, bf16[1024,704]{1,0:T(8,128)(2,1)S(1)}, u32[]{:S(2)}) copy-start(bf16[1024,704]{1,0:T(8,128)(2,1)S(1)} %get-tuple-element.235.refs_0_.refs_1_.refs_2_.refs_3_) | copy-start | bytes 4325380
  354.4 28.4 %copy-start.1 = (bf16[1024,704]{1,0:T(8,128)(2,1)S(1)}, bf16[1024,704]{1,0:T(8,128)(2,1)}, u32[]{:S(2)}) copy-start(bf16[1024,704]{1,0:T(8,128)(2,1)} %get-tuple-element.211.refs_0_.refs_1_.refs_2_.refs_3_) | copy-start | bytes 4325380
  382.7 10.2 %collective-permute-start.15 = (bf16[1024,2048]{1,0:T(8,128)(2,1)}, bf16[1024,2048]{1,0:T(8,128)(2,1)}, u32[]{:S(2)}, u32[]{:S(2)}) collective-permute-start(bf16[1024,2048]{1,0:T(8,128)(2,1)} %get-tuple-element.208), channel_id=1, source_target_pairs={{0,4},{4,0},{8,12},{12,8},{16,20},{20,16},{24,28},{28,24},{1,5},{5... | collective-permute-start | bytes 12582920 | tf_op jit(solution)/shard_map/ppermute | solution.py:30
  392.9 188.1 %reduce-scatter.5.cloned.1.call-start = ((), (), s32[]{:S(2)}) async-start(), calls=%async_computation.10 | async-start | bytes 3604480 | tf_op jit(solution)/shard_map/reduce_scatter | solution.py:1046
  393.0 16.8 %copy-start = (bf16[1024,704]{1,0:T(8,128)(2,1)S(1)}, bf16[1024,704]{1,0:T(8,128)(2,1)}, u32[]{:S(2)}) copy-start(bf16[1024,704]{1,0:T(8,128)(2,1)} %get-tuple-element.212.refs_4_.refs_5_.refs_6_.refs_7_.refs_0_) | copy-start | bytes 4325380
  406.8 25.7 %collective-permute-start.16 = (bf16[2,128,2048]{2,1,0:T(8,128)(2,1)S(1)}, bf16[2,128,2048]{2,1,0:T(8,128)(2,1)}, u32[]{:S(2)}, u32[]{:S(2)}) collective-permute-start(bf16[2,128,2048]{2,1,0:T(8,128)(2,1)S(1)} %bitcast.147), channel_id=1, source_target_pairs={{0,16},{4,20},{8,24},{12,28},{16,0},{20,4},{24,8},{28,12},{1,17},{... | collective-permute-start | bytes 3145736 | tf_op jit(solution)/shard_map/ppermute | solution.py:30
  408.3 25.5 %collective-permute-start.17 = (bf16[2,128,2048]{2,1,0:T(8,128)(2,1)}, bf16[2,128,2048]{2,1,0:T(8,128)(2,1)}, u32[]{:S(2)}, u32[]{:S(2)}) collective-permute-start(bf16[2,128,2048]{2,1,0:T(8,128)(2,1)} %bitcast.192), channel_id=1, source_target_pairs={{0,8},{4,12},{8,0},{12,4},{16,24},{20,28},{24,16},{28,20},{1,9},{5... | collective-permute-start | bytes 3145736 | tf_op jit(solution)/shard_map/ppermute | solution.py:30
  444.5 43.1 %collective-permute-start.20 = (bf16[1024,2048]{1,0:T(8,128)(2,1)}, bf16[1024,2048]{1,0:T(8,128)(2,1)}, u32[]{:S(2)}, u32[]{:S(2)}) collective-permute-start(bf16[1024,2048]{1,0:T(8,128)(2,1)} %convolution_convert_fusion), channel_id=1, source_target_pairs={{0,4},{4,0},{8,12},{12,8},{16,20},{20,16},{24,28},{28,24},{1,5},{5... | collective-permute-start | bytes 12582920 | tf_op jit(solution)/shard_map/ppermute | solution.py:30
  444.5 14.5 %collective-permute-start.18 = (bf16[1,128,2048]{2,1,0:T(8,128)(2,1)}, bf16[1,128,2048]{2,1,0:T(8,128)(2,1)S(1)}, u32[]{:S(2)}, u32[]{:S(2)}) collective-permute-start(bf16[1,128,2048]{2,1,0:T(8,128)(2,1)} %get-tuple-element.224), channel_id=1, source_target_pairs={{0,8},{4,12},{8,0},{12,4},{16,24},{20,28},{24,16},{28,20},{1,9},{5... | collective-permute-start | bytes 1572872 | tf_op jit(solution)/shard_map/ppermute | solution.py:30
  445.9 14.3 %collective-permute-start.19 = (bf16[1,128,2048]{2,1,0:T(8,128)(2,1)}, bf16[1,128,2048]{2,1,0:T(8,128)(2,1)S(1)}, u32[]{:S(2)}, u32[]{:S(2)}) collective-permute-start(bf16[1,128,2048]{2,1,0:T(8,128)(2,1)} %get-tuple-element.225), channel_id=1, source_target_pairs={{0,16},{4,20},{8,24},{12,28},{16,0},{20,4},{24,8},{28,12},{1,17},{... | collective-permute-start | bytes 1572872 | tf_op jit(solution)/shard_map/ppermute | solution.py:30
  470.5 31.4 %all-to-all-start.2 = ((f32[8,256,256]{2,1,0:T(8,128)}), f32[8,256,256]{2,1,0:T(8,128)}, u32[]{:S(2)}, u32[]{:S(2)}) async-start(f32[8,256,256]{2,1,0:T(8,128)} %get-tuple-element.231), calls=%async_computation.2 | async-start | bytes 4194304 | tf_op jit(solution)/shard_map/all_to_all | solution.py:229
  511.1 55.5 %all-to-all-start.3 = ((bf16[8,704,256]{2,1,0:T(8,128)(2,1)}), bf16[8,704,256]{2,1,0:T(8,128)(2,1)}, u32[]{:S(2)}, u32[]{:S(2)}) async-start(bf16[8,704,256]{2,1,0:T(8,128)(2,1)} %grad_plain.5), calls=%async_computation.5 | async-start | bytes 5767168 | tf_op jit(solution)/shard_map/all_to_all | solution.py:229
  515.5 25.6 %collective-permute-start.23 = (bf16[8,2,160,128]{3,2,1,0:T(8,128)(2,1)S(1)}, bf16[8,2,160,128]{3,2,1,0:T(8,128)(2,1)}, u32[]{:S(2)}, u32[]{:S(2)}) collective-permute-start(bf16[8,2,160,128]{3,2,1,0:T(8,128)(2,1)S(1)} %get-tuple-element.242), channel_id=1, source_target_pairs={{1,0},{2,1},{3,2},{5,4},{6,5},{7,6},{9,8},{10,9},{11,10},{13,12},{... | collective-permute-start | bytes 1966088 | tf_op jit(solution)/shard_map/ppermute | solution.py:644
  517.1 55.0 %collective-permute-start.21 = (bf16[2,128,2048]{2,1,0:T(8,128)(2,1)S(1)}, bf16[2,128,2048]{2,1,0:T(8,128)(2,1)}, u32[]{:S(2)}, u32[]{:S(2)}) collective-permute-start(bf16[2,128,2048]{2,1,0:T(8,128)(2,1)S(1)} %bitcast.145), channel_id=1, source_target_pairs={{0,16},{4,20},{8,24},{12,28},{16,0},{20,4},{24,8},{28,12},{1,17},{... | collective-permute-start | bytes 3145736 | tf_op jit(solution)/shard_map/ppermute | solution.py:30
  519.1 53.1 %collective-permute-start.22 = (bf16[2,128,2048]{2,1,0:T(8,128)(2,1)}, bf16[2,128,2048]{2,1,0:T(8,128)(2,1)}, u32[]{:S(2)}, u32[]{:S(2)}) collective-permute-start(bf16[2,128,2048]{2,1,0:T(8,128)(2,1)} %bitcast.190), channel_id=1, source_target_pairs={{0,8},{4,12},{8,0},{12,4},{16,24},{20,28},{24,16},{28,20},{1,9},{5... | collective-permute-start | bytes 3145736 | tf_op jit(solution)/shard_map/ppermute | solution.py:30
  544.5 34.4 %collective-permute-start.26 = (bf16[8,2,160,128]{3,2,1,0:T(8,128)(2,1)}, bf16[8,2,160,128]{3,2,1,0:T(8,128)(2,1)}, u32[]{:S(2)}, u32[]{:S(2)}) collective-permute-start(bf16[8,2,160,128]{3,2,1,0:T(8,128)(2,1)} %pad_maximum_fusion.12), channel_id=1, source_target_pairs={{2,0},{3,1},{6,4},{7,5},{10,8},{11,9},{14,12},{15,13},{18,16},{19,... | collective-permute-start | bytes 1966088 | tf_op jit(solution)/shard_map/ppermute | solution.py:644
  569.1 25.8 %collective-permute-start.27 = (bf16[1408,256]{1,0:T(8,128)(2,1)}, bf16[1408,256]{1,0:T(8,128)(2,1)}, u32[]{:S(2)}, u32[]{:S(2)}) collective-permute-start(bf16[1408,256]{1,0:T(8,128)(2,1)} %get-tuple-element.351), channel_id=1, source_target_pairs={{0,1},{1,0},{2,3},{3,2},{4,5},{5,4},{6,7},{7,6},{8,9},{9,8},{10,11... | collective-permute-start | bytes 2162696 | tf_op jit(solution)/shard_map/ppermute | solution.py:30
  576.8 18.1 %collective-permute-start.24 = (bf16[1,128,2048]{2,1,0:T(8,128)(2,1)S(1)}, bf16[1,128,2048]{2,1,0:T(8,128)(2,1)}, u32[]{:S(2)}, u32[]{:S(2)}) collective-permute-start(bf16[1,128,2048]{2,1,0:T(8,128)(2,1)S(1)} %get-tuple-element.259), channel_id=1, source_target_pairs={{0,8},{4,12},{8,0},{12,4},{16,24},{20,28},{24,16},{28,20},{1,9},{5... | collective-permute-start | bytes 1572872 | tf_op jit(solution)/shard_map/ppermute | solution.py:30
  578.3 16.6 %collective-permute-start.25 = (bf16[1,128,2048]{2,1,0:T(8,128)(2,1)S(1)}, bf16[1,128,2048]{2,1,0:T(8,128)(2,1)}, u32[]{:S(2)}, u32[]{:S(2)}) collective-permute-start(bf16[1,128,2048]{2,1,0:T(8,128)(2,1)S(1)} %get-tuple-element.260), channel_id=1, source_target_pairs={{0,16},{4,20},{8,24},{12,28},{16,0},{20,4},{24,8},{28,12},{1,17},{... | collective-permute-start | bytes 1572872 | tf_op jit(solution)/shard_map/ppermute | solution.py:30
  611.8 7.5 %collective-permute-start.28 = (bf16[1024,2048]{1,0:T(8,128)(2,1)}, bf16[1024,2048]{1,0:T(8,128)(2,1)}, u32[]{:S(2)}, u32[]{:S(2)}) collective-permute-start(bf16[1024,2048]{1,0:T(8,128)(2,1)} %convolution_convert_fusion.1), channel_id=1, source_target_pairs={{0,4},{4,0},{8,12},{12,8},{16,20},{20,16},{24,28},{28,24},{1,5},{5... | collective-permute-start | bytes 12582920 | tf_op jit(solution)/shard_map/ppermute | solution.py:30
  612.1 36.2 %collective-permute-start.35 = (bf16[512,768]{1,0:T(8,128)(2,1)}, bf16[512,768]{1,0:T(8,128)(2,1)}, u32[]{:S(2)}, u32[]{:S(2)}) collective-permute-start(bf16[512,768]{1,0:T(8,128)(2,1)} %get-tuple-element.274), channel_id=1, source_target_pairs={{0,1},{1,0},{2,3},{3,2},{4,5},{5,4},{6,7},{7,6},{8,9},{9,8},{10,11... | collective-permute-start | bytes 2359304 | tf_op jit(solution)/shard_map/ppermute | solution.py:30
  614.7 51.7 %collective-permute-start.31 = (bf16[1408,256]{1,0:T(8,128)(2,1)}, bf16[1408,256]{1,0:T(8,128)(2,1)}, u32[]{:S(2)}, u32[]{:S(2)}) collective-permute-start(bf16[1408,256]{1,0:T(8,128)(2,1)} %fusion.14), channel_id=1, source_target_pairs={{0,2},{1,3},{2,0},{3,1},{4,6},{5,7},{6,4},{7,5},{8,10},{9,11},{10,... | collective-permute-start | bytes 2162696 | tf_op jit(solution)/shard_map/ppermute | solution.py:30
  617.4 46.4 %collective-permute-start.32 = (bf16[1408,256]{1,0:T(8,128)(2,1)}, bf16[1408,256]{1,0:T(8,128)(2,1)}, u32[]{:S(2)}, u32[]{:S(2)}) collective-permute-start(bf16[1408,256]{1,0:T(8,128)(2,1)} %get-tuple-element.281), channel_id=1, source_target_pairs={{0,1},{1,0},{2,3},{3,2},{4,5},{5,4},{6,7},{7,6},{8,9},{9,8},{10,11... | collective-permute-start | bytes 2162696 | tf_op jit(solution)/shard_map/ppermute | solution.py:30
  629.4 37.0 %collective-permute-start.29 = (bf16[2,128,2048]{2,1,0:T(8,128)(2,1)S(1)}, bf16[2,128,2048]{2,1,0:T(8,128)(2,1)}, u32[]{:S(2)}, u32[]{:S(2)}) collective-permute-start(bf16[2,128,2048]{2,1,0:T(8,128)(2,1)S(1)} %bitcast.146), channel_id=1, source_target_pairs={{0,16},{4,20},{8,24},{12,28},{16,0},{20,4},{24,8},{28,12},{1,17},{... | collective-permute-start | bytes 3145736 | tf_op jit(solution)/shard_map/ppermute | solution.py:30
  631.2 35.2 %collective-permute-start.30 = (bf16[2,128,2048]{2,1,0:T(8,128)(2,1)}, bf16[2,128,2048]{2,1,0:T(8,128)(2,1)}, u32[]{:S(2)}, u32[]{:S(2)}) collective-permute-start(bf16[2,128,2048]{2,1,0:T(8,128)(2,1)} %bitcast.191), channel_id=1, source_target_pairs={{0,8},{4,12},{8,0},{12,4},{16,24},{20,28},{24,16},{28,20},{1,9},{5... | collective-permute-start | bytes 3145736 | tf_op jit(solution)/shard_map/ppermute | solution.py:30
  633.8 46.2 %all-to-all-start.4 = ((bf16[8,256,256]{2,1,0:T(8,128)(2,1)}), bf16[8,256,256]{2,1,0:T(8,128)(2,1)}, u32[]{:S(2)}, u32[]{:S(2)}) async-start(bf16[8,256,256]{2,1,0:T(8,128)(2,1)} %bitcast.163), calls=%async_computation.6 | async-start | bytes 2097152 | tf_op jit(solution)/shard_map/all_to_all | solution.py:229
  648.3 66.6 %collective-permute-start.37 = (bf16[512,768]{1,0:T(8,128)(2,1)S(1)}, bf16[512,768]{1,0:T(8,128)(2,1)}, u32[]{:S(2)}, u32[]{:S(2)}) collective-permute-start(bf16[512,768]{1,0:T(8,128)(2,1)S(1)} %get-tuple-element.301), channel_id=1, source_target_pairs={{0,1},{1,0},{2,3},{3,2},{4,5},{5,4},{6,7},{7,6},{8,9},{9,8},{10,11... | collective-permute-start | bytes 2359304 | tf_op jit(solution)/shard_map/ppermute | solution.py:30
  663.8 51.1 %collective-permute-start.36 = (bf16[512,768]{1,0:T(8,128)(2,1)}, bf16[512,768]{1,0:T(8,128)(2,1)}, u32[]{:S(2)}, u32[]{:S(2)}) collective-permute-start(bf16[512,768]{1,0:T(8,128)(2,1)} %add_convert_fusion), channel_id=1, source_target_pairs={{0,2},{1,3},{2,0},{3,1},{4,6},{5,7},{6,4},{7,5},{8,10},{9,11},{10,... | collective-permute-start | bytes 2359304 | tf_op jit(solution)/shard_map/ppermute | solution.py:30
  671.7 14.8 %collective-permute-start.33 = (bf16[1,128,2048]{2,1,0:T(8,128)(2,1)S(1)}, bf16[1,128,2048]{2,1,0:T(8,128)(2,1)S(1)}, u32[]{:S(2)}, u32[]{:S(2)}) collective-permute-start(bf16[1,128,2048]{2,1,0:T(8,128)(2,1)S(1)} %get-tuple-element.285), channel_id=1, source_target_pairs={{0,8},{4,12},{8,0},{12,4},{16,24},{20,28},{24,16},{28,20},{1,9},{5... | collective-permute-start | bytes 1572872 | tf_op jit(solution)/shard_map/ppermute | solution.py:30
  673.5 12.9 %collective-permute-start.34 = (bf16[1,128,2048]{2,1,0:T(8,128)(2,1)S(1)}, bf16[1,128,2048]{2,1,0:T(8,128)(2,1)S(1)}, u32[]{:S(2)}, u32[]{:S(2)}) collective-permute-start(bf16[1,128,2048]{2,1,0:T(8,128)(2,1)S(1)} %get-tuple-element.286), channel_id=1, source_target_pairs={{0,16},{4,20},{8,24},{12,28},{16,0},{20,4},{24,8},{28,12},{1,17},{... | collective-permute-start | bytes 1572872 | tf_op jit(solution)/shard_map/ppermute | solution.py:30
  686.2 16.4 %collective-permute-start.38 = (bf16[512,256]{1,0:T(8,128)(2,1)S(1)}, bf16[512,256]{1,0:T(8,128)(2,1)S(1)}, u32[]{:S(2)}, u32[]{:S(2)}) collective-permute-start(bf16[512,256]{1,0:T(8,128)(2,1)S(1)} %get-tuple-element.308), channel_id=1, source_target_pairs={{0,1},{1,0},{2,3},{3,2},{4,5},{5,4},{6,7},{7,6},{8,9},{9,8},{10,11... | collective-permute-start | bytes 786440 | tf_op jit(solution)/shard_map/ppermute | solution.py:30
  686.8 18.9 %copy-start.31 = (f32[256,2048]{1,0:T(8,128)S(1)}, f32[256,2048]{1,0:T(8,128)}, u32[]{:S(2)}) copy-start(f32[256,2048]{1,0:T(8,128)} %get-tuple-element.290) | copy-start | bytes 6291460
  702.6 22.6 %collective-permute-start.40 = (bf16[512,256]{1,0:T(8,128)(2,1)S(1)}, bf16[512,256]{1,0:T(8,128)(2,1)S(1)}, u32[]{:S(2)}, u32[]{:S(2)}) collective-permute-start(bf16[512,256]{1,0:T(8,128)(2,1)S(1)} %get-tuple-element.312), channel_id=1, source_target_pairs={{0,1},{1,0},{2,3},{3,2},{4,5},{5,4},{6,7},{7,6},{8,9},{9,8},{10,11... | collective-permute-start | bytes 786440 | tf_op jit(solution)/shard_map/ppermute | solution.py:30
  703.0 22.2 %collective-permute-start.39 = (bf16[512,256]{1,0:T(8,128)(2,1)S(1)}, bf16[512,256]{1,0:T(8,128)(2,1)S(1)}, u32[]{:S(2)}, u32[]{:S(2)}) collective-permute-start(bf16[512,256]{1,0:T(8,128)(2,1)S(1)} %add_convert_fusion.1), channel_id=1, source_target_pairs={{0,2},{1,3},{2,0},{3,1},{4,6},{5,7},{6,4},{7,5},{8,10},{9,11},{10,... | collective-permute-start | bytes 786440 | tf_op jit(solution)/shard_map/ppermute | solution.py:30
  705.6 2.0 collective-permute-start.41
  707.7 4.0 collective-permute-start.42
  711.7 4.0 collective-permute-start.43
  715.7 4.0 collective-permute-start.44
  719.7 4.9 collective-permute-start.45
  (47 other events, 225.7 us)
Sparse Core Ops, SparseCore 0:
  9.9 57.0 all-gather.12
  68.9 54.3 all-gather.8
  146.5 72.9 all-gather.10
  221.6 105.3 all-gather.14
  334.6 55.9 all-gather.16
  393.3 54.4 reduce-scatter.2
  450.7 56.0 reduce-scatter.4
